TPU v7x, 32 devices: a whole 2x2x4 slice. The times are simulated.
32 devices in a mesh: ctx: 16 (over z, y, x), tp: 2 (over core).
Axes of the slice: x: 2, y: 2, z: 4, core: 2. Of those that a mesh axis runs over, the one named last changes fastest.
Arguments:
- queries: bfloat16 [4096, 8192], P('ctx', 'tp'), may hold values from -6 to 6
- key_branch: bfloat16 [4096, 8192], P('ctx', 'tp'), may hold values from -6 to 6
- value_branch: bfloat16 [4096, 8192], P('ctx', 'tp'), may hold values from -6 to 6
- cotangent: bfloat16 [4096, 8192], P('ctx', 'tp'), may hold values from -6 to 6
- filters: float32 [512, 128], replicated, may hold values from -0.5 to 0.5
- skip_bias: float32 [8192], P('tp'), may hold values from -1 to 1
- contig_start: int32 [4096], replicated, may hold values from 0 to 4095, as said below
Outputs:
- output: bfloat16 [4096, 8192], P('ctx', 'tp')
- grad_query: bfloat16 [4096, 8192], P('ctx', 'tp')
- grad_key: bfloat16 [4096, 8192], P('ctx', 'tp')
- grad_value: bfloat16 [4096, 8192], P('ctx', 'tp')
- grad_filter: float32 [512, 128], replicated
- grad_bias: float32 [8192], P('tp')
Inputs may be any that keep to these rules, and one draw needn't show every extreme that they name: contig_start[0] is 0, and for t > 0 contig_start[t] is either t (a new contig begins) or contig_start[t - 1]; the last token begins a contig of its own.
All inputs are finite; a program needn't handle non-finite values.
Results may differ from a plain program's by a relative error of at most 0.0056.
Values may be sent and summed in bfloat16 or wider, within the bound.
No kernel may reach another device: no remote copies, remote signals or barrier semaphores. Data moves between devices by JAX's collectives and lax.ppermute only.
A program may use at most 128 MiB of HBM per device.

v0:
```python
import math

import jax
import jax.numpy as jnp
from jax import lax
from jax.sharding import PartitionSpec as P


def passed_along(value, axis, steps):
    count = lax.axis_size(axis)
    initial, last = (max(0, -steps), min(count, count - steps))
    return lax.ppermute(value, axis, [(source, source + steps) for source in range(initial, last)])


def toeplitz(filter_taps):
    group_count, filter_size = filter_taps.shape
    leading = jnp.zeros((group_count, 1), filter_taps.dtype)
    trailing = jnp.zeros((group_count, filter_size), filter_taps.dtype)
    pattern = jnp.concatenate([leading, filter_taps[:, ::-1], trailing], axis=1)
    tiled = jnp.tile(pattern, (1, filter_size))[:, : 2 * filter_size * filter_size]
    return tiled.reshape(group_count, filter_size, 2 * filter_size)


def fold_lags(products):
    group_count, filter_size, window_size = products.shape
    flattened = products.reshape(group_count, filter_size * window_size)
    flattened = jnp.concatenate(
        [flattened, jnp.zeros((group_count, filter_size), products.dtype)], axis=1
    )
    columns = flattened.reshape(group_count, filter_size, window_size + 1).sum(axis=1)
    return columns[:, 1 : filter_size + 1][:, ::-1]


def hyena_pass(
    queries,
    key_branch,
    value_branch,
    cotangent,
    gated_signal,
    signal_grad,
    left_rim,
    right_rim,
    row_starts,
    next_starts,
    filter_taps,
    bias_part,
    first_row,
):
    row_count, channel_count = gated_signal.shape
    group_count, filter_size = filter_taps.shape
    per_group = channel_count // group_count
    block_count = row_count // filter_size
    padded = jnp.concatenate(
        [jnp.zeros((1, channel_count), jnp.bfloat16), left_rim, gated_signal], axis=0
    )
    windows = jnp.concatenate(
        [
            padded[:row_count].reshape(block_count, filter_size, group_count, per_group),
            padded[filter_size:].reshape(block_count, filter_size, group_count, per_group),
        ],
        axis=1,
    )
    grads_ext = jnp.concatenate(
        [signal_grad, right_rim, jnp.zeros((1, channel_count), jnp.bfloat16)], axis=0
    )
    grads_ext = grads_ext.reshape(block_count + 1, filter_size, group_count, per_group)
    starts_ext = jnp.concatenate([row_starts, next_starts]).reshape(block_count + 1, filter_size)
    source_pos = (
        first_row + (jnp.arange(block_count + 1, dtype=jnp.int32)[:, None] - 1) * filter_size
    )
    source_pos = source_pos + jnp.arange(2 * filter_size, dtype=jnp.int32)[None, :]
    visible = source_pos[:, None, :] >= starts_ext[:, :, None]
    band = jnp.where(visible[:, None], toeplitz(filter_taps)[None], jnp.zeros((), jnp.bfloat16))
    convolved = jnp.einsum(
        "bgts,bsgc->btgc", band[:block_count], windows, preferred_element_type=jnp.float32
    ).reshape(row_count, channel_count)
    back_terms = jnp.einsum("bgts,btgc->bsgc", band, grads_ext, preferred_element_type=jnp.float32)
    gated_grad = (back_terms[:block_count, filter_size:] + back_terms[1:, :filter_size]).reshape(
        row_count, channel_count
    )
    filtered = convolved + bias_part[None, :] * gated_signal.astype(jnp.float32)
    output = (queries.astype(jnp.float32) * filtered).astype(jnp.bfloat16)
    grad_query = (cotangent.astype(jnp.float32) * filtered).astype(jnp.bfloat16)
    gated_grad = gated_grad + bias_part[None, :] * signal_grad.astype(jnp.float32)
    grad_key = (gated_grad * value_branch.astype(jnp.float32)).astype(jnp.bfloat16)
    grad_value = (gated_grad * key_branch.astype(jnp.float32)).astype(jnp.bfloat16)
    bias_term = jnp.sum(signal_grad.astype(jnp.float32) * gated_signal.astype(jnp.float32), axis=0)
    products = jnp.einsum(
        "btgc,bsgc->bgts", grads_ext[:block_count], windows, preferred_element_type=jnp.float32
    )
    products = jnp.where(visible[:block_count, None], products, jnp.zeros((), jnp.float32)).sum(
        axis=0
    )
    return (output, grad_query, grad_key, grad_value, fold_lags(products), bias_term)


def gate_pair(first_input, second_input):
    return (first_input.astype(jnp.float32) * second_input.astype(jnp.float32)).astype(jnp.bfloat16)


def body(queries, key_branch, value_branch, cotangent, filters, skip_bias, contig_start):
    row_count, channel_count = queries.shape
    group_total, filter_size = filters.shape
    ctx_count = lax.axis_size("ctx")
    tp_count = lax.axis_size("tp")
    shard_index = lax.axis_index("ctx")
    tensor_index = lax.axis_index("tp")
    token_count = row_count * ctx_count
    per_group = channel_count * tp_count // group_total
    local_groups = channel_count // per_group
    starts_pad = jnp.concatenate([contig_start, jnp.zeros((filter_size,), jnp.int32)])
    gated_signal = gate_pair(key_branch, value_branch)
    signal_grad = gate_pair(cotangent, queries)
    left_rim = passed_along(gated_signal[row_count - filter_size + 1 :], "ctx", 1)
    right_rim = passed_along(signal_grad[: filter_size - 1], "ctx", -1)
    row_starts = lax.dynamic_slice_in_dim(contig_start, shard_index * row_count, row_count, 0)
    next_starts = lax.dynamic_slice_in_dim(
        starts_pad, (shard_index + 1) * row_count, filter_size, 0
    )
    filter_taps = lax.dynamic_slice_in_dim(
        filters, tensor_index * local_groups, local_groups, 0
    ).astype(jnp.bfloat16)
    batch_groups = min(local_groups, 16)
    batch_count = local_groups // batch_groups
    batch_width = batch_groups * per_group

    def one_batch(batch_index):
        first_col = batch_index * batch_width

        def cols_of(array):
            return lax.dynamic_slice_in_dim(array, first_col, batch_width, 1)

        return hyena_pass(
            cols_of(queries),
            cols_of(key_branch),
            cols_of(value_branch),
            cols_of(cotangent),
            cols_of(gated_signal),
            cols_of(signal_grad),
            cols_of(left_rim),
            cols_of(right_rim),
            row_starts,
            next_starts,
            lax.dynamic_slice_in_dim(filter_taps, batch_index * batch_groups, batch_groups, 0),
            lax.dynamic_slice_in_dim(skip_bias, first_col, batch_width, 0),
            shard_index * row_count,
        )

    pieces = lax.map(one_batch, jnp.arange(batch_count, dtype=jnp.int32))

    def merge_batches(stacked):
        return jnp.transpose(stacked, (1, 0, 2)).reshape(row_count, channel_count)

    output = merge_batches(pieces[0])
    grad_query = merge_batches(pieces[1])
    grad_key = merge_batches(pieces[2])
    grad_value = merge_batches(pieces[3])
    filter_rows = pieces[4].reshape(local_groups, filter_size)
    bias_part = pieces[5].reshape(channel_count)
    filter_part = lax.dynamic_update_slice(
        jnp.zeros((group_total, filter_size), jnp.float32),
        filter_rows,
        (tensor_index * local_groups, 0),
    )
    filter_sum = lax.psum(filter_part, ("ctx", "tp"))
    bias_sum = lax.psum(bias_part, "ctx")
    grad_filter = filter_sum * (1.0 / math.sqrt(token_count * per_group))
    grad_bias = bias_sum * (1.0 / math.sqrt(token_count))
    return (output, grad_query, grad_key, grad_value, grad_filter, grad_bias)


def solution(mesh):
    return jax.shard_map(
        body,
        mesh=mesh,
        in_specs=(
            P("ctx", "tp"),
            P("ctx", "tp"),
            P("ctx", "tp"),
            P("ctx", "tp"),
            P(),
            P("tp"),
            P(),
        ),
        out_specs=(P("ctx", "tp"), P("ctx", "tp"), P("ctx", "tp"), P("ctx", "tp"), P(), P("tp")),
        check_vma=False,
    )
```

profile of v0, /device:TPU:0, one launch (start us, length us, event | category | flops | bytes accessed | tf_op | source)
XLA Modules:
  0.0 702.7 jit_solution(18328573101783210402)
XLA Ops:
  7.2 4.2 copy.23
  18.1 5.8 collective-permute-start
  23.9 4.1 copy.27
  28.0 4.1 copy.28
  32.0 4.1 multiply_convert_fusion.4
  40.6 27.5 %collective-permute-done = bf16[127,4096]{0,1:T(8,128)(2,1)} collective-permute-done((bf16[127,4096]{0,1:T(8,128)(2,1)}, bf16[127,4096]{0,1:T(8,128)(2,1)}, u32[]{:S(2)}, u32[]{:S(2)}) %collective-permute-start) | collective-permute-done | bytes 1040416 | tf_op jit(solution)/shard_map/ppermute | solution.py:12
  70.1 423.0 %while.22 = (s32[]{:T(128)}, bf16[16,256,256]{1,2,0:T(8,128)(2,1)}, bf16[16,256,256]{1,2,0:T(8,128)(2,1)}, bf16[16,256,256]{1,2,0:T(8,128)(2,1)}, bf16[16,256,25...) while((s32[]{:T(128)}, bf16[16,256,256]{1,2,0:T(8,128)(2,1)}, ...), condition=%wide.region_4.5_spmd, body=%wide.region_0.4_spmd.sunk | while | flops 125295200 | bytes 67632560 | solution.py:149
  85.8 3.7 reshape.132
  112.3 3.7 reshape.132
  138.7 3.7 reshape.132
  165.1 3.7 reshape.132
  191.6 3.7 reshape.132
  218.0 3.7 reshape.132
  244.5 3.7 reshape.132
  270.9 3.7 reshape.132
  297.3 3.7 reshape.132
  323.8 3.7 reshape.132
  350.2 3.7 reshape.132
  403.1 3.7 reshape.132
  456.0 3.7 reshape.132
  493.1 75.0 %psum.15 = f32[4096]{0:T(1024)S(1)} all-reduce(f32[4096]{0:T(1024)S(1)} %bitcast.142), channel_id=1, replica_groups=mesh['ctx'=16,'tp'=2] {'ctx'}, use_global_device_ids=true, to_apply=%region_6.7 | all-reduce | flops 4096 | bytes 32768 | tf_op jit(solution)/shard_map/psum | solution.py:166
  568.2 4.2 copy.35
  576.1 4.2 copy.37
  583.7 110.4 %all-reduce.4.cloned.1.call-done = f32[512,128]{1,0:T(8,128)} async-done(((f32[512,128]{1,0:T(8,128)}), f32[512,128]{1,0:T(8,128)}) %all-reduce.4.cloned.1.call-update) | async-done | bytes 262160 | tf_op jit(solution)/shard_map/psum | solution.py:165
  (1131 shorter events, 370.4 us)
Async XLA Ops:
  7.2 32.8 %copy-start = (f32[512,128]{1,0:T(8,128)S(1)}, f32[512,128]{1,0:T(8,128)}, u32[]{:S(2)}) copy-start(f32[512,128]{1,0:T(8,128)} %param.13) | copy-start | bytes 786436
  7.2 687.0 %all-reduce.4.cloned.1.call-start = ((), (), s32[]{:S(2)}) async-start(), calls=%async_computation | async-start | bytes 524288 | tf_op jit(solution)/shard_map/psum | solution.py:165
  18.1 50.0 %collective-permute-start = (bf16[127,4096]{0,1:T(8,128)(2,1)}, bf16[127,4096]{0,1:T(8,128)(2,1)}, u32[]{:S(2)}, u32[]{:S(2)}) collective-permute-start(bf16[127,4096]{0,1:T(8,128)(2,1)} %slice.60), channel_id=1, source_target_pairs={{0,2},{2,4},{4,6},{6,8},{8,10},{10,12},{12,14},{14,16},{16,18},{18... | collective-permute-start | bytes 3121160 | tf_op jit(solution)/shard_map/ppermute | solution.py:12
  38.4 31.6 %collective-permute-start.1 = (bf16[127,4096]{0,1:T(8,128)(2,1)}, bf16[127,4096]{0,1:T(8,128)(2,1)}, u32[]{:S(2)}, u32[]{:S(2)}) collective-permute-start(bf16[127,4096]{0,1:T(8,128)(2,1)} %slice.61), channel_id=1, source_target_pairs={{2,0},{4,2},{6,4},{8,6},{10,8},{12,10},{14,12},{16,14},{18,16},{20... | collective-permute-start | bytes 3121160 | tf_op jit(solution)/shard_map/ppermute | solution.py:12
  70.1 6.5 copy-start.8
  74.0 6.2 copy-start.5
  96.5 6.5 copy-start.8
  100.4 6.2 copy-start.5
  122.9 6.5 copy-start.8
  126.9 6.2 copy-start.5
  149.4 6.5 copy-start.8
  153.3 6.2 copy-start.5
  175.8 6.5 copy-start.8
  202.3 6.5 copy-start.8
  228.7 6.5 copy-start.8
  255.1 6.5 copy-start.8
  281.6 6.5 copy-start.8
  308.0 6.5 copy-start.8
  334.4 6.5 copy-start.8
  360.9 6.5 copy-start.8
  387.3 6.5 copy-start.8
  413.8 6.5 copy-start.8
  440.2 6.5 copy-start.8
  466.7 6.5 copy-start.8
  (194 other events, 419.9 us)
Sparse Core Ops, SparseCore 0:
  573.3 120.8 all-reduce.3
where the time goes:
time: 708 us; the launch traced here: 703 us
  local copies, waits for them, and re-layouts  304 us (43%)
  waiting for transfers between devices  140 us (20%)
  other arithmetic  105 us (15%)
  blocking collectives  75 us (11%)
  matrix products  31.6 us (4%)
  loops' own time  26.2 us (4%)
  between operations  14.2 us (2%)
  starting transfers between devices  7.14 us (1%)
    psum x1, waiting for transfers between devices, body(): filter_sum = lax.psum(filter_part, ('ctx', 'tp'))  110 us
    psum x1, blocking collectives, body(): bias_sum = lax.psum(bias_part, 'ctx')  75 us
    reshape x16, local copies, waits for them, and re-layouts, fold_lags(): flattened.reshape(group_count, filter_size, window_size + 1).sum(axis=1)  59.3 us
    while x464, local copies, waits for them, and re-layouts  35.7 us
    dynamic_update_slice x16, other arithmetic, body(): pieces = lax.map(one_batch, jnp.arange(batch_count, dtype=jnp.int32))  33.4 us
    another operation x32, local copies, waits for them, and re-layouts, toeplitz(): jnp.tile(pattern, (1, filter_size))[:, :2 * filter_size * filter_size]  31.8 us
    ppermute x2, waiting for transfers between devices, passed_along(): lax.ppermute(value, axis, [(source, source + steps) for source in range(i...  29.5 us
    another operation x1, loops' own time, body(): pieces = lax.map(one_batch, jnp.arange(batch_count, dtype=jnp.int32))  26.2 us
  transfers between devices with their start and end apart: 3, of which 3 were waited for; matrix products, arithmetic and copies ran while one was open for 4% of the time, Pallas kernels for 0%

commit v1 on v0

v1 whole, which is shorter than its diff:
```python
import functools
import math

import jax
import jax.numpy as jnp
from jax import lax
from jax.experimental import pallas as pl
from jax.experimental.pallas import tpu as pltpu
from jax.sharding import PartitionSpec as P

F32, BF16 = jnp.float32, jnp.bfloat16
LANES = 128
TB = 16
WIDE = 256
X_CHUNKS = 1
DY_CHUNKS = 1


def lane_iota(shape):
    return lax.broadcasted_iota(jnp.int32, shape, len(shape) - 1)


def swap_chunks(arrays, chunk):
    count = len(arrays)
    pos = lane_iota(arrays[0].shape) // chunk
    turned = [pltpu.roll(a, n * chunk, 1) if n else a for n, a in enumerate(arrays)]
    rows = [turned[(-i) % count] for i in range(count)]
    bit = 1
    while bit < count:
        moved = (pos & bit) != 0
        rows = [jnp.where(moved, rows[(i - bit) % count], rows[i]) for i in range(count)]
        bit *= 2
    return [pltpu.roll(a, LANES - n * chunk, 1) if n else a for n, a in enumerate(rows)]


def to_groups(block, chunk):
    per = LANES // chunk
    sets = []
    for first in range(0, block.shape[0], TB * per):
        parts = [block[first + TB * n : first + TB * (n + 1)] for n in range(per)]
        sets.append(swap_chunks(parts, chunk))
    return [[s[g] for s in sets] for g in range(per)]


def windows(ext, chunk, count):
    per = LANES // chunk
    width = len(ext) - count // per
    out = []
    for i in range(count + 1):
        whole, part = divmod(i, per)
        if part == 0:
            vregs = ext[whole : whole + width]
        else:
            turned = [pltpu.roll(a, LANES - chunk * part, 1) for a in ext[whole : whole + width + 1]]
            keep = lane_iota(ext[0].shape) < LANES - chunk * part
            vregs = [jnp.where(keep, turned[v], turned[v + 1]) for v in range(width)]
        out.append(vregs[0] if width == 1 else jnp.concatenate(vregs, axis=1))
    return out


def side_by_side(vregs):
    return vregs[0] if len(vregs) == 1 else jnp.concatenate(vregs, axis=1)


def product_bf16(a, b):
    return (a.astype(F32) * b.astype(F32)).astype(BF16)


def from_groups(chunked, sub_groups, row_count, chunk):
    per = LANES // chunk
    rows = []
    for first in range(0, row_count // (TB * per)):
        parts = [chunked[g, :, first * LANES : (first + 1) * LANES] for g in range(sub_groups)]
        rows += swap_chunks(parts, chunk)
    return jnp.concatenate(rows, axis=0)


def skew_left(products):
    moved = pltpu.roll(products, WIDE - products.shape[0], 1, stride=1, stride_axis=0)
    return jnp.sum(moved, axis=0, keepdims=True)


def turned_rows(block):
    size = block.shape[0]
    ones = lax.broadcasted_iota(jnp.int32, (size, size), 0) + lane_iota((size, size)) == size - 1
    return jnp.dot(ones.astype(F32).astype(BF16), block, preferred_element_type=F32).astype(BF16)


def conv_kernel(chunk, filter_size, classes, q_ref, ct_ref, k_ref, v_ref, rim_ref, mask_ref, sel_ref, order_ref,
                taps_ref, bias_ref, *rest):
    out_ref, gq_ref, gf_ref, gb_ref, x_s, dy_s, conv_s, grad_s = rest[-8:]
    row_count, width = q_ref.shape
    per = LANES // chunk
    steps = filter_size // TB
    span = (steps + 1) * TB
    row = lax.broadcasted_iota(jnp.int32, (2 * TB, WIDE), 0)
    col = lane_iota((2 * TB, WIDE))
    band = ((row < TB) & (col < span)) | ((row >= TB) & (col >= span) & (col < span + TB))
    turned_band = ((row >= TB) & (col < span)) | ((row < TB) & (col >= span) & (col < span + TB))

    def one(sub, carry):
        lanes = pl.ds(pl.multiple_of(sub * LANES, LANES), LANES)
        x = product_bf16(k_ref[:, lanes], v_ref[:, lanes])
        dy = product_bf16(ct_ref[:, lanes], q_ref[:, lanes])
        gb_ref[:, lanes] = jnp.sum(x.astype(F32) * dy.astype(F32), axis=0, keepdims=True)
        xs, dys, rims = to_groups(x, chunk), to_groups(dy, chunk), to_groups(rim_ref[:, lanes], chunk)
        for g in range(per):
            xg, dyg = side_by_side(xs[g]), side_by_side(dys[g])
            x_s[g], dy_s[g] = xg, dyg
            window = jnp.concatenate(windows(rims[g] + xs[g], chunk, steps) + [xg], axis=0) * mask_ref[...]
            base = jnp.broadcast_to(taps_ref[pl.ds(sub * per + g, 1), :], (2 * TB, WIDE))
            taps = jnp.where(band, pltpu.roll(base, 0, 1, stride=1, stride_axis=0), 0.0).astype(BF16)
            y = jnp.dot(taps[:, : span + TB], window, preferred_element_type=F32)
            conv_s[g] = y[:TB] * sel_ref[:TB, :] + y[TB:] * sel_ref[TB:, :]
            dy2 = jnp.concatenate([dyg, dyg], axis=0) * mask_ref[span - TB : span + TB, :]
            pairs = lax.dot_general(turned_rows(dy2), window, (((1,), (1,)), ((), ())), preferred_element_type=F32)
            pairs = jnp.concatenate([pairs, jnp.zeros((2 * TB, WIDE - span - TB), F32)], axis=1)
            grad_s[g : g + 1, :] = skew_left(jnp.where(turned_band, pairs, 0.0))

        def more(index, carry):
            level, g = index // per, index % per
            here = order_ref[...] == level.astype(F32)
            xq = jnp.where(here, x_s[g].astype(F32), 0.0).astype(BF16)
            dyq = jnp.where(here, dy_s[g].astype(F32), 0.0).astype(BF16)
            base = jnp.broadcast_to(taps_ref[pl.ds(sub * per + g, 1), :], (TB, WIDE))
            taps = pltpu.roll(base, 0, 1, stride=1, stride_axis=0).astype(BF16)
            y = jnp.dot(taps[:, filter_size : filter_size + TB], xq, preferred_element_type=F32)
            conv_s[g] += jnp.where(here, y, 0.0)
            pairs = lax.dot_general(turned_rows(dyq), xq, (((1,), (1,)), ((), ())), preferred_element_type=F32)
            pairs = jnp.concatenate(
                [jnp.zeros((TB, filter_size), F32), pairs, jnp.zeros((TB, WIDE - filter_size - TB), F32)], axis=1
            )
            grad_s[pl.ds(g, 1), :] += skew_left(pairs)
            return carry

        lax.fori_loop(2 * per, classes[0] * per, more, 0)
        first = pl.multiple_of(sub * per, per)
        gf_ref[pl.ds(first, per), :] = grad_s[:, :filter_size]
        conv = from_groups(conv_s, per, row_count, chunk)
        filtered = conv + bias_ref[:, lanes] * x.astype(F32)
        out_ref[:, lanes] = (q_ref[:, lanes].astype(F32) * filtered).astype(BF16)
        gq_ref[:, lanes] = (ct_ref[:, lanes].astype(F32) * filtered).astype(BF16)
        return carry

    lax.fori_loop(0, width // LANES, one, 0)


def back_kernel(chunk, filter_size, classes, q_ref, ct_ref, k_ref, v_ref, rim_ref, mask_ref, sel_ref, order_ref,
                taps_ref, bias_ref, *rest):
    gk_ref, gv_ref, dy_s, back_s = rest[-4:]
    row_count, width = q_ref.shape
    per = LANES // chunk
    steps = filter_size // TB
    span = (steps + 1) * TB
    row = lax.broadcasted_iota(jnp.int32, (2 * TB, WIDE), 0)
    col = lane_iota((2 * TB, WIDE))
    band = (row >= TB) | (col < TB)

    def one(sub, carry):
        lanes = pl.ds(pl.multiple_of(sub * LANES, LANES), LANES)
        dy = product_bf16(ct_ref[:, lanes], q_ref[:, lanes])
        dys, rims = to_groups(dy, chunk), to_groups(rim_ref[:, lanes], chunk)
        for g in range(per):
            dyg = side_by_side(dys[g])
            dy_s[g] = dyg
            window = jnp.concatenate([dyg] + windows(dys[g] + rims[g], chunk, steps), axis=0) * mask_ref[...]
            base = jnp.broadcast_to(taps_ref[pl.ds(sub * per + g, 1), :], (2 * TB, WIDE))
            taps = jnp.where(band, pltpu.roll(base, 0, 1, stride=1, stride_axis=0), 0.0).astype(BF16)
            y = jnp.dot(taps[:, : span + TB], window, preferred_element_type=F32)
            back_s[g] = y[:TB] * sel_ref[:TB, :] + y[TB:] * sel_ref[TB:, :]

        def more(index, carry):
            level, g = index // per, index % per
            here = order_ref[...] == level.astype(F32)
            dyq = jnp.where(here, dy_s[g].astype(F32), 0.0).astype(BF16)
            base = jnp.broadcast_to(taps_ref[pl.ds(sub * per + g, 1), :], (TB, WIDE))
            taps = pltpu.roll(base, 0, 1, stride=1, stride_axis=0).astype(BF16)
            y = jnp.dot(taps[:, :TB], dyq, preferred_element_type=F32)
            back_s[g] += jnp.where(here, y, 0.0)
            return carry

        lax.fori_loop(2 * per, classes[0] * per, more, 0)
        back = from_groups(back_s, per, row_count, chunk)
        back = back + bias_ref[:, lanes] * dy.astype(F32)
        gk_ref[:, lanes] = (back * v_ref[:, lanes].astype(F32)).astype(BF16)
        gv_ref[:, lanes] = (back * k_ref[:, lanes].astype(F32)).astype(BF16)
        return carry

    lax.fori_loop(0, width // LANES, one, 0)


def run_part(kernel, name, part, parts, classes, big, rim, masks, taps, bias, small, previous):
    row_count, channels = big[0].shape
    mask, sel, order = masks
    group_count, filter_size = taps.shape[0], rim.shape[0]
    chunk = channels // group_count
    width = channels // parts
    block = math.gcd(width, 512)
    groups = block // chunk
    count, first = width // block, part * (width // block)
    at = lambda i, c: (0, first + i)
    whole = lambda i, c: (0, 0)
    cols = lambda rows: pl.BlockSpec((rows, block), at)
    fixed = lambda a: pl.BlockSpec(a.shape, whole)
    in_specs = [cols(row_count)] * 4 + [pl.BlockSpec((rim.shape[0], block), lambda i, c: (0, i))]
    in_specs += [fixed(mask), fixed(sel), fixed(order)]
    in_specs += [pl.BlockSpec((groups, WIDE), lambda i, c: (first + i, 0)), cols(1)]
    out_shape = [jax.ShapeDtypeStruct((row_count, channels), BF16)] * 2
    out_specs = [cols(row_count)] * 2
    scratch = [pltpu.VMEM((LANES // chunk, TB, row_count), BF16)]
    if small:
        out_shape += [jax.ShapeDtypeStruct((group_count, filter_size), F32), jax.ShapeDtypeStruct((1, channels), F32)]
        out_specs += [pl.BlockSpec((groups, filter_size), lambda i, c: (first + i, 0)), cols(1)]
        scratch += [pltpu.VMEM((LANES // chunk, TB, row_count), BF16)]
    scratch += [pltpu.VMEM((LANES // chunk, TB, row_count), F32)]
    if small:
        scratch += [pltpu.VMEM((LANES // chunk, WIDE), F32)]
    operands = [*big, rim, mask, sel, order, taps, bias]
    aliases = {}
    if previous is not None:
        aliases = {1 + len(operands) + i: i for i in range(len(previous))}
        in_specs += [pl.BlockSpec(memory_space=pl.ANY)] * len(previous)
        operands += list(previous)
    return pl.pallas_call(
        functools.partial(kernel, chunk, filter_size),
        grid_spec=pltpu.PrefetchScalarGridSpec(
            num_scalar_prefetch=1, grid=(count,), in_specs=in_specs, out_specs=out_specs, scratch_shapes=scratch
        ),
        out_shape=out_shape,
        input_output_aliases=aliases,
        compiler_params=pltpu.CompilerParams(vmem_limit_bytes=48 * 1024 * 1024),
        cost_estimate=pl.CostEstimate(
            flops=2 * row_count * width * 512, bytes_accessed=12 * row_count * width, transcendentals=0
        ),
        name=name,
    )(classes, *operands)


def reset_masks(starts, base, row_count, steps, chunk):
    blocks = row_count // TB
    near = lax.dynamic_slice_in_dim(starts, base, row_count + steps * TB, 0) - base
    ahead = near.reshape(blocks + steps, TB)
    own = ahead[:blocks]
    pos = jnp.arange(row_count, dtype=jnp.int32).reshape(blocks, TB)
    begins = (own == pos) & (jnp.arange(TB) > 0)[None, :]
    order = jnp.cumsum(begins.astype(jnp.int32), axis=1)
    behind = order[:, -1:] - order
    back = jnp.arange(steps, 0, -1, dtype=jnp.int32)[:, None, None]
    seen = [(pos[None] - TB * back) >= own[None, :, :1], (order == 0)[None], (order == 1)[None]]
    mask_x = jnp.concatenate(seen, axis=0)
    later = jnp.stack([ahead[m : m + blocks] for m in range(1, steps + 1)])
    kept = [(behind == 1)[None], (behind == 0)[None], later <= pos[None, :, -1:]]
    mask_dy = jnp.concatenate(kept, axis=0)

    def laid_out(a, kind):
        rows = a.shape[0] * TB
        flat = jnp.transpose(a, (0, 2, 1)).reshape(rows, blocks).astype(kind)
        return jnp.broadcast_to(flat[:, :, None], (rows, blocks, chunk)).reshape(rows, row_count)

    masks_x = (laid_out(mask_x, BF16), laid_out(mask_x[steps:], F32), laid_out(order[None], F32))
    masks_dy = (laid_out(mask_dy, BF16), laid_out(mask_dy[:2], F32), laid_out(behind[None], F32))
    classes = (1 + jnp.max(order)).reshape(1)
    return classes, masks_x, masks_dy


def passed_along(value, axis, steps):
    count = lax.axis_size(axis)
    initial, last = (max(0, -steps), min(count, count - steps))
    return lax.ppermute(value, axis, [(source, source + steps) for source in range(initial, last)])


def sum_over(value, axis):
    count = lax.axis_size(axis)
    if count & (count - 1):
        return lax.psum(value, axis)
    step = 1
    while step < count:
        value = value + lax.ppermute(value, axis, [(i, i ^ step) for i in range(count)])
        step *= 2
    return value


def rows_of_all(value, axis):
    count = lax.axis_size(axis)
    if count != 2:
        return lax.all_gather(value, axis, axis=0, tiled=True)
    other = lax.ppermute(value, axis, [(0, 1), (1, 0)])
    is_first = lax.axis_index(axis) == 0
    return jnp.concatenate([jnp.where(is_first, value, other), jnp.where(is_first, other, value)], axis=0)


def body(queries, key_branch, value_branch, cotangent, filters, skip_bias, contig_start):
    row_count, channels = queries.shape
    group_total, filter_size = filters.shape
    ctx_count, tp_count = lax.axis_size("ctx"), lax.axis_size("tp")
    shard, tensor = lax.axis_index("ctx"), lax.axis_index("tp")
    token_count = row_count * ctx_count
    chunk = channels * tp_count // group_total
    groups = channels // chunk
    steps = filter_size // TB

    def rims(a, b, first, direction, parts):
        width = channels // parts
        sent = []
        for part in range(parts):
            cut = lambda m: lax.slice(m, (first, part * width), (first + filter_size, (part + 1) * width))
            sent.append(passed_along(product_bf16(cut(a), cut(b)), "ctx", direction))
        return sent

    left = rims(key_branch, value_branch, row_count - filter_size, 1, X_CHUNKS)
    right = rims(cotangent, queries, 0, -1, DY_CHUNKS)

    starts = jnp.concatenate([contig_start, jnp.full((filter_size,), 2**30, jnp.int32)])
    classes, masks_x, masks_dy = reset_masks(starts, shard * row_count, row_count, steps, chunk)
    taps = lax.dynamic_slice_in_dim(filters, tensor * groups, groups, 0)
    taps_x = jnp.pad(taps[:, ::-1], ((0, 0), (1, WIDE - filter_size - 1)))
    taps_dy = jnp.pad(taps, ((0, 0), (0, WIDE - filter_size)))
    bias = skip_bias.reshape(1, channels)
    big = (queries, cotangent, key_branch, value_branch)

    done = None
    for part in range(X_CHUNKS):
        done = run_part(conv_kernel, "conv", part, X_CHUNKS, classes, big, left[part], masks_x, taps_x, bias, True, done)
    output, grad_query, filter_part, bias_part = done
    done = None
    for part in range(DY_CHUNKS):
        done = run_part(back_kernel, "back", part, DY_CHUNKS, classes, big, right[part], masks_dy, taps_dy, bias, False, done)
    grad_key, grad_value = done

    terms = jnp.concatenate([filter_part, bias_part.reshape(channels // filter_size, filter_size)], axis=0)
    terms = sum_over(terms, "ctx")
    filter_sum = rows_of_all(terms[:groups], "tp")
    grad_filter = filter_sum[:, ::-1] * (1.0 / math.sqrt(token_count * chunk))
    grad_bias = terms[groups:].reshape(channels) * (1.0 / math.sqrt(token_count))
    return (output, grad_query, grad_key, grad_value, grad_filter, grad_bias)


def solution(mesh):
    wide = P("ctx", "tp")
    return jax.shard_map(
        body,
        mesh=mesh,
        in_specs=(wide, wide, wide, wide, P(), P("tp"), P()),
        out_specs=(wide, wide, wide, wide, P(), P("tp")),
        check_vma=False,
    )
```

time: 708 us -> 157 us (0.22)
  local copies, waits for them, and re-layouts: 304 us -> 31.2 us
  waiting for transfers between devices: 140 us -> 30.6 us
  other arithmetic: 105 us -> 10.4 us
  blocking collectives: 75 us -> 0 us
  Pallas kernels: 0 us -> 67.1 us
  matrix products: 31.6 us -> 0 us
  loops' own time: 26.2 us -> 0 us
  between operations: 14.2 us -> 1.58 us
  starting transfers between devices: 7.14 us -> 15 us
    psum x1 -> x0, waiting for transfers between devices: 110 us -> none  [body(): filter_sum = lax.psum(filter_part, ('ctx', 'tp'))]
    reshape x68 -> x6, local copies, waits for them, and re-layouts: 86.8 us -> 5.94 us  [laid_out(): jnp.broadcast_to(flat[:, :, None], (rows, blocks, chunk))]
    psum x1 -> x0, blocking collectives: 75 us -> none  [body(): bias_sum = lax.psum(bias_part, 'ctx')]
    pallas_call x0 -> x2, Pallas kernels: none -> 67.1 us  [run_part(): pl.pallas_call(functools.partial(kernel, chunk, filter_size), grid_spec=p...]
    dynamic_slice x66 -> x1, local copies, waits for them, and re-layouts: 48.1 us -> 0.68 us  [body(): taps = lax.dynamic_slice_in_dim(filters, tensor * groups, groups, 0)]
    while x466 -> x0, local copies, waits for them, and re-layouts: 43.9 us -> none
    dynamic_update_slice x16 -> x0, other arithmetic: 33.4 us -> none  [body(): pieces = lax.map(one_batch, jnp.arange(batch_count, dtype=jnp.int32))]
    dot_general x48 -> x0, matrix products: 31.6 us -> none  [the longest x16 12.6 us: hyena_pass(): jnp.einsum('btgc,bsgc->bgts', grads_ext[:block_count], windows, preferred...]
  transfers between devices with their start and end apart: 3 -> 7, of which waited for: 3 -> 5; matrix products, arithmetic and copies ran while one was open for 4% -> 21% of each run, Pallas kernels for 0% -> 43%
where the time goes in v1:
time: 157 us; the launch traced here: 156 us
  Pallas kernels  67.1 us (43%)
  local copies, waits for them, and re-layouts  31.2 us (20%)
  waiting for transfers between devices  30.6 us (19%)
  starting transfers between devices  15 us (10%)
  other arithmetic  10.4 us (7%)
  between operations  1.58 us (1%)
    pallas_call x2, Pallas kernels, run_part(): pl.pallas_call(functools.partial(kernel, chunk, filter_size), grid_spec=p...  67.1 us
    ppermute x2, waiting for transfers between devices, passed_along(): lax.ppermute(value, axis, [(source, source + steps) for source in range(i...  18.4 us
    ppermute x4, waiting for transfers between devices, sum_over(): lax.ppermute(value, axis, [(i, i ^ step) for i in range(count)])  11.5 us
    unnamed x45, local copies, waits for them, and re-layouts  9.08 us
    ppermute x4, starting transfers between devices, sum_over(): lax.ppermute(value, axis, [(i, i ^ step) for i in range(count)])  7.7 us
    ppermute x2, starting transfers between devices, passed_along(): lax.ppermute(value, axis, [(source, source + steps) for source in range(i...  7.23 us
    reshape x6, local copies, waits for them, and re-layouts, laid_out(): jnp.broadcast_to(flat[:, :, None], (rows, blocks, chunk))  5.94 us
    another operation x9, local copies, waits for them, and re-layouts, reset_masks(): later = jnp.stack([ahead[m:m + blocks] for m in range(1, steps + 1)])  5.4 us
  transfers between devices with their start and end apart: 7, of which 5 were waited for; matrix products, arithmetic and copies ran while one was open for 21% of the time, Pallas kernels for 43%

profile of v1, /device:TPU:0, one launch (start us, length us, event | category | flops | bytes accessed | tf_op | source)
XLA Modules:
  0.0 155.9 jit_solution(12906862547049474358)
XLA Ops:
  0.7 2.9 %multiply_convert_fusion.1 = bf16[128,4096]{1,0:T(8,128)(2,1)} fusion(bf16[256,4096]{1,0:T(8,128)(2,1)} %v_ref.3, bf16[256,4096]{1,0:T(8,128)(2,1)} %k_ref.3), kind=kLoop, calls=%fused_computation.1 | loop fusion | flops 2097152 | bytes 3145728 | tf_op jit(solution)/shard_map/convert_element_type | solution.py:66
  3.6 6.0 %collective-permute-start = (bf16[128,4096]{1,0:T(8,128)(2,1)}, bf16[128,4096]{1,0:T(8,128)(2,1)}, u32[]{:S(2)}, u32[]{:S(2)}) collective-permute-start(bf16[128,4096]{1,0:T(8,128)(2,1)} %multiply_convert_fusion.1), channel_id=1, source_target_pairs={{0,2},{2,4},{4,6},{6,8},{8,10},{10,12},{12,14},{14,16},{16,18},{18... | collective-permute-start | bytes 3145736 | tf_op jit(solution)/shard_map/ppermute | solution.py:269
  9.5 2.4 %multiply_convert_fusion = bf16[128,4096]{1,0:T(8,128)(2,1)} fusion(bf16[256,4096]{1,0:T(8,128)(2,1)S(1)} %copy-done.1, bf16[256,4096]{1,0:T(8,128)(2,1)} %ct_ref.3), kind=kLoop, calls=%fused_computation | loop fusion | flops 2097152 | bytes 3145728 | tf_op jit(solution)/shard_map/convert_element_type | solution.py:66
  12.0 1.3 collective-permute-start.1
  22.0 1.0 copy.34.mask_ref
  25.4 1.0 reshape.277.order_ref
  27.1 1.6 %rev.6 = f32[256,128]{1,0:T(8,128)} reverse(f32[256,128]{1,0:T(8,128)} %constant_dynamic-slice_fusion), dimensions={1} | reverse | bytes 262144 | tf_op jit(solution)/shard_map/rev | solution.py:316
  29.4 1.0 pad.9.taps_ref
  35.3 18.4 %collective-permute-done.rim_ref = bf16[128,4096]{1,0:T(8,128)(2,1)} collective-permute-done((bf16[128,4096]{1,0:T(8,128)(2,1)}, bf16[128,4096]{1,0:T(8,128)(2,1)}, u32[]{:S(2)}, u32[]{:S(2)}) %collective-permute-start) | collective-permute-done | bytes 1048608 | tf_op jit(solution)/shard_map/ppermute | solution.py:269
  53.7 1.6 %copy-done.2 = bf16[256,4096]{1,0:T(8,128)(2,1)S(1)} copy-done((bf16[256,4096]{1,0:T(8,128)(2,1)S(1)}, bf16[256,4096]{1,0:T(8,128)(2,1)}, u32[]{:S(2)}) %copy-start.2) | copy-done | bytes 2097176
  55.4 41.8 %conv.1 = (bf16[256,4096]{1,0:T(8,128)(2,1)}, bf16[256,4096]{1,0:T(8,128)(2,1)}, f32[256,128]{1,0:T(8,128)S(1)}, f32[1,4096]{1,0:T(1,128)S(1)}) custom-call(s32[1]{0:T(128)} %bitcast.classes, bf16[256,4096]{1,0:T(8,128)(2,1)S(1)} %copy-done.1, bf16[256,4096]{1,0:T(8,128)(2,1)S(1)} %copy-done.2, bf16[256,4096]{1,0:T(8,128)(2,1)} %k_ref.3, ...), custom_call_target="tpu_custom_call" | custom-call | flops 1073741824 | bytes 12582912 | tf_op jit(solution)/shard_map/conv/pallas_call | solution.py:224
  97.1 2.5 %collective-permute-start.2 = (f32[288,128]{1,0:T(8,128)S(1)}, f32[288,128]{1,0:T(8,128)S(1)}, u32[]{:S(2)}, u32[]{:S(2)}) collective-permute-start(f32[288,128]{1,0:T(8,128)S(1)} %pad_maximum_fusion.1), channel_id=1, source_target_pairs={{0,2},{2,0},{4,6},{6,4},{8,10},{10,8},{12,14},{14,12},{16,18},{18,... | collective-permute-start | bytes 442376 | tf_op jit(solution)/shard_map/ppermute | solution.py:278
  99.9 2.9 %collective-permute-done.2 = f32[288,128]{1,0:T(8,128)S(1)} collective-permute-done((f32[288,128]{1,0:T(8,128)S(1)}, f32[288,128]{1,0:T(8,128)S(1)}, u32[]{:S(2)}, u32[]{:S(2)}) %collective-permute-start.2) | collective-permute-done | bytes 147488 | tf_op jit(solution)/shard_map/ppermute | solution.py:278
  103.0 5.0 %collective-permute-done.3 = f32[288,128]{1,0:T(8,128)S(1)} collective-permute-done((f32[288,128]{1,0:T(8,128)S(1)}, f32[288,128]{1,0:T(8,128)S(1)}, u32[]{:S(2)}, u32[]{:S(2)}) %collective-permute-start.3) | collective-permute-done | bytes 147488 | tf_op jit(solution)/shard_map/ppermute | solution.py:278
  108.1 1.6 %collective-permute-start.4 = (f32[288,128]{1,0:T(8,128)S(1)}, f32[288,128]{1,0:T(8,128)S(1)}, u32[]{:S(2)}, u32[]{:S(2)}) collective-permute-start(f32[288,128]{1,0:T(8,128)S(1)} %add.46), channel_id=1, source_target_pairs={{0,8},{2,10},{4,12},{6,14},{8,0},{10,2},{12,4},{14,6},{16,24},{18,... | collective-permute-start | bytes 442376 | tf_op jit(solution)/shard_map/ppermute | solution.py:278
  109.8 3.5 %collective-permute-done.4 = f32[288,128]{1,0:T(8,128)S(1)} collective-permute-done((f32[288,128]{1,0:T(8,128)S(1)}, f32[288,128]{1,0:T(8,128)S(1)}, u32[]{:S(2)}, u32[]{:S(2)}) %collective-permute-start.4) | collective-permute-done | bytes 147488 | tf_op jit(solution)/shard_map/ppermute | solution.py:278
  113.9 3.4 %collective-permute-start.5 = (f32[288,128]{1,0:T(8,128)}, f32[288,128]{1,0:T(8,128)}, u32[]{:S(2)}, u32[]{:S(2)}) collective-permute-start(f32[288,128]{1,0:T(8,128)} %add.47), channel_id=1, source_target_pairs={{0,16},{2,18},{4,20},{6,22},{8,24},{10,26},{12,28},{14,30},{16,0},... | collective-permute-start | bytes 442376 | tf_op jit(solution)/shard_map/ppermute | solution.py:278
  117.4 1.6 %pad.10.taps_ref = f32[256,256]{1,0:T(8,128)} pad(f32[256,128]{1,0:T(8,128)} %constant_dynamic-slice_fusion, f32[]{:T(128)} %constant.39.clone.1), padding=0_0x0_128 | pad | bytes 393220 | tf_op jit(solution)/shard_map/jit(_pad)/pad | solution.py:317
  120.0 1.0 copy.39.mask_ref
  121.7 1.0 copy.40.sel_ref
  123.4 1.0 reshape.281.order_ref
  124.4 1.6 %copy-done.3 = bf16[256,4096]{1,0:T(8,128)(2,1)S(1)} copy-done((bf16[256,4096]{1,0:T(8,128)(2,1)S(1)}, bf16[256,4096]{1,0:T(8,128)(2,1)}, u32[]{:S(2)}) %copy-start.3) | copy-done | bytes 2097176
  127.0 25.4 %back.1 = (bf16[256,4096]{1,0:T(8,128)(2,1)}, bf16[256,4096]{1,0:T(8,128)(2,1)}) custom-call(s32[1]{0:T(128)} %bitcast.classes, bf16[256,4096]{1,0:T(8,128)(2,1)S(1)} %copy-done.1, bf16[256,4096]{1,0:T(8,128)(2,1)S(1)} %copy-done.3, bf16[256,4096]{1,0:T(8,128)(2,1)} %k_ref.3, bf16[256,4096]{1,0:T(8,128)(2,1)} %v_ref.3, ...), custom_call_target="tpu_custom_call" | custom-call | flops 1073741824 | bytes 12582912 | tf_op jit(solution)/shard_map/back/pallas_call | solution.py:224
  152.3 1.0 add.48
  (105 shorter events, 23.7 us)
Async XLA Ops:
  0.6 25.8 %copy-start = (f32[512,128]{1,0:T(8,128)S(1)}, f32[512,128]{1,0:T(8,128)}, u32[]{:S(2)}) copy-start(f32[512,128]{1,0:T(8,128)} %param.11) | copy-start | bytes 786436
  0.6 8.9 %copy-start.1 = (bf16[256,4096]{1,0:T(8,128)(2,1)S(1)}, bf16[256,4096]{1,0:T(8,128)(2,1)}, u32[]{:S(2)}) copy-start(bf16[256,4096]{1,0:T(8,128)(2,1)} %q_ref.3) | copy-start | bytes 6291460
  3.6 9.7 %copy-start.16 = (s32[4096]{0:T(1024)S(1)}, s32[4096]{0:T(1024)}, u32[]{:S(2)}) copy-start(s32[4096]{0:T(1024)} %param.13) | copy-start | bytes 49156
  3.6 50.2 %copy-start.5 = (f32[4096]{0:T(1024)S(1)}, f32[4096]{0:T(1024)}, u32[]{:S(2)}) copy-start(f32[4096]{0:T(1024)} %param.12) | copy-start | bytes 49156
  3.6 50.2 %collective-permute-start = (bf16[128,4096]{1,0:T(8,128)(2,1)}, bf16[128,4096]{1,0:T(8,128)(2,1)}, u32[]{:S(2)}, u32[]{:S(2)}) collective-permute-start(bf16[128,4096]{1,0:T(8,128)(2,1)} %multiply_convert_fusion.1), channel_id=1, source_target_pairs={{0,2},{2,4},{4,6},{6,8},{8,10},{10,12},{12,14},{14,16},{16,18},{18... | collective-permute-start | bytes 3145736 | tf_op jit(solution)/shard_map/ppermute | solution.py:269
  12.0 112.5 %collective-permute-start.1 = (bf16[128,4096]{1,0:T(8,128)(2,1)}, bf16[128,4096]{1,0:T(8,128)(2,1)S(1)}, u32[]{:S(2)}, u32[]{:S(2)}) collective-permute-start(bf16[128,4096]{1,0:T(8,128)(2,1)} %multiply_convert_fusion), channel_id=1, source_target_pairs={{2,0},{4,2},{6,4},{8,6},{10,8},{12,10},{14,12},{16,14},{18,16},{20... | collective-permute-start | bytes 3145736 | tf_op jit(solution)/shard_map/ppermute | solution.py:269
  13.3 7.8 %copy-start.8 = (s32[16,16]{1,0:T(8,128)}, s32[16,16]{1,0:T(8,128)S(1)}, u32[]{:S(2)}) copy-start(s32[16,16]{1,0:T(8,128)S(1)} %multiply_add_fusion) | copy-start | bytes 3076
  13.9 7.2 %copy-start.6 = (s32[16,16]{1,0:T(8,128)}, s32[16,16]{1,0:T(8,128)S(1)}, u32[]{:S(2)}) copy-start(s32[16,16]{1,0:T(8,128)S(1)} %reduce_window_sum.13) | copy-start | bytes 3076
  14.1 1.5 copy-start.17
  53.7 1.6 %copy-start.2 = (bf16[256,4096]{1,0:T(8,128)(2,1)S(1)}, bf16[256,4096]{1,0:T(8,128)(2,1)}, u32[]{:S(2)}) copy-start(bf16[256,4096]{1,0:T(8,128)(2,1)} %ct_ref.3) | copy-start | bytes 6291460
  55.3 44.4 %copy-start.11 = (s32[1,16,16]{2,1,0:T(8,128)S(1)}, s32[1,16,16]{2,1,0:T(8,128)}, u32[]{:S(2)}) copy-start(s32[1,16,16]{2,1,0:T(8,128)} %stack.34) | copy-start | bytes 3076
  55.3 44.4 %copy-start.9 = (s32[16,16]{1,0:T(8,128)S(1)}, s32[16,16]{1,0:T(8,128)}, u32[]{:S(2)}) copy-start(s32[16,16]{1,0:T(8,128)} %copy-done.8) | copy-start | bytes 3076
  55.3 54.4 %copy-start.7 = (s32[16,16]{1,0:T(8,128)S(1)}, s32[16,16]{1,0:T(8,128)}, u32[]{:S(2)}) copy-start(s32[16,16]{1,0:T(8,128)} %copy-done.6) | copy-start | bytes 3076
  55.3 54.4 %copy-start.18 = (s32[16]{0:T(128)S(1)}, s32[16]{0:T(128)}, u32[]{:S(2)}) copy-start(s32[16]{0:T(128)} %copy-done.17) | copy-start | bytes 196
  55.3 62.1 %copy-start.13 = (pred[1,16,16]{2,1,0:T(8,128)(4,1)S(1)}, pred[1,16,16]{2,1,0:T(8,128)(4,1)}, u32[]{:S(2)}) copy-start(pred[1,16,16]{2,1,0:T(8,128)(4,1)} %copy-done.12) | copy-start | bytes 772
  55.4 62.0 %copy-start.15 = (pred[1,16,16]{2,1,0:T(8,128)(4,1)S(1)}, pred[1,16,16]{2,1,0:T(8,128)(4,1)}, u32[]{:S(2)}) copy-start(pred[1,16,16]{2,1,0:T(8,128)(4,1)} %copy-done.14) | copy-start | bytes 772
  97.1 22.0 %copy-start.10 = (f32[2,16,16]{1,2,0:T(8,128)S(1)}, f32[2,16,16]{1,2,0:T(8,128)}, u32[]{:S(2)}) copy-start(f32[2,16,16]{1,2,0:T(8,128)} %get-tuple-element.35) | copy-start | bytes 6148
  97.1 5.7 %collective-permute-start.2 = (f32[288,128]{1,0:T(8,128)S(1)}, f32[288,128]{1,0:T(8,128)S(1)}, u32[]{:S(2)}, u32[]{:S(2)}) collective-permute-start(f32[288,128]{1,0:T(8,128)S(1)} %pad_maximum_fusion.1), channel_id=1, source_target_pairs={{0,2},{2,0},{4,6},{6,4},{8,10},{10,8},{12,14},{14,12},{16,18},{18,... | collective-permute-start | bytes 442376 | tf_op jit(solution)/shard_map/ppermute | solution.py:278
  102.8 5.2 %collective-permute-start.3 = (f32[288,128]{1,0:T(8,128)S(1)}, f32[288,128]{1,0:T(8,128)S(1)}, u32[]{:S(2)}, u32[]{:S(2)}) collective-permute-start(f32[288,128]{1,0:T(8,128)S(1)} %fusion.7), channel_id=1, source_target_pairs={{0,4},{2,6},{4,0},{6,2},{8,12},{10,14},{12,8},{14,10},{16,20},{18,... | collective-permute-start | bytes 442376 | tf_op jit(solution)/shard_map/ppermute | solution.py:278
  108.1 5.2 %collective-permute-start.4 = (f32[288,128]{1,0:T(8,128)S(1)}, f32[288,128]{1,0:T(8,128)S(1)}, u32[]{:S(2)}, u32[]{:S(2)}) collective-permute-start(f32[288,128]{1,0:T(8,128)S(1)} %add.46), channel_id=1, source_target_pairs={{0,8},{2,10},{4,12},{6,14},{8,0},{10,2},{12,4},{14,6},{16,24},{18,... | collective-permute-start | bytes 442376 | tf_op jit(solution)/shard_map/ppermute | solution.py:278
  113.9 38.4 %collective-permute-start.5 = (f32[288,128]{1,0:T(8,128)}, f32[288,128]{1,0:T(8,128)}, u32[]{:S(2)}, u32[]{:S(2)}) collective-permute-start(f32[288,128]{1,0:T(8,128)} %add.47), channel_id=1, source_target_pairs={{0,16},{2,18},{4,20},{6,22},{8,24},{10,26},{12,28},{14,30},{16,0},... | collective-permute-start | bytes 442376 | tf_op jit(solution)/shard_map/ppermute | solution.py:278
  124.4 1.6 %copy-start.3 = (bf16[256,4096]{1,0:T(8,128)(2,1)S(1)}, bf16[256,4096]{1,0:T(8,128)(2,1)}, u32[]{:S(2)}) copy-start(bf16[256,4096]{1,0:T(8,128)(2,1)} %ct_ref.3) | copy-start | bytes 6291460
  126.0 0.9 copy-start.4
  153.4 1.4 collective-permute-start.6
  (2 other events, 1.4 us)

commit v2 on v1

v2 whole, which is shorter than its diff:
```python
import functools
import math

import jax
import jax.numpy as jnp
from jax import lax
from jax.experimental import pallas as pl
from jax.experimental.pallas import tpu as pltpu
from jax.sharding import PartitionSpec as P

F32, BF16 = jnp.float32, jnp.bfloat16
LANES = 128
TB = 16
WIDE = 256
KINDS = 3
PARTS = 4
IN_FLIGHT = 2


def iota(shape, axis):
    return lax.broadcasted_iota(jnp.int32, shape, axis)


def flag(condition, kind=BF16):
    return jnp.where(condition, 1.0, 0.0).astype(kind)


def permutation(size):
    return flag(iota((size, size), 0) + iota((size, size), 1) == size - 1)


def chunk_of(shape, kind, chunk):
    return (iota(shape, 1) // chunk).astype(F32).astype(kind)


def swap_chunks(arrays, bits, chunk):
    count = len(arrays)
    turned = [pltpu.roll(a, n * chunk, 1) if n else a for n, a in enumerate(arrays)]
    rows = [turned[(-i) % count] for i in range(count)]
    for power, moved in enumerate(bits):
        bit = 1 << power
        rows = [jnp.where(moved, rows[(i - bit) % count], rows[i]) for i in range(count)]
    return [pltpu.roll(a, LANES - n * chunk, 1) if n else a for n, a in enumerate(rows)]


def chunk_bits(kind, chunk):
    pos = iota((TB, LANES), 1) // chunk
    return [flag((pos >> power) & 1 == 1, kind) > 0 for power in range((LANES // chunk).bit_length() - 1)]


def to_groups(block, bits, chunk):
    per = LANES // chunk
    sets = []
    for first in range(0, block.shape[0], TB * per):
        parts = [block[first + TB * n : first + TB * (n + 1)] for n in range(per)]
        sets.append(swap_chunks(parts, bits, chunk))
    return [[s[g] for s in sets] for g in range(per)]


def from_groups(chunked, bits, chunk):
    rows = []
    for first in range(0, chunked[0].shape[1], LANES):
        rows += swap_chunks([a[:, first : first + LANES] for a in chunked], bits, chunk)
    return jnp.concatenate(rows, axis=0)


def windows(ext, pos, chunk, count):
    per = LANES // chunk
    width = len(ext) - count // per
    out = []
    for i in range(count + 1):
        whole, part = divmod(i, per)
        if part == 0:
            vregs = ext[whole : whole + width]
        else:
            turned = [pltpu.roll(a, LANES - chunk * part, 1) for a in ext[whole : whole + width + 1]]
            vregs = [jnp.where(pos < per - part, turned[v], turned[v + 1]) for v in range(width)]
        out.append(side_by_side(vregs))
    return out


def side_by_side(vregs):
    return vregs[0] if len(vregs) == 1 else jnp.concatenate(vregs, axis=1)


def product_bf16(a, b):
    return (a.astype(F32) * b.astype(F32)).astype(BF16)


def skew_left(products):
    moved = pltpu.roll(products, WIDE - products.shape[0], 1, stride=1, stride_axis=0)
    return jnp.sum(moved, axis=0, keepdims=True)


def shifted_taps(row, first):
    base = jnp.concatenate([row, jnp.zeros((1, WIDE - row.shape[1]), F32)], axis=1)
    base = jnp.broadcast_to(base, (TB, WIDE))
    return pltpu.roll(base, first, 1, stride=1, stride_axis=0).astype(BF16)


def with_kinds(taps, own, chunk):
    pos = chunk_of((TB, LANES), BF16, chunk)
    zero = jnp.zeros((TB, LANES), BF16)
    rows = [taps]
    for kind in range(1, KINDS):
        rows.append(jnp.concatenate([zero, jnp.where(pos == kind, pltpu.roll(own, kind * TB, 1), zero)], axis=1))
    return jnp.concatenate(rows, axis=0)


def chosen(products, sel_ref):
    return sum(products[kind * TB : (kind + 1) * TB] * sel_ref[kind * TB : (kind + 1) * TB, :] for kind in range(KINDS))


def conv_kernel(chunk, info, q_ref, ct_ref, k_ref, v_ref, rim_ref, mask_ref, turned_ref, sel_ref, order_ref,
                taps_ref, bias_ref, *rest):
    out_ref, gq_ref, gf_ref, gb_ref, x_s, dy_s, conv_s, grad_s = rest[-8:]
    row_count, width = q_ref.shape
    filter_size = taps_ref.shape[1]
    per = LANES // chunk
    steps = filter_size // TB
    span = (steps + 1) * TB
    depth = span + (KINDS - 1) * TB

    def one(sub, further):
        lanes = pl.ds(pl.multiple_of(sub * LANES, LANES), LANES)
        slot = 0
        bits, bits32 = chunk_bits(BF16, chunk), chunk_bits(F32, chunk)
        pos = chunk_of((TB, LANES), BF16, chunk)
        kind = KINDS - 1 - iota((KINDS * TB, WIDE), 0) // TB
        col = iota((KINDS * TB, WIDE), 1) - (kind + 1) * TB
        band = (col < filter_size) & ((kind == 0) | (col >= filter_size - TB))
        x = product_bf16(k_ref[:, lanes], v_ref[:, lanes])
        dy = product_bf16(ct_ref[:, lanes], q_ref[:, lanes])
        gb_ref[:, lanes] = jnp.sum(x.astype(F32) * dy.astype(F32), axis=0, keepdims=True)
        xs, dys = to_groups(x, bits, chunk), to_groups(dy, bits, chunk)
        rims = to_groups(rim_ref[:, lanes], bits, chunk)
        taps = taps_ref[pl.ds(pl.multiple_of(sub * per, per), per), :].astype(BF16)
        taps = jnp.dot(taps, permutation(filter_size), preferred_element_type=F32)
        for g in range(per):
            xg, dyg = side_by_side(xs[g]), side_by_side(dys[g])
            if further:
                x_s[slot, g], dy_s[slot, g] = xg, dyg
            window = windows(rims[g] + xs[g], pos, chunk, steps) + [xg] * (KINDS - 1)
            window = jnp.concatenate(window, axis=0) * mask_ref[...]
            band_taps = shifted_taps(taps[g : g + 1], 1)
            band_taps = with_kinds(band_taps, band_taps[:, LANES:], chunk)
            conv_s[slot, g] = chosen(jnp.dot(band_taps[:, :depth], window, preferred_element_type=F32), sel_ref)
            turned = jnp.dot(permutation(TB), dyg, preferred_element_type=F32).astype(BF16)
            turned = jnp.concatenate([turned] * KINDS, axis=0) * turned_ref[...]
            pairs = lax.dot_general(turned, window, (((1,), (1,)), ((), ())), preferred_element_type=F32)
            pairs = jnp.concatenate([pairs, jnp.zeros((KINDS * TB, WIDE - depth), F32)], axis=1)
            grad_s[slot, g : g + 1, :] = skew_left(jnp.where(band, pairs, 0.0))

        def more(index, carry):
            level, g = index // per, index % per
            here = order_ref[...] == level.astype(F32)
            xq = jnp.where(here, x_s[slot, g].astype(F32), 0.0).astype(BF16)
            dyq = jnp.where(here, dy_s[slot, g].astype(F32), 0.0).astype(BF16)
            row = taps_ref[pl.ds(sub * per + g, 1), :].astype(BF16)
            row = jnp.dot(row, permutation(filter_size), preferred_element_type=F32)
            own = shifted_taps(row, 1)[:, filter_size : filter_size + TB]
            conv_s[slot, g] += jnp.where(here, jnp.dot(own, xq, preferred_element_type=F32), 0.0)
            turned = jnp.dot(permutation(TB), dyq, preferred_element_type=F32).astype(BF16)
            pairs = lax.dot_general(turned, xq, (((1,), (1,)), ((), ())), preferred_element_type=F32)
            pairs = jnp.concatenate(
                [jnp.zeros((TB, filter_size), F32), pairs, jnp.zeros((TB, WIDE - filter_size - TB), F32)], axis=1
            )
            grad_s[slot, pl.ds(g, 1), :] += skew_left(pairs)
            return carry

        if further:
            lax.fori_loop(KINDS * per, info[0] * per, more, 0)
        gf_ref[pl.ds(pl.multiple_of(sub * per, per), per), :] = jnp.dot(
            grad_s[slot, :, :filter_size],
            permutation(filter_size).astype(F32),
            precision=lax.Precision.HIGHEST,
            preferred_element_type=F32,
        )
        conv = from_groups([conv_s[slot, g] for g in range(per)], bits32, chunk)
        filtered = conv + bias_ref[:, lanes] * x.astype(F32)
        out_ref[:, lanes] = (q_ref[:, lanes].astype(F32) * filtered).astype(BF16)
        gq_ref[:, lanes] = (ct_ref[:, lanes].astype(F32) * filtered).astype(BF16)

    for_all_lanes(one, width // LANES, info)


def back_kernel(chunk, info, q_ref, ct_ref, k_ref, v_ref, rim_ref, mask_ref, sel_ref, order_ref,
                taps_ref, bias_ref, *rest):
    gk_ref, gv_ref, dy_s, back_s = rest[-4:]
    row_count, width = q_ref.shape
    filter_size = taps_ref.shape[1]
    per = LANES // chunk
    steps = filter_size // TB
    depth = (steps + KINDS) * TB

    def one(sub, further):
        lanes = pl.ds(pl.multiple_of(sub * LANES, LANES), LANES)
        slot = 0
        bits, bits32 = chunk_bits(BF16, chunk), chunk_bits(F32, chunk)
        pos = chunk_of((TB, LANES), BF16, chunk)
        dy = product_bf16(ct_ref[:, lanes], q_ref[:, lanes])
        dys, rims = to_groups(dy, bits, chunk), to_groups(rim_ref[:, lanes], bits, chunk)
        taps = taps_ref[pl.ds(pl.multiple_of(sub * per, per), per), :]
        for g in range(per):
            dyg = side_by_side(dys[g])
            if further:
                dy_s[slot, g] = dyg
            window = windows(dys[g] + rims[g], pos, chunk, steps) + [dyg] * (KINDS - 1)
            window = jnp.concatenate(window, axis=0) * mask_ref[...]
            band_taps = shifted_taps(taps[g : g + 1], 0)
            band_taps = with_kinds(band_taps, band_taps[:, :LANES], chunk)
            back_s[slot, g] = chosen(jnp.dot(band_taps[:, :depth], window, preferred_element_type=F32), sel_ref)

        def more(index, carry):
            level, g = index // per, index % per
            here = order_ref[...] == level.astype(F32)
            dyq = jnp.where(here, dy_s[slot, g].astype(F32), 0.0).astype(BF16)
            own = shifted_taps(taps_ref[pl.ds(sub * per + g, 1), :], 0)[:, :TB]
            back_s[slot, g] += jnp.where(here, jnp.dot(own, dyq, preferred_element_type=F32), 0.0)
            return carry

        if further:
            lax.fori_loop(KINDS * per, info[0] * per, more, 0)
        back = from_groups([back_s[slot, g] for g in range(per)], bits32, chunk)
        back = back + bias_ref[:, lanes] * dy.astype(F32)
        gk_ref[:, lanes] = (back * v_ref[:, lanes].astype(F32)).astype(BF16)
        gv_ref[:, lanes] = (back * k_ref[:, lanes].astype(F32)).astype(BF16)

    for_all_lanes(one, width // LANES, info)


def for_all_lanes(one, count, info):
    def run(further):
        def step(sub, carry):
            one(sub, further)
            return carry

        lax.fori_loop(0, count, step, 0)

    pl.when(info[0] <= KINDS)(lambda: run(False))
    pl.when(info[0] > KINDS)(lambda: run(True))


def run_part(kernel, name, part, info, big, rim, masks, filters, bias, small, previous):
    row_count, channels = big[0].shape
    filter_size = filters.shape[1]
    chunk = TB
    width = channels // PARTS
    block = math.gcd(width, 512)
    groups = block // chunk
    count, first = width // block, part * (width // block)
    cols = lambda rows: pl.BlockSpec((rows, block), lambda i, c: (0, first + i))
    in_specs = [cols(row_count)] * 4 + [pl.BlockSpec((rim.shape[0], block), lambda i, c: (0, i))]
    in_specs += [pl.BlockSpec(a.shape, lambda i, c: (0, 0)) for a in masks]
    taps_at = lambda i, c: (c[1] * (channels // block) + first + i, 0)
    in_specs += [pl.BlockSpec((groups, filter_size), taps_at), cols(1)]
    out_shape = [jax.ShapeDtypeStruct((row_count, channels), BF16)] * 2
    out_specs = [cols(row_count)] * 2
    slots, per = 1, LANES // chunk
    scratch = [pltpu.VMEM((slots, per, TB, row_count), BF16)] * (2 if small else 1)
    scratch += [pltpu.VMEM((slots, per, TB, row_count), F32)]
    if small:
        out_shape += [jax.ShapeDtypeStruct((channels // chunk, filter_size), F32), jax.ShapeDtypeStruct((1, channels), F32)]
        out_specs += [pl.BlockSpec((groups, filter_size), lambda i, c: (first + i, 0)), cols(1)]
        scratch += [pltpu.VMEM((slots, per, WIDE), F32)]
    operands = [*big, rim, *masks, filters, bias]
    aliases = {}
    if previous is not None:
        aliases = {1 + len(operands) + i: i for i in range(len(previous))}
        in_specs += [pl.BlockSpec(memory_space=pl.ANY)] * len(previous)
        operands += list(previous)
    return pl.pallas_call(
        functools.partial(kernel, chunk),
        grid_spec=pltpu.PrefetchScalarGridSpec(
            num_scalar_prefetch=1, grid=(count,), in_specs=in_specs, out_specs=out_specs, scratch_shapes=scratch
        ),
        out_shape=out_shape,
        input_output_aliases=aliases,
        compiler_params=pltpu.CompilerParams(vmem_limit_bytes=48 * 1024 * 1024),
        cost_estimate=pl.CostEstimate(flops=row_count * width, bytes_accessed=row_count * width, transcendentals=0),
        name=name,
    )(info, *operands)


def reset_kernel(steps, near_ref, mask_x, turned_x, sel_x, order_x, mask_dy, sel_dy, order_dy, kinds):
    total = near_ref.shape[1]
    rows = total - steps * TB
    near = jnp.clip(near_ref[...], -1024, 1024).astype(F32)
    lane, row = iota((TB, total), 1), iota((TB, total), 0)
    spread = jnp.where(lane % TB == row, jnp.broadcast_to(near, (TB, total)), 0.0)
    same = flag(iota((total, total), 0) // TB == iota((total, total), 1) // TB, F32)
    begin = jnp.dot(spread, same, precision=lax.Precision.HIGHEST, preferred_element_type=F32)
    begin = jnp.floor(begin + 0.5)
    own = begin[:, :rows]
    block = iota((TB, rows), 1) // TB * TB
    pos = (block + iota((TB, rows), 0)).astype(F32)
    marks = flag((own == pos) & (iota((TB, rows), 0) > 0))
    before = flag(iota((TB, TB), 0) >= iota((TB, TB), 1))
    order = jnp.dot(before, marks, preferred_element_type=F32)
    behind = order[TB - 1 :] - order
    first = jnp.broadcast_to(own[:1], (TB, rows))
    for i in range(steps):
        mask_x[i * TB : (i + 1) * TB, :] = flag(pos - TB * (steps - i) >= first)
        later = pltpu.roll(begin, total - (i + 1) * TB, 1)[:, :rows]
        mask_dy[(i + 1) * TB : (i + 2) * TB, :] = flag(later <= (block + TB - 1).astype(F32))
    turn = permutation(TB)
    for kind in range(KINDS):
        at = steps + kind
        mask_x[at * TB : (at + 1) * TB, :] = flag(order == kind)
        sel_x[kind * TB : (kind + 1) * TB, :] = flag(order == kind, F32)
        at = KINDS - 1 - kind
        turned = jnp.dot(turn, flag(order == kind), preferred_element_type=F32)
        turned_x[at * TB : (at + 1) * TB, :] = turned.astype(BF16)
        at = steps + kind if kind else 0
        mask_dy[at * TB : (at + 1) * TB, :] = flag(behind == kind)
        sel_dy[kind * TB : (kind + 1) * TB, :] = flag(behind == kind, F32)
    order_x[...], order_dy[...] = order, behind
    kinds[0] = 1 + jnp.max(order).astype(jnp.int32)


def reset_masks(near, row_count, steps):
    depth, high = (steps + KINDS) * TB, KINDS * TB
    shapes = [(depth, BF16), (high, BF16), (high, F32), (TB, F32), (depth, BF16), (high, F32), (TB, F32)]
    out = pl.pallas_call(
        functools.partial(reset_kernel, steps),
        out_shape=[jax.ShapeDtypeStruct((rows, row_count), kind) for rows, kind in shapes]
        + [jax.ShapeDtypeStruct((1,), jnp.int32)],
        out_specs=[pl.BlockSpec(memory_space=pltpu.VMEM)] * len(shapes) + [pl.BlockSpec(memory_space=pltpu.SMEM)],
        compiler_params=pltpu.CompilerParams(vmem_limit_bytes=32 * 1024 * 1024),
        name="resets",
    )(near)
    return out[:4], out[4:7], out[7]


def passed_along(value, axis, steps):
    count = lax.axis_size(axis)
    initial, last = (max(0, -steps), min(count, count - steps))
    return lax.ppermute(value, axis, [(source, source + steps) for source in range(initial, last)])


def sum_over(value, axis):
    count = lax.axis_size(axis)
    if count & (count - 1):
        return lax.psum(value, axis)
    step = 1
    while step < count:
        value = value + lax.ppermute(value, axis, [(i, i ^ step) for i in range(count)])
        step *= 2
    return value


def rows_of_all(value, axis):
    count = lax.axis_size(axis)
    if count != 2:
        return lax.all_gather(value, axis, axis=0, tiled=True)
    other = lax.ppermute(value, axis, [(0, 1), (1, 0)])
    is_first = lax.axis_index(axis) == 0
    return jnp.concatenate([jnp.where(is_first, value, other), jnp.where(is_first, other, value)], axis=0)


def body(queries, key_branch, value_branch, cotangent, filters, skip_bias, contig_start):
    row_count, channels = queries.shape
    group_total, filter_size = filters.shape
    ctx_count, tp_count = lax.axis_size("ctx"), lax.axis_size("tp")
    shard, tensor = lax.axis_index("ctx"), lax.axis_index("tp")
    token_count = row_count * ctx_count
    chunk = channels * tp_count // group_total
    groups = channels // chunk
    width = channels // PARTS

    def rim(a, b, first, part):
        cut = lambda m: lax.slice(m, (first, part * width), (first + filter_size, (part + 1) * width))
        return product_bf16(cut(a), cut(b))

    sends = [(rim(key_branch, value_branch, row_count - filter_size, part), 1) for part in range(PARTS)]
    sends += [(rim(cotangent, queries, 0, part), -1) for part in range(PARTS)]
    halos = []
    for index, (sent, direction) in enumerate(sends):
        if index >= IN_FLIGHT:
            sent, halos[index - IN_FLIGHT] = lax.optimization_barrier((sent, halos[index - IN_FLIGHT]))
        halos.append(passed_along(sent, "ctx", direction))

    starts = jnp.concatenate([contig_start, jnp.full((filter_size,), 2**30, jnp.int32)])
    first = shard * row_count
    near = (lax.dynamic_slice_in_dim(starts, first, row_count + filter_size, 0) - first)[None, :]
    masks_x, masks_dy, kinds = reset_masks(near, row_count, filter_size // TB)
    info = jnp.concatenate([kinds, tensor.astype(jnp.int32).reshape(1)])
    bias = skip_bias.reshape(1, channels)
    big = (queries, cotangent, key_branch, value_branch)

    done = None
    for part in range(PARTS):
        done = run_part(conv_kernel, "conv", part, info, big, halos[part], masks_x, filters, bias, True, done)
    output, grad_query, filter_part, bias_part = done
    done = None
    for part in range(PARTS):
        done = run_part(back_kernel, "back", part, info, big, halos[PARTS + part], masks_dy, filters, bias, False, done)
    grad_key, grad_value = done

    terms = jnp.concatenate([filter_part, bias_part.reshape(channels // filter_size, filter_size)], axis=0)
    terms = sum_over(terms, "ctx")
    grad_filter = rows_of_all(terms[:groups], "tp") * (1.0 / math.sqrt(token_count * chunk))
    grad_bias = terms[groups:].reshape(channels) * (1.0 / math.sqrt(token_count))
    return (output, grad_query, grad_key, grad_value, grad_filter, grad_bias)


def solution(mesh):
    wide = P("ctx", "tp")
    return jax.shard_map(
        body,
        mesh=mesh,
        in_specs=(wide, wide, wide, wide, P(), P("tp"), P()),
        out_specs=(wide, wide, wide, wide, P(), P("tp")),
        check_vma=False,
    )
```

time: 157 us -> 149 us (0.949)
  local copies, waits for them, and re-layouts: 31.2 us -> 1.63 us
  starting transfers between devices: 15 us -> 40.5 us
  Pallas kernels: 67.1 us -> 87.6 us
  waiting for transfers between devices: 30.6 us -> 10.1 us
  other arithmetic: 10.4 us -> 8.25 us
    pallas_call x2 -> x9, Pallas kernels: 67.1 us -> 87.6 us  [the longest x8 86.5 us: run_part(): pl.pallas_call(functools.partial(kernel, chunk), grid_spec=pltpu.Prefetch...]
    ppermute x2 -> x8, starting transfers between devices: 7.23 us -> 22.3 us  [passed_along(): lax.ppermute(value, axis, [(source, source + steps) for source in range(i...]
    ppermute x2 -> x8, waiting for transfers between devices: 18.4 us -> 3.69 us  [passed_along(): lax.ppermute(value, axis, [(source, source + steps) for source in range(i...]
    ppermute x4, starting transfers between devices: 7.7 us -> 18.2 us  [sum_over(): lax.ppermute(value, axis, [(i, i ^ step) for i in range(count)])]
    unnamed x45 -> x12, local copies, waits for them, and re-layouts: 9.08 us -> 1.61 us
    reshape x6 -> x0, local copies, waits for them, and re-layouts: 5.94 us -> none  [laid_out(): jnp.broadcast_to(flat[:, :, None], (rows, blocks, chunk))]
    ppermute x4, waiting for transfers between devices: 11.5 us -> 5.73 us  [sum_over(): lax.ppermute(value, axis, [(i, i ^ step) for i in range(count)])]
    another operation x9 -> x0, local copies, waits for them, and re-layouts: 5.4 us -> none  [reset_masks(): later = jnp.stack([ahead[m:m + blocks] for m in range(1, steps + 1)])]
  transfers between devices with their start and end apart: 7 -> 13, of which waited for: 5 -> 7; matrix products, arithmetic and copies ran while one was open for 21% -> 3% of each run, Pallas kernels for 43% -> 41%
where the time goes in v2:
time: 149 us
  Pallas kernels  87.6 us (59%)
  starting transfers between devices  40.5 us (27%)
  waiting for transfers between devices  10.1 us (7%)
  other arithmetic  8.25 us (6%)
  local copies, waits for them, and re-layouts  1.63 us (1%)
    pallas_call x8, Pallas kernels, run_part(): pl.pallas_call(functools.partial(kernel, chunk), grid_spec=pltpu.Prefetch...  86.5 us
    ppermute x8, starting transfers between devices, passed_along(): lax.ppermute(value, axis, [(source, source + steps) for source in range(i...  22.3 us
    ppermute x4, starting transfers between devices, sum_over(): lax.ppermute(value, axis, [(i, i ^ step) for i in range(count)])  18.2 us
    ppermute x4, waiting for transfers between devices, sum_over(): lax.ppermute(value, axis, [(i, i ^ step) for i in range(count)])  5.73 us
    convert_element_type x2, other arithmetic, product_bf16(): return (a.astype(F32) * b.astype(F32)).astype(BF16)  5.1 us
    ppermute x8, waiting for transfers between devices, passed_along(): lax.ppermute(value, axis, [(source, source + steps) for source in range(i...  3.69 us
  transfers between devices with their start and end apart: 13, of which 7 were waited for; matrix products, arithmetic and copies ran while one was open for 3% of the time, Pallas kernels for 41%

profile of v2, /device:TPU:0, one launch (start us, length us, event | category | flops | bytes accessed | tf_op | source)
XLA Modules:
  0.0 148.9 jit_solution(753467711445865077)
XLA Ops:
  0.7 2.8 %multiply_convert_fusion.2 = (bf16[128,1024]{1,0:T(8,128)(2,1)}, bf16[128,1024]{1,0:T(8,128)(2,1)S(1)}, bf16[128,1024]{1,0:T(8,128)(2,1)}, bf16[128,1024]{1,0:T(8,128)(2,1)}) fusion(bf16[256,4096]{1,0:T(8,128)(2,1)} %v_ref.15, bf16[256,4096]{1,0:T(8,128)(2,1)} %k_ref.15), kind=kLoop, calls=%fused_computation.2 | loop fusion | flops 2097152 | bytes 3145728 | tf_op jit(solution)/shard_map/convert_element_type | solution.py:87
  3.5 5.0 %collective-permute-start = (bf16[128,1024]{1,0:T(8,128)(2,1)}, bf16[128,1024]{1,0:T(8,128)(2,1)S(1)}, u32[]{:S(2)}, u32[]{:S(2)}) collective-permute-start(bf16[128,1024]{1,0:T(8,128)(2,1)} %get-tuple-element.100), channel_id=1, source_target_pairs={{0,2},{2,4},{4,6},{6,8},{8,10},{10,12},{12,14},{14,16},{16,18},{18... | collective-permute-start | bytes 786440 | tf_op jit(solution)/shard_map/ppermute | solution.py:338
  8.5 3.4 %collective-permute-start.2 = (bf16[128,1024]{1,0:T(8,128)(2,1)}, bf16[128,1024]{1,0:T(8,128)(2,1)S(1)}, u32[]{:S(2)}, u32[]{:S(2)}) collective-permute-start(bf16[128,1024]{1,0:T(8,128)(2,1)} %get-tuple-element.98), channel_id=1, source_target_pairs={{0,2},{2,4},{4,6},{6,8},{8,10},{10,12},{12,14},{14,16},{16,18},{18... | collective-permute-start | bytes 786440 | tf_op jit(solution)/shard_map/ppermute | solution.py:338
  13.8 1.6 %collective-permute-done.rim_ref = bf16[128,1024]{1,0:T(8,128)(2,1)S(1)} collective-permute-done((bf16[128,1024]{1,0:T(8,128)(2,1)}, bf16[128,1024]{1,0:T(8,128)(2,1)S(1)}, u32[]{:S(2)}, u32[]{:S(2)}) %collective-permute-start) | collective-permute-done | bytes 262176 | tf_op jit(solution)/shard_map/ppermute | solution.py:338
  15.4 4.3 %collective-permute-start.1 = (bf16[128,1024]{1,0:T(8,128)(2,1)}, bf16[128,1024]{1,0:T(8,128)(2,1)S(1)}, u32[]{:S(2)}, u32[]{:S(2)}) collective-permute-start(bf16[128,1024]{1,0:T(8,128)(2,1)} %get-tuple-element.51), channel_id=1, source_target_pairs={{0,2},{2,4},{4,6},{6,8},{8,10},{10,12},{12,14},{14,16},{16,18},{18... | collective-permute-start | bytes 786440 | tf_op jit(solution)/shard_map/ppermute | solution.py:338
  19.7 1.3 collective-permute-done.2.rim_ref
  21.1 4.3 %collective-permute-start.3 = (bf16[128,1024]{1,0:T(8,128)(2,1)S(1)}, bf16[128,1024]{1,0:T(8,128)(2,1)S(1)}, u32[]{:S(2)}, u32[]{:S(2)}) collective-permute-start(bf16[128,1024]{1,0:T(8,128)(2,1)S(1)} %get-tuple-element.57), channel_id=1, source_target_pairs={{0,2},{2,4},{4,6},{6,8},{8,10},{10,12},{12,14},{14,16},{16,18},{18... | collective-permute-start | bytes 786440 | tf_op jit(solution)/shard_map/ppermute | solution.py:338
  25.4 2.3 %multiply_convert_fusion = (bf16[128,1024]{1,0:T(8,128)(2,1)}, bf16[128,1024]{1,0:T(8,128)(2,1)}, bf16[128,1024]{1,0:T(8,128)(2,1)S(1)}, bf16[128,1024]{1,0:T(8,128)(2,1)S(1)}) fusion(bf16[256,4096]{1,0:T(8,128)(2,1)S(1)} %copy-done, bf16[256,4096]{1,0:T(8,128)(2,1)} %ct_ref.15), kind=kLoop, calls=%fused_computation | loop fusion | flops 2097152 | bytes 3145728 | tf_op jit(solution)/shard_map/convert_element_type | solution.py:87
  27.7 13.2 %conv.4 = (bf16[256,4096]{1,0:T(8,128)(2,1)}, bf16[256,4096]{1,0:T(8,128)(2,1)}, f32[256,128]{1,0:T(8,128)S(1)}, f32[1,4096]{1,0:T(1,128)S(1)}) custom-call(s32[2]{0:T(128)S(1)} %pad_add_fusion.info, bf16[256,4096]{1,0:T(8,128)(2,1)S(1)} %copy-done, bf16[256,4096]{1,0:T(8,128)(2,1)S(1)} %copy-done.1, bf16[256,4096]{1,0:T(8,128)(2,1)} %k_ref.15, ...), custom_call_target="tpu_custom_call" | custom-call | flops 262144 | bytes 262144 | tf_op jit(solution)/shard_map/conv/pallas_call | solution.py:272
  40.9 13.2 %conv.5 = (bf16[256,4096]{1,0:T(8,128)(2,1)}, bf16[256,4096]{1,0:T(8,128)(2,1)}, f32[256,128]{1,0:T(8,128)S(1)}, f32[1,4096]{1,0:T(1,128)S(1)}) custom-call(s32[2]{0:T(128)S(1)} %pad_add_fusion.info, bf16[256,4096]{1,0:T(8,128)(2,1)S(1)} %copy-done, ...), custom_call_target="tpu_custom_call", output_to_operand_aliasing={{0}: (12, {}), {1}: (13, {}), {2}: (14, {}), {3}: (15, {})} | custom-call | flops 262144 | bytes 262144 | tf_op jit(solution)/shard_map/conv/pallas_call | solution.py:272
  54.1 13.2 %conv.6 = (bf16[256,4096]{1,0:T(8,128)(2,1)}, bf16[256,4096]{1,0:T(8,128)(2,1)}, f32[256,128]{1,0:T(8,128)S(1)}, f32[1,4096]{1,0:T(1,128)S(1)}) custom-call(s32[2]{0:T(128)S(1)} %pad_add_fusion.info, bf16[256,4096]{1,0:T(8,128)(2,1)S(1)} %copy-done, ...), custom_call_target="tpu_custom_call", output_to_operand_aliasing={{0}: (12, {}), {1}: (13, {}), {2}: (14, {}), {3}: (15, {})} | custom-call | flops 262144 | bytes 262144 | tf_op jit(solution)/shard_map/conv/pallas_call | solution.py:272
  67.4 13.2 %conv.7 = (bf16[256,4096]{1,0:T(8,128)(2,1)}, bf16[256,4096]{1,0:T(8,128)(2,1)}, f32[256,128]{1,0:T(8,128)S(1)}, f32[1,4096]{1,0:T(1,128)S(1)}) custom-call(s32[2]{0:T(128)S(1)} %pad_add_fusion.info, bf16[256,4096]{1,0:T(8,128)(2,1)S(1)} %copy-done, ...), custom_call_target="tpu_custom_call", output_to_operand_aliasing={{0}: (12, {}), {1}: (13, {}), {2}: (14, {}), {3}: (15, {})} | custom-call | flops 262144 | bytes 262144 | tf_op jit(solution)/shard_map/conv/pallas_call | solution.py:272
  80.6 2.3 %collective-permute-start.8 = (f32[288,128]{1,0:T(8,128)S(1)}, f32[288,128]{1,0:T(8,128)S(1)}, u32[]{:S(2)}, u32[]{:S(2)}) collective-permute-start(f32[288,128]{1,0:T(8,128)S(1)} %pad_maximum_fusion), channel_id=1, source_target_pairs={{0,2},{2,0},{4,6},{6,4},{8,10},{10,8},{12,14},{14,12},{16,18},{18,... | collective-permute-start | bytes 442376 | tf_op jit(solution)/shard_map/ppermute | solution.py:347
  85.5 1.8 %collective-permute-done.8 = f32[288,128]{1,0:T(8,128)S(1)} collective-permute-done((f32[288,128]{1,0:T(8,128)S(1)}, f32[288,128]{1,0:T(8,128)S(1)}, u32[]{:S(2)}, u32[]{:S(2)}) %collective-permute-start.8) | collective-permute-done | bytes 147488 | tf_op jit(solution)/shard_map/ppermute | solution.py:347
  87.3 3.0 %collective-permute-start.9 = (f32[288,128]{1,0:T(8,128)S(1)}, f32[288,128]{1,0:T(8,128)S(1)}, u32[]{:S(2)}, u32[]{:S(2)}) collective-permute-start(f32[288,128]{1,0:T(8,128)S(1)} %fusion.2), channel_id=1, source_target_pairs={{0,4},{2,6},{4,0},{6,2},{8,12},{10,14},{12,8},{14,10},{16,20},{18,... | collective-permute-start | bytes 442376 | tf_op jit(solution)/shard_map/ppermute | solution.py:347
  90.3 3.1 %collective-permute-done.9 = f32[288,128]{1,0:T(8,128)S(1)} collective-permute-done((f32[288,128]{1,0:T(8,128)S(1)}, f32[288,128]{1,0:T(8,128)S(1)}, u32[]{:S(2)}, u32[]{:S(2)}) %collective-permute-start.9) | collective-permute-done | bytes 147488 | tf_op jit(solution)/shard_map/ppermute | solution.py:347
  93.5 3.0 %collective-permute-start.10 = (f32[288,128]{1,0:T(8,128)S(1)}, f32[288,128]{1,0:T(8,128)S(1)}, u32[]{:S(2)}, u32[]{:S(2)}) collective-permute-start(f32[288,128]{1,0:T(8,128)S(1)} %add.19), channel_id=1, source_target_pairs={{0,8},{2,10},{4,12},{6,14},{8,0},{10,2},{12,4},{14,6},{16,24},{18,... | collective-permute-start | bytes 442376 | tf_op jit(solution)/shard_map/ppermute | solution.py:347
  98.6 1.5 collective-permute-start.5
  100.9 9.8 %collective-permute-start.11 = (f32[288,128]{1,0:T(8,128)S(1)}, f32[288,128]{1,0:T(8,128)}, u32[]{:S(2)}, u32[]{:S(2)}) collective-permute-start(f32[288,128]{1,0:T(8,128)S(1)} %add.20), channel_id=1, source_target_pairs={{0,16},{2,18},{4,20},{6,22},{8,24},{10,26},{12,28},{14,30},{16,0},... | collective-permute-start | bytes 442376 | tf_op jit(solution)/shard_map/ppermute | solution.py:347
  110.7 1.6 %copy-done.2 = bf16[256,4096]{1,0:T(8,128)(2,1)S(1)} copy-done((bf16[256,4096]{1,0:T(8,128)(2,1)S(1)}, bf16[256,4096]{1,0:T(8,128)(2,1)}, u32[]{:S(2)}) %copy-start.2) | copy-done | bytes 2097176
  112.3 8.4 %back.4 = (bf16[256,4096]{1,0:T(8,128)(2,1)}, bf16[256,4096]{1,0:T(8,128)(2,1)}) custom-call(s32[2]{0:T(128)S(1)} %pad_add_fusion.info, bf16[256,4096]{1,0:T(8,128)(2,1)S(1)} %copy-done, bf16[256,4096]{1,0:T(8,128)(2,1)S(1)} %copy-done.2, bf16[256,4096]{1,0:T(8,128)(2,1)} %k_ref.15, bf16[256,4096]{1,0:T(8,128)(2,1)} %v_ref.15, ...), custom_call_target="tpu_custom_call" | custom-call | flops 262144 | bytes 262144 | tf_op jit(solution)/shard_map/back/pallas_call | solution.py:272
  120.6 8.4 %back.5 = (bf16[256,4096]{1,0:T(8,128)(2,1)}, bf16[256,4096]{1,0:T(8,128)(2,1)}) custom-call(s32[2]{0:T(128)S(1)} %pad_add_fusion.info, bf16[256,4096]{1,0:T(8,128)(2,1)S(1)} %copy-done, bf16[256,4096]{1,0:T(8,128)(2,1)S(1)} %copy-done.2, bf16[256,4096]{1,0:T(8,128)(2,1)} %k_ref.15, ...), custom_call_target="tpu_custom_call", output_to_operand_aliasing={{0}: (11, {}), {1}: (12, {})} | custom-call | flops 262144 | bytes 262144 | tf_op jit(solution)/shard_map/back/pallas_call | solution.py:272
  129.0 8.4 %back.6 = (bf16[256,4096]{1,0:T(8,128)(2,1)}, bf16[256,4096]{1,0:T(8,128)(2,1)}) custom-call(s32[2]{0:T(128)S(1)} %pad_add_fusion.info, bf16[256,4096]{1,0:T(8,128)(2,1)S(1)} %copy-done, bf16[256,4096]{1,0:T(8,128)(2,1)S(1)} %copy-done.2, bf16[256,4096]{1,0:T(8,128)(2,1)} %k_ref.15, ...), custom_call_target="tpu_custom_call", output_to_operand_aliasing={{0}: (11, {}), {1}: (12, {})} | custom-call | flops 262144 | bytes 262144 | tf_op jit(solution)/shard_map/back/pallas_call | solution.py:272
  137.4 8.4 %back.7 = (bf16[256,4096]{1,0:T(8,128)(2,1)}, bf16[256,4096]{1,0:T(8,128)(2,1)}) custom-call(s32[2]{0:T(128)S(1)} %pad_add_fusion.info, bf16[256,4096]{1,0:T(8,128)(2,1)S(1)} %copy-done, bf16[256,4096]{1,0:T(8,128)(2,1)S(1)} %copy-done.2, bf16[256,4096]{1,0:T(8,128)(2,1)} %k_ref.15, ...), custom_call_target="tpu_custom_call", output_to_operand_aliasing={{0}: (11, {}), {1}: (12, {})} | custom-call | flops 262144 | bytes 262144 | tf_op jit(solution)/shard_map/back/pallas_call | solution.py:272
  (37 shorter events, 10.6 us)
Async XLA Ops:
  0.6 11.2 %copy-start.5 = (s32[4096]{0:T(1024)S(1)}, s32[4096]{0:T(1024)}, u32[]{:S(2)}) copy-start(s32[4096]{0:T(1024)} %param.13) | copy-start | bytes 49156
  0.6 24.7 %copy-start = (bf16[256,4096]{1,0:T(8,128)(2,1)S(1)}, bf16[256,4096]{1,0:T(8,128)(2,1)}, u32[]{:S(2)}) copy-start(bf16[256,4096]{1,0:T(8,128)(2,1)} %q_ref.15) | copy-start | bytes 6291460
  3.5 24.2 %copy-start.3 = (f32[512,128]{1,0:T(8,128)S(1)}, f32[512,128]{1,0:T(8,128)}, u32[]{:S(2)}) copy-start(f32[512,128]{1,0:T(8,128)} %taps_ref.15) | copy-start | bytes 786436
  3.5 24.2 %copy-start.4 = (f32[4096]{0:T(1024)S(1)}, f32[4096]{0:T(1024)}, u32[]{:S(2)}) copy-start(f32[4096]{0:T(1024)} %param.12) | copy-start | bytes 49156
  3.5 12.0 %collective-permute-start = (bf16[128,1024]{1,0:T(8,128)(2,1)}, bf16[128,1024]{1,0:T(8,128)(2,1)S(1)}, u32[]{:S(2)}, u32[]{:S(2)}) collective-permute-start(bf16[128,1024]{1,0:T(8,128)(2,1)} %get-tuple-element.100), channel_id=1, source_target_pairs={{0,2},{2,4},{4,6},{6,8},{8,10},{10,12},{12,14},{14,16},{16,18},{18... | collective-permute-start | bytes 786440 | tf_op jit(solution)/shard_map/ppermute | solution.py:338
  8.5 12.6 %collective-permute-start.2 = (bf16[128,1024]{1,0:T(8,128)(2,1)}, bf16[128,1024]{1,0:T(8,128)(2,1)S(1)}, u32[]{:S(2)}, u32[]{:S(2)}) collective-permute-start(bf16[128,1024]{1,0:T(8,128)(2,1)} %get-tuple-element.98), channel_id=1, source_target_pairs={{0,2},{2,4},{4,6},{6,8},{8,10},{10,12},{12,14},{14,16},{16,18},{18... | collective-permute-start | bytes 786440 | tf_op jit(solution)/shard_map/ppermute | solution.py:338
  11.9 15.8 %copy-start.1 = (bf16[256,4096]{1,0:T(8,128)(2,1)S(1)}, bf16[256,4096]{1,0:T(8,128)(2,1)}, u32[]{:S(2)}) copy-start(bf16[256,4096]{1,0:T(8,128)(2,1)} %ct_ref.15) | copy-start | bytes 6291460
  15.4 38.7 %collective-permute-start.1 = (bf16[128,1024]{1,0:T(8,128)(2,1)}, bf16[128,1024]{1,0:T(8,128)(2,1)S(1)}, u32[]{:S(2)}, u32[]{:S(2)}) collective-permute-start(bf16[128,1024]{1,0:T(8,128)(2,1)} %get-tuple-element.51), channel_id=1, source_target_pairs={{0,2},{2,4},{4,6},{6,8},{8,10},{10,12},{12,14},{14,16},{16,18},{18... | collective-permute-start | bytes 786440 | tf_op jit(solution)/shard_map/ppermute | solution.py:338
  21.1 33.1 %collective-permute-start.3 = (bf16[128,1024]{1,0:T(8,128)(2,1)S(1)}, bf16[128,1024]{1,0:T(8,128)(2,1)S(1)}, u32[]{:S(2)}, u32[]{:S(2)}) collective-permute-start(bf16[128,1024]{1,0:T(8,128)(2,1)S(1)} %get-tuple-element.57), channel_id=1, source_target_pairs={{0,2},{2,4},{4,6},{6,8},{8,10},{10,12},{12,14},{14,16},{16,18},{18... | collective-permute-start | bytes 786440 | tf_op jit(solution)/shard_map/ppermute | solution.py:338
  80.6 6.7 %collective-permute-start.8 = (f32[288,128]{1,0:T(8,128)S(1)}, f32[288,128]{1,0:T(8,128)S(1)}, u32[]{:S(2)}, u32[]{:S(2)}) collective-permute-start(f32[288,128]{1,0:T(8,128)S(1)} %pad_maximum_fusion), channel_id=1, source_target_pairs={{0,2},{2,0},{4,6},{6,4},{8,10},{10,8},{12,14},{14,12},{16,18},{18,... | collective-permute-start | bytes 442376 | tf_op jit(solution)/shard_map/ppermute | solution.py:347
  82.9 15.7 %collective-permute-start.4 = (bf16[128,1024]{1,0:T(8,128)(2,1)S(1)}, bf16[128,1024]{1,0:T(8,128)(2,1)S(1)}, u32[]{:S(2)}, u32[]{:S(2)}) collective-permute-start(bf16[128,1024]{1,0:T(8,128)(2,1)S(1)} %get-tuple-element.75), channel_id=1, source_target_pairs={{2,0},{4,2},{6,4},{8,6},{10,8},{12,10},{14,12},{16,14},{18,16},{20... | collective-permute-start | bytes 786440 | tf_op jit(solution)/shard_map/ppermute | solution.py:338
  84.2 13.1 %collective-permute-start.6 = (bf16[128,1024]{1,0:T(8,128)(2,1)S(1)}, bf16[128,1024]{1,0:T(8,128)(2,1)S(1)}, u32[]{:S(2)}, u32[]{:S(2)}) collective-permute-start(bf16[128,1024]{1,0:T(8,128)(2,1)S(1)} %get-tuple-element.80), channel_id=1, source_target_pairs={{2,0},{4,2},{6,4},{8,6},{10,8},{12,10},{14,12},{16,14},{18,16},{20... | collective-permute-start | bytes 786440 | tf_op jit(solution)/shard_map/ppermute | solution.py:338
  87.3 6.2 %collective-permute-start.9 = (f32[288,128]{1,0:T(8,128)S(1)}, f32[288,128]{1,0:T(8,128)S(1)}, u32[]{:S(2)}, u32[]{:S(2)}) collective-permute-start(f32[288,128]{1,0:T(8,128)S(1)} %fusion.2), channel_id=1, source_target_pairs={{0,4},{2,6},{4,0},{6,2},{8,12},{10,14},{12,8},{14,10},{16,20},{18,... | collective-permute-start | bytes 442376 | tf_op jit(solution)/shard_map/ppermute | solution.py:347
  93.5 7.4 %collective-permute-start.10 = (f32[288,128]{1,0:T(8,128)S(1)}, f32[288,128]{1,0:T(8,128)S(1)}, u32[]{:S(2)}, u32[]{:S(2)}) collective-permute-start(f32[288,128]{1,0:T(8,128)S(1)} %add.19), channel_id=1, source_target_pairs={{0,8},{2,10},{4,12},{6,14},{8,0},{10,2},{12,4},{14,6},{16,24},{18,... | collective-permute-start | bytes 442376 | tf_op jit(solution)/shard_map/ppermute | solution.py:347
  97.3 31.8 %collective-permute-start.7 = (bf16[128,1024]{1,0:T(8,128)(2,1)}, bf16[128,1024]{1,0:T(8,128)(2,1)}, u32[]{:S(2)}, u32[]{:S(2)}) collective-permute-start(bf16[128,1024]{1,0:T(8,128)(2,1)} %get-tuple-element.81), channel_id=1, source_target_pairs={{2,0},{4,2},{6,4},{8,6},{10,8},{12,10},{14,12},{16,14},{18,16},{20... | collective-permute-start | bytes 786440 | tf_op jit(solution)/shard_map/ppermute | solution.py:338
  98.6 38.9 %collective-permute-start.5 = (bf16[128,1024]{1,0:T(8,128)(2,1)}, bf16[128,1024]{1,0:T(8,128)(2,1)S(1)}, u32[]{:S(2)}, u32[]{:S(2)}) collective-permute-start(bf16[128,1024]{1,0:T(8,128)(2,1)} %get-tuple-element.76), channel_id=1, source_target_pairs={{2,0},{4,2},{6,4},{8,6},{10,8},{12,10},{14,12},{16,14},{18,16},{20... | collective-permute-start | bytes 786440 | tf_op jit(solution)/shard_map/ppermute | solution.py:338
  100.9 44.9 %collective-permute-start.11 = (f32[288,128]{1,0:T(8,128)S(1)}, f32[288,128]{1,0:T(8,128)}, u32[]{:S(2)}, u32[]{:S(2)}) collective-permute-start(f32[288,128]{1,0:T(8,128)S(1)} %add.20), channel_id=1, source_target_pairs={{0,16},{2,18},{4,20},{6,22},{8,24},{10,26},{12,28},{14,30},{16,0},... | collective-permute-start | bytes 442376 | tf_op jit(solution)/shard_map/ppermute | solution.py:347
  110.7 1.6 %copy-start.2 = (bf16[256,4096]{1,0:T(8,128)(2,1)S(1)}, bf16[256,4096]{1,0:T(8,128)(2,1)}, u32[]{:S(2)}) copy-start(bf16[256,4096]{1,0:T(8,128)(2,1)} %ct_ref.15) | copy-start | bytes 6291460
  146.8 1.4 collective-permute-start.12

commit v3 on v2

--- a/solution.py
+++ b/solution.py
@@ -13,7 +13,7 @@
 TB = 16
 WIDE = 256
 KINDS = 3
-PARTS = 4
+PARTS = 2
 IN_FLIGHT = 2
 
 
@@ -105,6 +105,14 @@
     for kind in range(1, KINDS):
         rows.append(jnp.concatenate([zero, jnp.where(pos == kind, pltpu.roll(own, kind * TB, 1), zero)], axis=1))
     return jnp.concatenate(rows, axis=0)
+
+
+def both(one, two):
+    rows, width = one[0].shape[0], one[1].shape[1]
+    taps = jnp.concatenate([one[0], two[0]], axis=0)
+    window = jnp.concatenate([one[1], two[1]], axis=1)
+    y = jnp.dot(taps, window, preferred_element_type=F32)
+    return y[:rows, :width], y[rows:, width:]
 
 
 def chosen(products, sel_ref):
@@ -136,6 +144,7 @@
         rims = to_groups(rim_ref[:, lanes], bits, chunk)
         taps = taps_ref[pl.ds(pl.multiple_of(sub * per, per), per), :].astype(BF16)
         taps = jnp.dot(taps, permutation(filter_size), preferred_element_type=F32)
+        pair = []
         for g in range(per):
             xg, dyg = side_by_side(xs[g]), side_by_side(dys[g])
             if further:
@@ -143,8 +152,10 @@
             window = windows(rims[g] + xs[g], pos, chunk, steps) + [xg] * (KINDS - 1)
             window = jnp.concatenate(window, axis=0) * mask_ref[...]
             band_taps = shifted_taps(taps[g : g + 1], 1)
-            band_taps = with_kinds(band_taps, band_taps[:, LANES:], chunk)
-            conv_s[slot, g] = chosen(jnp.dot(band_taps[:, :depth], window, preferred_element_type=F32), sel_ref)
+            pair.append((with_kinds(band_taps, band_taps[:, LANES:], chunk)[:, :depth], window))
+            if g % 2:
+                conv_s[slot, g - 1], conv_s[slot, g] = [chosen(y, sel_ref) for y in both(*pair)]
+                pair = []
             turned = jnp.dot(permutation(TB), dyg, preferred_element_type=F32).astype(BF16)
             turned = jnp.concatenate([turned] * KINDS, axis=0) * turned_ref[...]
             pairs = lax.dot_general(turned, window, (((1,), (1,)), ((), ())), preferred_element_type=F32)
@@ -201,6 +212,7 @@
         dy = product_bf16(ct_ref[:, lanes], q_ref[:, lanes])
         dys, rims = to_groups(dy, bits, chunk), to_groups(rim_ref[:, lanes], bits, chunk)
         taps = taps_ref[pl.ds(pl.multiple_of(sub * per, per), per), :]
+        pair = []
         for g in range(per):
             dyg = side_by_side(dys[g])
             if further:
@@ -208,8 +220,10 @@
             window = windows(dys[g] + rims[g], pos, chunk, steps) + [dyg] * (KINDS - 1)
             window = jnp.concatenate(window, axis=0) * mask_ref[...]
             band_taps = shifted_taps(taps[g : g + 1], 0)
-            band_taps = with_kinds(band_taps, band_taps[:, :LANES], chunk)
-            back_s[slot, g] = chosen(jnp.dot(band_taps[:, :depth], window, preferred_element_type=F32), sel_ref)
+            pair.append((with_kinds(band_taps, band_taps[:, :LANES], chunk)[:, :depth], window))
+            if g % 2:
+                back_s[slot, g - 1], back_s[slot, g] = [chosen(y, sel_ref) for y in both(*pair)]
+                pair = []
 
         def more(index, carry):
             level, g = index // per, index % per

time: 149 us -> 157 us (1.054)
  the two profiles are of different devices: /device:TPU:0 before, /device:TPU:11 now
where the time goes in v3:
time: 157 us
  Pallas kernels  80 us (51%)
  waiting for transfers between devices  45.2 us (29%)
  starting transfers between devices  19.1 us (12%)
  other arithmetic  9.52 us (6%)
  local copies, waits for them, and re-layouts  2.43 us (2%)
    pallas_call x4, Pallas kernels, run_part(): pl.pallas_call(functools.partial(kernel, chunk), grid_spec=pltpu.Prefetch...  78.9 us
    ppermute x4, waiting for transfers between devices, sum_over(): lax.ppermute(value, axis, [(i, i ^ step) for i in range(count)])  29.6 us
    ppermute x4, waiting for transfers between devices, passed_along(): lax.ppermute(value, axis, [(source, source + steps) for source in range(i...  15.3 us
    ppermute x4, starting transfers between devices, passed_along(): lax.ppermute(value, axis, [(source, source + steps) for source in range(i...  11.6 us
    ppermute x4, starting transfers between devices, sum_over(): lax.ppermute(value, axis, [(i, i ^ step) for i in range(count)])  5.81 us
    convert_element_type x2, other arithmetic, product_bf16(): return (a.astype(F32) * b.astype(F32)).astype(BF16)  5.63 us
  transfers between devices with their start and end apart: 9, of which 5 were waited for; matrix products, arithmetic and copies ran while one was open for 3% of the time, Pallas kernels for 20%

profile of v3, /device:TPU:11, one launch (start us, length us, event | category | flops | bytes accessed | tf_op | source)
XLA Modules:
  0.0 157.0 jit_solution(16832108421053775306)
XLA Ops:
  0.7 3.0 %multiply_convert_fusion = (bf16[128,2048]{1,0:T(8,128)(2,1)}, bf16[128,2048]{1,0:T(8,128)(2,1)}) fusion(bf16[256,4096]{1,0:T(8,128)(2,1)} %v_ref.7, bf16[256,4096]{1,0:T(8,128)(2,1)} %k_ref.7), kind=kLoop, calls=%fused_computation | loop fusion | flops 2097152 | bytes 3145728 | tf_op jit(solution)/shard_map/convert_element_type | solution.py:87
  3.7 3.2 %collective-permute-start = (bf16[128,2048]{1,0:T(8,128)(2,1)}, bf16[128,2048]{1,0:T(8,128)(2,1)S(1)}, u32[]{:S(2)}, u32[]{:S(2)}) collective-permute-start(bf16[128,2048]{1,0:T(8,128)(2,1)} %get-tuple-element.55), channel_id=1, source_target_pairs={{0,2},{2,4},{4,6},{6,8},{8,10},{10,12},{12,14},{14,16},{16,18},{18... | collective-permute-start | bytes 1572872 | tf_op jit(solution)/shard_map/ppermute | solution.py:352
  6.9 3.1 %collective-permute-start.1 = (bf16[128,2048]{1,0:T(8,128)(2,1)}, bf16[128,2048]{1,0:T(8,128)(2,1)S(1)}, u32[]{:S(2)}, u32[]{:S(2)}) collective-permute-start(bf16[128,2048]{1,0:T(8,128)(2,1)} %get-tuple-element.54), channel_id=1, source_target_pairs={{0,2},{2,4},{4,6},{6,8},{8,10},{10,12},{12,14},{14,16},{16,18},{18... | collective-permute-start | bytes 1572872 | tf_op jit(solution)/shard_map/ppermute | solution.py:352
  10.2 1.1 resets.1
  11.3 0.7 pad_add_fusion.info
  12.1 2.6 %multiply_convert_fusion.1 = (bf16[128,2048]{1,0:T(8,128)(2,1)}, bf16[128,2048]{1,0:T(8,128)(2,1)}) fusion(bf16[256,4096]{1,0:T(8,128)(2,1)S(1)} %copy-done, bf16[256,4096]{1,0:T(8,128)(2,1)} %ct_ref.7), kind=kLoop, calls=%fused_computation.1 | loop fusion | flops 2097152 | bytes 3145728 | tf_op jit(solution)/shard_map/convert_element_type | solution.py:87
  14.7 4.0 %collective-permute-done.rim_ref = bf16[128,2048]{1,0:T(8,128)(2,1)S(1)} collective-permute-done((bf16[128,2048]{1,0:T(8,128)(2,1)}, bf16[128,2048]{1,0:T(8,128)(2,1)S(1)}, u32[]{:S(2)}, u32[]{:S(2)}) %collective-permute-start) | collective-permute-done | bytes 524320 | tf_op jit(solution)/shard_map/ppermute | solution.py:352
  18.7 11.2 %collective-permute-done.1.rim_ref = bf16[128,2048]{1,0:T(8,128)(2,1)S(1)} collective-permute-done((bf16[128,2048]{1,0:T(8,128)(2,1)}, bf16[128,2048]{1,0:T(8,128)(2,1)S(1)}, u32[]{:S(2)}, u32[]{:S(2)}) %collective-permute-start.1) | collective-permute-done | bytes 524320 | tf_op jit(solution)/shard_map/ppermute | solution.py:352
  30.0 24.7 %conv.2 = (bf16[256,4096]{1,0:T(8,128)(2,1)}, bf16[256,4096]{1,0:T(8,128)(2,1)}, f32[256,128]{1,0:T(8,128)S(1)}, f32[1,4096]{1,0:T(1,128)S(1)}) custom-call(s32[2]{0:T(128)S(1)} %pad_add_fusion.info, bf16[256,4096]{1,0:T(8,128)(2,1)S(1)} %copy-done, bf16[256,4096]{1,0:T(8,128)(2,1)S(1)} %copy-done.1, bf16[256,4096]{1,0:T(8,128)(2,1)} %k_ref.7, ...), custom_call_target="tpu_custom_call" | custom-call | flops 524288 | bytes 524288 | tf_op jit(solution)/shard_map/conv/pallas_call | solution.py:286
  54.6 24.7 %conv.3 = (bf16[256,4096]{1,0:T(8,128)(2,1)}, bf16[256,4096]{1,0:T(8,128)(2,1)}, f32[256,128]{1,0:T(8,128)S(1)}, f32[1,4096]{1,0:T(1,128)S(1)}) custom-call(s32[2]{0:T(128)S(1)} %pad_add_fusion.info, bf16[256,4096]{1,0:T(8,128)(2,1)S(1)} %copy-done, ...), custom_call_target="tpu_custom_call", output_to_operand_aliasing={{0}: (12, {}), {1}: (13, {}), {2}: (14, {}), {3}: (15, {})} | custom-call | flops 524288 | bytes 524288 | tf_op jit(solution)/shard_map/conv/pallas_call | solution.py:286
  79.3 2.1 %collective-permute-start.4 = (f32[288,128]{1,0:T(8,128)S(1)}, f32[288,128]{1,0:T(8,128)S(1)}, u32[]{:S(2)}, u32[]{:S(2)}) collective-permute-start(f32[288,128]{1,0:T(8,128)S(1)} %pad_maximum_fusion), channel_id=1, source_target_pairs={{0,2},{2,0},{4,6},{6,4},{8,10},{10,8},{12,14},{14,12},{16,18},{18,... | collective-permute-start | bytes 442376 | tf_op jit(solution)/shard_map/ppermute | solution.py:361
  81.4 1.9 %collective-permute-start.2 = (bf16[128,2048]{1,0:T(8,128)(2,1)}, bf16[128,2048]{1,0:T(8,128)(2,1)S(1)}, u32[]{:S(2)}, u32[]{:S(2)}) collective-permute-start(bf16[128,2048]{1,0:T(8,128)(2,1)} %get-tuple-element.43), channel_id=1, source_target_pairs={{2,0},{4,2},{6,4},{8,6},{10,8},{12,10},{14,12},{16,14},{18,16},{20... | collective-permute-start | bytes 1572872 | tf_op jit(solution)/shard_map/ppermute | solution.py:352
  83.4 3.3 %collective-permute-start.3 = (bf16[128,2048]{1,0:T(8,128)(2,1)}, bf16[128,2048]{1,0:T(8,128)(2,1)S(1)}, u32[]{:S(2)}, u32[]{:S(2)}) collective-permute-start(bf16[128,2048]{1,0:T(8,128)(2,1)} %get-tuple-element.47), channel_id=1, source_target_pairs={{2,0},{4,2},{6,4},{8,6},{10,8},{12,10},{14,12},{16,14},{18,16},{20... | collective-permute-start | bytes 1572872 | tf_op jit(solution)/shard_map/ppermute | solution.py:352
  86.7 1.3 collective-permute-start.5
  88.0 24.7 %collective-permute-done.5 = f32[288,128]{1,0:T(8,128)S(1)} collective-permute-done((f32[288,128]{1,0:T(8,128)S(1)}, f32[288,128]{1,0:T(8,128)S(1)}, u32[]{:S(2)}, u32[]{:S(2)}) %collective-permute-start.5) | collective-permute-done | bytes 147488 | tf_op jit(solution)/shard_map/ppermute | solution.py:361
  112.8 4.9 %collective-permute-done.6 = f32[288,128]{1,0:T(8,128)S(1)} collective-permute-done((f32[288,128]{1,0:T(8,128)S(1)}, f32[288,128]{1,0:T(8,128)S(1)}, u32[]{:S(2)}, u32[]{:S(2)}) %collective-permute-start.6) | collective-permute-done | bytes 147488 | tf_op jit(solution)/shard_map/ppermute | solution.py:361
  118.3 2.3 %collective-permute-start.7 = (f32[288,128]{1,0:T(8,128)}, f32[288,128]{1,0:T(8,128)}, u32[]{:S(2)}, u32[]{:S(2)}) collective-permute-start(f32[288,128]{1,0:T(8,128)} %add.20), channel_id=1, source_target_pairs={{0,16},{2,18},{4,20},{6,22},{8,24},{10,26},{12,28},{14,30},{16,0},... | collective-permute-start | bytes 442376 | tf_op jit(solution)/shard_map/ppermute | solution.py:361
  120.7 1.6 %copy-done.2 = bf16[256,4096]{1,0:T(8,128)(2,1)S(1)} copy-done((bf16[256,4096]{1,0:T(8,128)(2,1)S(1)}, bf16[256,4096]{1,0:T(8,128)(2,1)}, u32[]{:S(2)}) %copy-start.2) | copy-done | bytes 2097176
  122.3 0.8 copy-done.6
  123.1 14.8 %back.2 = (bf16[256,4096]{1,0:T(8,128)(2,1)}, bf16[256,4096]{1,0:T(8,128)(2,1)}) custom-call(s32[2]{0:T(128)S(1)} %pad_add_fusion.info, bf16[256,4096]{1,0:T(8,128)(2,1)S(1)} %copy-done, bf16[256,4096]{1,0:T(8,128)(2,1)S(1)} %copy-done.2, bf16[256,4096]{1,0:T(8,128)(2,1)} %k_ref.7, bf16[256,4096]{1,0:T(8,128)(2,1)} %v_ref.7, ...), custom_call_target="tpu_custom_call" | custom-call | flops 524288 | bytes 524288 | tf_op jit(solution)/shard_map/back/pallas_call | solution.py:286
  137.8 14.8 %back.3 = (bf16[256,4096]{1,0:T(8,128)(2,1)}, bf16[256,4096]{1,0:T(8,128)(2,1)}) custom-call(s32[2]{0:T(128)S(1)} %pad_add_fusion.info, bf16[256,4096]{1,0:T(8,128)(2,1)S(1)} %copy-done, bf16[256,4096]{1,0:T(8,128)(2,1)S(1)} %copy-done.2, bf16[256,4096]{1,0:T(8,128)(2,1)} %k_ref.7, ...), custom_call_target="tpu_custom_call", output_to_operand_aliasing={{0}: (11, {}), {1}: (12, {})} | custom-call | flops 524288 | bytes 524288 | tf_op jit(solution)/shard_map/back/pallas_call | solution.py:286
  152.6 1.0 add.21
  153.6 1.7 %collective-permute-start.8 = (f32[256,128]{1,0:T(8,128)S(1)}, f32[256,128]{1,0:T(8,128)S(1)}, u32[]{:S(2)}, u32[]{:S(2)}) collective-permute-start(f32[256,128]{1,0:T(8,128)S(1)} %slice.40), channel_id=1, source_target_pairs={{0,1},{1,0},{2,3},{3,2},{4,5},{5,4},{6,7},{7,6},{8,9},{9,8},{10,11... | collective-permute-start | bytes 393224 | tf_op jit(solution)/shard_map/ppermute | solution.py:370
  156.3 0.7 maximum_multiply_fusion
  (29 shorter events, 1.9 us)
Async XLA Ops:
  0.6 9.4 %copy-start.7 = (s32[4096]{0:T(1024)S(1)}, s32[4096]{0:T(1024)}, u32[]{:S(2)}) copy-start(s32[4096]{0:T(1024)} %param.13) | copy-start | bytes 49156
  0.6 11.4 %copy-start = (bf16[256,4096]{1,0:T(8,128)(2,1)S(1)}, bf16[256,4096]{1,0:T(8,128)(2,1)}, u32[]{:S(2)}) copy-start(bf16[256,4096]{1,0:T(8,128)(2,1)} %q_ref.7) | copy-start | bytes 6291460
  3.7 26.3 %copy-start.3 = (f32[512,128]{1,0:T(8,128)S(1)}, f32[512,128]{1,0:T(8,128)}, u32[]{:S(2)}) copy-start(f32[512,128]{1,0:T(8,128)} %taps_ref.7) | copy-start | bytes 786436
  3.7 26.3 %copy-start.4 = (f32[4096]{0:T(1024)S(1)}, f32[4096]{0:T(1024)}, u32[]{:S(2)}) copy-start(f32[4096]{0:T(1024)} %param.12) | copy-start | bytes 49156
  3.7 15.0 %collective-permute-start = (bf16[128,2048]{1,0:T(8,128)(2,1)}, bf16[128,2048]{1,0:T(8,128)(2,1)S(1)}, u32[]{:S(2)}, u32[]{:S(2)}) collective-permute-start(bf16[128,2048]{1,0:T(8,128)(2,1)} %get-tuple-element.55), channel_id=1, source_target_pairs={{0,2},{2,4},{4,6},{6,8},{8,10},{10,12},{12,14},{14,16},{16,18},{18... | collective-permute-start | bytes 1572872 | tf_op jit(solution)/shard_map/ppermute | solution.py:352
  6.9 23.0 %collective-permute-start.1 = (bf16[128,2048]{1,0:T(8,128)(2,1)}, bf16[128,2048]{1,0:T(8,128)(2,1)S(1)}, u32[]{:S(2)}, u32[]{:S(2)}) collective-permute-start(bf16[128,2048]{1,0:T(8,128)(2,1)} %get-tuple-element.54), channel_id=1, source_target_pairs={{0,2},{2,4},{4,6},{6,8},{8,10},{10,12},{12,14},{14,16},{16,18},{18... | collective-permute-start | bytes 1572872 | tf_op jit(solution)/shard_map/ppermute | solution.py:352
  10.1 19.9 %copy-start.1 = (bf16[256,4096]{1,0:T(8,128)(2,1)S(1)}, bf16[256,4096]{1,0:T(8,128)(2,1)}, u32[]{:S(2)}) copy-start(bf16[256,4096]{1,0:T(8,128)(2,1)} %ct_ref.7) | copy-start | bytes 6291460
  11.3 18.6 %copy-start.5 = (f32[48,256]{1,0:T(8,128)}, f32[48,256]{1,0:T(8,128)S(1)}, u32[]{:S(2)}) copy-start(f32[48,256]{1,0:T(8,128)S(1)} %get-tuple-element.45.sel_ref) | copy-start | bytes 147460
  79.3 7.3 %collective-permute-start.4 = (f32[288,128]{1,0:T(8,128)S(1)}, f32[288,128]{1,0:T(8,128)S(1)}, u32[]{:S(2)}, u32[]{:S(2)}) collective-permute-start(f32[288,128]{1,0:T(8,128)S(1)} %pad_maximum_fusion), channel_id=1, source_target_pairs={{0,2},{2,0},{4,6},{6,4},{8,10},{10,8},{12,14},{14,12},{16,18},{18,... | collective-permute-start | bytes 442376 | tf_op jit(solution)/shard_map/ppermute | solution.py:361
  81.4 56.4 %collective-permute-start.2 = (bf16[128,2048]{1,0:T(8,128)(2,1)}, bf16[128,2048]{1,0:T(8,128)(2,1)S(1)}, u32[]{:S(2)}, u32[]{:S(2)}) collective-permute-start(bf16[128,2048]{1,0:T(8,128)(2,1)} %get-tuple-element.43), channel_id=1, source_target_pairs={{2,0},{4,2},{6,4},{8,6},{10,8},{12,10},{14,12},{16,14},{18,16},{20... | collective-permute-start | bytes 1572872 | tf_op jit(solution)/shard_map/ppermute | solution.py:352
  83.4 37.3 %collective-permute-start.3 = (bf16[128,2048]{1,0:T(8,128)(2,1)}, bf16[128,2048]{1,0:T(8,128)(2,1)S(1)}, u32[]{:S(2)}, u32[]{:S(2)}) collective-permute-start(bf16[128,2048]{1,0:T(8,128)(2,1)} %get-tuple-element.47), channel_id=1, source_target_pairs={{2,0},{4,2},{6,4},{8,6},{10,8},{12,10},{14,12},{16,14},{18,16},{20... | collective-permute-start | bytes 1572872 | tf_op jit(solution)/shard_map/ppermute | solution.py:352
  86.7 26.0 %collective-permute-start.5 = (f32[288,128]{1,0:T(8,128)S(1)}, f32[288,128]{1,0:T(8,128)S(1)}, u32[]{:S(2)}, u32[]{:S(2)}) collective-permute-start(f32[288,128]{1,0:T(8,128)S(1)} %fusion.2), channel_id=1, source_target_pairs={{0,4},{2,6},{4,0},{6,2},{8,12},{10,14},{12,8},{14,10},{16,20},{18,... | collective-permute-start | bytes 442376 | tf_op jit(solution)/shard_map/ppermute | solution.py:361
  112.7 5.0 %collective-permute-start.6 = (f32[288,128]{1,0:T(8,128)S(1)}, f32[288,128]{1,0:T(8,128)S(1)}, u32[]{:S(2)}, u32[]{:S(2)}) collective-permute-start(f32[288,128]{1,0:T(8,128)S(1)} %add.19), channel_id=1, source_target_pairs={{0,8},{2,10},{4,12},{6,14},{8,0},{10,2},{12,4},{14,6},{16,24},{18,... | collective-permute-start | bytes 442376 | tf_op jit(solution)/shard_map/ppermute | solution.py:361
  118.3 34.2 %collective-permute-start.7 = (f32[288,128]{1,0:T(8,128)}, f32[288,128]{1,0:T(8,128)}, u32[]{:S(2)}, u32[]{:S(2)}) collective-permute-start(f32[288,128]{1,0:T(8,128)} %add.20), channel_id=1, source_target_pairs={{0,16},{2,18},{4,20},{6,22},{8,24},{10,26},{12,28},{14,30},{16,0},... | collective-permute-start | bytes 442376 | tf_op jit(solution)/shard_map/ppermute | solution.py:361
  120.7 1.6 %copy-start.2 = (bf16[256,4096]{1,0:T(8,128)(2,1)S(1)}, bf16[256,4096]{1,0:T(8,128)(2,1)}, u32[]{:S(2)}) copy-start(bf16[256,4096]{1,0:T(8,128)(2,1)} %ct_ref.7) | copy-start | bytes 6291460
  122.3 0.8 copy-start.6
  153.6 2.7 %collective-permute-start.8 = (f32[256,128]{1,0:T(8,128)S(1)}, f32[256,128]{1,0:T(8,128)S(1)}, u32[]{:S(2)}, u32[]{:S(2)}) collective-permute-start(f32[256,128]{1,0:T(8,128)S(1)} %slice.40), channel_id=1, source_target_pairs={{0,1},{1,0},{2,3},{3,2},{4,5},{5,4},{6,7},{7,6},{8,9},{9,8},{10,11... | collective-permute-start | bytes 393224 | tf_op jit(solution)/shard_map/ppermute | solution.py:370

commit v4 on v2

v4 whole, which is shorter than its diff:
```python
import functools
import math

import jax
import jax.numpy as jnp
from jax import lax
from jax.experimental import pallas as pl
from jax.experimental.pallas import tpu as pltpu
from jax.sharding import PartitionSpec as P

F32, BF16 = jnp.float32, jnp.bfloat16
LANES = 128
TB = 16
WIDE = 256
KINDS = 3
PARTS = 2
TOGETHER = 2


def iota(shape, axis):
    return lax.broadcasted_iota(jnp.int32, shape, axis)


def flag(condition, kind=BF16):
    return jnp.where(condition, 1.0, 0.0).astype(kind)


def permutation(size):
    return flag(iota((size, size), 0) + iota((size, size), 1) == size - 1)


def chunk_of(shape, kind, chunk):
    return (iota(shape, 1) // chunk).astype(F32).astype(kind)


def swap_chunks(arrays, bits, chunk):
    count = len(arrays)
    turned = [pltpu.roll(a, n * chunk, 1) if n else a for n, a in enumerate(arrays)]
    rows = [turned[(-i) % count] for i in range(count)]
    for power, moved in enumerate(bits):
        bit = 1 << power
        rows = [jnp.where(moved, rows[(i - bit) % count], rows[i]) for i in range(count)]
    return [pltpu.roll(a, LANES - n * chunk, 1) if n else a for n, a in enumerate(rows)]


def chunk_bits(kind, chunk):
    pos = iota((TB, LANES), 1) // chunk
    return [flag((pos >> power) & 1 == 1, kind) > 0 for power in range((LANES // chunk).bit_length() - 1)]


def to_groups(block, bits, chunk):
    per = LANES // chunk
    sets = []
    for first in range(0, block.shape[0], TB * per):
        parts = [block[first + TB * n : first + TB * (n + 1)] for n in range(per)]
        sets.append(swap_chunks(parts, bits, chunk))
    return [[s[g] for s in sets] for g in range(per)]


def from_groups(chunked, bits, chunk):
    rows = []
    for first in range(0, chunked[0].shape[1], LANES):
        rows += swap_chunks([a[:, first : first + LANES] for a in chunked], bits, chunk)
    return jnp.concatenate(rows, axis=0)


def windows(ext, pos, chunk, count):
    per = LANES // chunk
    width = len(ext) - count // per
    out = []
    for i in range(count + 1):
        whole, part = divmod(i, per)
        if part == 0:
            vregs = ext[whole : whole + width]
        else:
            turned = [pltpu.roll(a, LANES - chunk * part, 1) for a in ext[whole : whole + width + 1]]
            vregs = [jnp.where(pos < per - part, turned[v], turned[v + 1]) for v in range(width)]
        out.append(side_by_side(vregs))
    return out


def side_by_side(vregs):
    return vregs[0] if len(vregs) == 1 else jnp.concatenate(vregs, axis=1)


def product_bf16(a, b):
    return (a.astype(F32) * b.astype(F32)).astype(BF16)


def skew_left(products):
    moved = pltpu.roll(products, WIDE - products.shape[0], 1, stride=1, stride_axis=0)
    return jnp.sum(moved, axis=0, keepdims=True)


def shifted_taps(row, first):
    base = jnp.concatenate([row, jnp.zeros((1, WIDE - row.shape[1]), F32)], axis=1)
    base = jnp.broadcast_to(base, (TB, WIDE))
    return pltpu.roll(base, first, 1, stride=1, stride_axis=0).astype(BF16)


def chosen(products, sel_ref):
    return sum(products[kind * TB : (kind + 1) * TB] * sel_ref[kind * TB : (kind + 1) * TB, :] for kind in range(KINDS))


def with_kinds(taps, own, chunk):
    pos = chunk_of((TB, LANES), BF16, chunk)
    zero = jnp.zeros((TB, LANES), BF16)
    further = [jnp.where(pos == kind, pltpu.roll(own, kind * TB, 1), zero) for kind in range(1, KINDS)]
    return jnp.concatenate([taps[:, :LANES], taps[:, LANES:]] + further, axis=0)


def band_of(stored):
    none = jnp.zeros(((KINDS - 1) * TB, LANES), BF16)
    return jnp.concatenate([jnp.concatenate([stored[:TB], none], axis=0), stored[TB:]], axis=1)


def prepare_kernel(chunk, info, q_ref, ct_ref, k_ref, v_ref, taps_ref, x_ref, dy_ref, turned_ref, bx_ref, bdy_ref, gb_ref):
    width = q_ref.shape[1]
    filter_size = taps_ref.shape[1]
    per = LANES // chunk
    for sub in range(width // LANES):
        lanes = pl.ds(sub * LANES, LANES)
        bits = chunk_bits(BF16, chunk)
        x = product_bf16(k_ref[:, lanes], v_ref[:, lanes])
        dy = product_bf16(ct_ref[:, lanes], q_ref[:, lanes])
        gb_ref[:, lanes] = jnp.sum(x.astype(F32) * dy.astype(F32), axis=0, keepdims=True)
        xs, dys = to_groups(x, bits, chunk), to_groups(dy, bits, chunk)
        taps = taps_ref[pl.ds(sub * per, per), :]
        back = jnp.dot(taps.astype(BF16), permutation(filter_size), preferred_element_type=F32)
        for g in range(per):
            at = sub * per + g
            x_ref[at] = side_by_side(xs[g])
            dyg = side_by_side(dys[g])
            dy_ref[at] = dyg
            turned_ref[at] = jnp.dot(permutation(TB), dyg, preferred_element_type=F32).astype(BF16)
            band = shifted_taps(back[g : g + 1], 1)
            bx_ref[at] = with_kinds(band, band[:, LANES:], chunk)
            band = shifted_taps(taps[g : g + 1], 0)
            bdy_ref[at] = with_kinds(band, band[:, :LANES], chunk)


def conv_kernel(chunk, filter_size, info, q_ref, ct_ref, x_ref, turned_ref, taps_ref, bias_ref, rim_ref, mask_ref,
                turned_mask_ref, sel_ref, order_ref, turned_order_ref, *rest):
    out_ref, gq_ref, gf_ref, conv_s, grad_s = rest[-5:]
    width = q_ref.shape[1]
    per = LANES // chunk
    steps = filter_size // TB
    depth = (steps + KINDS) * TB

    def one(sub, slot, further):
        lanes = pl.ds(pl.multiple_of(sub * LANES, LANES), LANES)
        bits, bits32 = chunk_bits(BF16, chunk), chunk_bits(F32, chunk)
        pos = chunk_of((TB, LANES), BF16, chunk)
        kind = KINDS - 1 - iota((KINDS * TB, WIDE), 0) // TB
        col = iota((KINDS * TB, WIDE), 1) - (kind + 1) * TB
        band = (col < filter_size) & ((kind == 0) | (col >= filter_size - TB))
        rims = to_groups(rim_ref[:, lanes], bits, chunk)
        for g in range(per):
            at = sub * per + g
            xg = x_ref[at]
            ext = rims[g] + [xg[:, i : i + LANES] for i in range(0, xg.shape[1], LANES)]
            window = windows(ext, pos, chunk, steps) + [xg] * (KINDS - 1)
            window = jnp.concatenate(window, axis=0) * mask_ref[...]
            y = jnp.dot(band_of(taps_ref[at])[:, :depth], window, preferred_element_type=F32)
            conv_s[slot, g] = chosen(y, sel_ref) + bias_ref[pl.ds(at, 1), :] * xg.astype(F32)
            turned = jnp.concatenate([turned_ref[at]] * KINDS, axis=0) * turned_mask_ref[...]
            pairs = lax.dot_general(turned, window, (((1,), (1,)), ((), ())), preferred_element_type=F32)
            pairs = jnp.concatenate([pairs, jnp.zeros((KINDS * TB, WIDE - depth), F32)], axis=1)
            grad_s[slot, g : g + 1, :] = skew_left(jnp.where(band, pairs, 0.0))

        def more(index, carry):
            level, g = index // per, index % per
            at = sub * per + g
            here = order_ref[...] == level.astype(F32)
            xq = jnp.where(here, x_ref[at].astype(F32), 0.0).astype(BF16)
            turned = turned_order_ref[...] == level.astype(F32)
            turned = jnp.where(turned, turned_ref[at].astype(F32), 0.0).astype(BF16)
            own = taps_ref[at][TB : 2 * TB, :TB]
            conv_s[slot, g] += jnp.where(here, jnp.dot(own, xq, preferred_element_type=F32), 0.0)
            pairs = lax.dot_general(turned, xq, (((1,), (1,)), ((), ())), preferred_element_type=F32)
            pairs = jnp.concatenate(
                [jnp.zeros((TB, filter_size), F32), pairs, jnp.zeros((TB, WIDE - filter_size - TB), F32)], axis=1
            )
            grad_s[slot, pl.ds(g, 1), :] += skew_left(pairs)
            return carry

        if further:
            lax.fori_loop(KINDS * per, info[0] * per, more, 0)
        gf_ref[pl.ds(pl.multiple_of(sub * per, per), per), :] = jnp.dot(
            grad_s[slot, :, :filter_size],
            permutation(filter_size).astype(F32),
            precision=lax.Precision.HIGHEST,
            preferred_element_type=F32,
        )
        filtered = from_groups([conv_s[slot, g] for g in range(per)], bits32, chunk)
        out_ref[:, lanes] = (q_ref[:, lanes].astype(F32) * filtered).astype(BF16)
        gq_ref[:, lanes] = (ct_ref[:, lanes].astype(F32) * filtered).astype(BF16)

    for_all_lanes(one, width // LANES, info)


def back_kernel(chunk, filter_size, info, k_ref, v_ref, dy_ref, taps_ref, bias_ref, rim_ref, mask_ref, sel_ref,
                order_ref, *rest):
    gk_ref, gv_ref, back_s = rest[-3:]
    width = k_ref.shape[1]
    per = LANES // chunk
    steps = filter_size // TB
    depth = (steps + KINDS) * TB

    def one(sub, slot, further):
        lanes = pl.ds(pl.multiple_of(sub * LANES, LANES), LANES)
        bits, bits32 = chunk_bits(BF16, chunk), chunk_bits(F32, chunk)
        pos = chunk_of((TB, LANES), BF16, chunk)
        rims = to_groups(rim_ref[:, lanes], bits, chunk)
        for g in range(per):
            at = sub * per + g
            dyg = dy_ref[at]
            ext = [dyg[:, i : i + LANES] for i in range(0, dyg.shape[1], LANES)] + rims[g]
            window = windows(ext, pos, chunk, steps) + [dyg] * (KINDS - 1)
            window = jnp.concatenate(window, axis=0) * mask_ref[...]
            y = jnp.dot(band_of(taps_ref[at])[:, :depth], window, preferred_element_type=F32)
            back_s[slot, g] = chosen(y, sel_ref) + bias_ref[pl.ds(at, 1), :] * dyg.astype(F32)

        def more(index, carry):
            level, g = index // per, index % per
            at = sub * per + g
            here = order_ref[...] == level.astype(F32)
            dyq = jnp.where(here, dy_ref[at].astype(F32), 0.0).astype(BF16)
            own = taps_ref[at][:TB, :TB]
            back_s[slot, g] += jnp.where(here, jnp.dot(own, dyq, preferred_element_type=F32), 0.0)
            return carry

        if further:
            lax.fori_loop(KINDS * per, info[0] * per, more, 0)
        back = from_groups([back_s[slot, g] for g in range(per)], bits32, chunk)
        gk_ref[:, lanes] = (back * v_ref[:, lanes].astype(F32)).astype(BF16)
        gv_ref[:, lanes] = (back * k_ref[:, lanes].astype(F32)).astype(BF16)

    for_all_lanes(one, width // LANES, info)


def for_all_lanes(one, count, info):
    together = math.gcd(count, TOGETHER)

    def run(further):
        def step(index, carry):
            for slot in range(together):
                one(index * together + slot, slot, further)
            return carry

        lax.fori_loop(0, count // together, step, 0)

    pl.when(info[0] <= KINDS)(lambda: run(False))
    pl.when(info[0] > KINDS)(lambda: run(True))


def call(kernel, name, info, count, ins, outs, scratch=(), previous=None):
    operands = [a for a, _, _ in ins]
    in_specs = [pl.BlockSpec(block, at) for _, block, at in ins]
    aliases = {}
    if previous is not None:
        aliases = {1 + len(operands) + i: i for i in range(len(previous))}
        in_specs += [pl.BlockSpec(memory_space=pl.ANY)] * len(previous)
        operands += list(previous)
    return pl.pallas_call(
        kernel,
        grid_spec=pltpu.PrefetchScalarGridSpec(
            num_scalar_prefetch=1,
            grid=(count,),
            in_specs=in_specs,
            out_specs=[pl.BlockSpec(block, at) for _, _, block, at in outs],
            scratch_shapes=list(scratch),
        ),
        out_shape=[jax.ShapeDtypeStruct(shape, kind) for shape, kind, _, _ in outs],
        input_output_aliases=aliases,
        compiler_params=pltpu.CompilerParams(vmem_limit_bytes=48 * 1024 * 1024),
        cost_estimate=pl.CostEstimate(flops=2**24, bytes_accessed=2**20, transcendentals=0),
        name=name,
    )(info, *operands)


def wide(array, block, first):
    return (array, (array.shape[0], block), lambda i, c: (0, first + i))


def per_group(array, groups, first):
    rest = array.shape[1:]
    return (array, (groups, *rest), lambda i, c: (first + i, *[0] * len(rest)))


def fixed(array):
    return (array, array.shape, lambda i, c: (0, 0))


def prepare(info, big, filters):
    row_count, channels = big[0].shape
    chunk, block = TB, math.gcd(channels, 512)
    groups, total, filter_size = block // chunk, channels // chunk, filters.shape[1]
    taps = (filters, (groups, filter_size), lambda i, c: (c[1] * (channels // block) + i, 0))
    ins = [wide(a, block, 0) for a in big] + [taps]
    shapes = [(TB, row_count)] * 3 + [((1 + KINDS) * TB, LANES)] * 2
    outs = [((total, *s), BF16, (groups, *s), lambda i, c: (i, 0, 0)) for s in shapes]
    outs.append(((1, channels), F32, (1, block), lambda i, c: (0, i)))
    return call(functools.partial(prepare_kernel, chunk), "prepare", info, channels // block, ins, outs)


def run_part(kernel, name, part, info, pair, grouped, rim, rim_first, masks, filter_size, small, previous):
    row_count, channels = pair[0].shape
    chunk, width = TB, channels // PARTS
    block = math.gcd(width, 512)
    groups, first = block // chunk, part * (width // block)
    per = LANES // chunk
    ins = [wide(a, block, first) for a in pair] + [per_group(a, groups, first) for a in grouped]
    ins += [wide(rim, block, rim_first * (width // block))] + [fixed(a) for a in masks]
    outs = [((row_count, channels), BF16, (row_count, block), lambda i, c: (0, first + i))] * 2
    scratch = [pltpu.VMEM((TOGETHER, per, TB, row_count), F32)]
    if small:
        outs += [((channels // chunk, filter_size), F32, (groups, filter_size), lambda i, c: (first + i, 0))]
        scratch += [pltpu.VMEM((TOGETHER, per, WIDE), F32)]
    kernel = functools.partial(kernel, chunk, filter_size)
    return call(kernel, name, info, width // block, ins, outs, scratch, previous)


def reset_kernel(steps, near_ref, mask_x, turned_x, sel_x, order_x, turned_order_x, mask_dy, sel_dy, order_dy, kinds):
    total = near_ref.shape[1]
    rows = total - steps * TB
    near = jnp.clip(near_ref[...], -1024, 1024).astype(F32)
    lane, row = iota((TB, total), 1), iota((TB, total), 0)
    spread = jnp.where(lane % TB == row, jnp.broadcast_to(near, (TB, total)), 0.0)
    same = flag(iota((total, total), 0) // TB == iota((total, total), 1) // TB, F32)
    begin = jnp.dot(spread, same, precision=lax.Precision.HIGHEST, preferred_element_type=F32)
    begin = jnp.floor(begin + 0.5)
    own = begin[:, :rows]
    block = iota((TB, rows), 1) // TB * TB
    pos = (block + iota((TB, rows), 0)).astype(F32)
    marks = flag((own == pos) & (iota((TB, rows), 0) > 0))
    before = flag(iota((TB, TB), 0) >= iota((TB, TB), 1))
    order = jnp.dot(before, marks, preferred_element_type=F32)
    behind = order[TB - 1 :] - order
    first = jnp.broadcast_to(own[:1], (TB, rows))
    for i in range(steps):
        mask_x[i * TB : (i + 1) * TB, :] = flag(pos - TB * (steps - i) >= first)
        later = pltpu.roll(begin, total - (i + 1) * TB, 1)[:, :rows]
        mask_dy[(i + 1) * TB : (i + 2) * TB, :] = flag(later <= (block + TB - 1).astype(F32))
    turn = permutation(TB)
    for kind in range(KINDS):
        at = steps + kind
        mask_x[at * TB : (at + 1) * TB, :] = flag(order == kind)
        sel_x[kind * TB : (kind + 1) * TB, :] = flag(order == kind, F32)
        at = KINDS - 1 - kind
        turned = jnp.dot(turn, flag(order == kind), preferred_element_type=F32)
        turned_x[at * TB : (at + 1) * TB, :] = turned.astype(BF16)
        at = steps + kind if kind else 0
        mask_dy[at * TB : (at + 1) * TB, :] = flag(behind == kind)
        sel_dy[kind * TB : (kind + 1) * TB, :] = flag(behind == kind, F32)
    order_x[...], order_dy[...] = order, behind
    turned_order_x[...] = jnp.dot(turn, order.astype(BF16), preferred_element_type=F32)
    kinds[0] = 1 + jnp.max(order).astype(jnp.int32)


def reset_masks(near, row_count, steps):
    depth, high = (steps + KINDS) * TB, KINDS * TB
    shapes = [(depth, BF16), (high, BF16), (high, F32), (TB, F32), (TB, F32), (depth, BF16), (high, F32), (TB, F32)]
    out = pl.pallas_call(
        functools.partial(reset_kernel, steps),
        out_shape=[jax.ShapeDtypeStruct((rows, row_count), kind) for rows, kind in shapes]
        + [jax.ShapeDtypeStruct((1,), jnp.int32)],
        out_specs=[pl.BlockSpec(memory_space=pltpu.VMEM)] * len(shapes) + [pl.BlockSpec(memory_space=pltpu.SMEM)],
        compiler_params=pltpu.CompilerParams(vmem_limit_bytes=32 * 1024 * 1024),
        name="resets",
    )(near)
    return out[:5], out[5:8], out[8]


def passed_along(value, axis, steps):
    count = lax.axis_size(axis)
    initial, last = (max(0, -steps), min(count, count - steps))
    return lax.ppermute(value, axis, [(source, source + steps) for source in range(initial, last)])


def sum_over(value, axis):
    count = lax.axis_size(axis)
    if count & (count - 1):
        return lax.psum(value, axis)
    step = 1
    while step < count:
        value = value + lax.ppermute(value, axis, [(i, i ^ step) for i in range(count)])
        step *= 2
    return value


def rows_of_all(value, axis):
    count = lax.axis_size(axis)
    if count != 2:
        return lax.all_gather(value, axis, axis=0, tiled=True)
    other = lax.ppermute(value, axis, [(0, 1), (1, 0)])
    is_first = lax.axis_index(axis) == 0
    return jnp.concatenate([jnp.where(is_first, value, other), jnp.where(is_first, other, value)], axis=0)


def body(queries, key_branch, value_branch, cotangent, filters, skip_bias, contig_start):
    row_count, channels = queries.shape
    group_total, filter_size = filters.shape
    ctx_count, tp_count = lax.axis_size("ctx"), lax.axis_size("tp")
    shard, tensor = lax.axis_index("ctx"), lax.axis_index("tp")
    token_count = row_count * ctx_count
    chunk = channels * tp_count // group_total
    groups = channels // chunk
    width = channels // PARTS

    tail = lambda m: m[row_count - filter_size :]
    left = passed_along(product_bf16(tail(key_branch), tail(value_branch)), "ctx", 1)

    starts = jnp.concatenate([contig_start, jnp.full((filter_size,), 2**30, jnp.int32)])
    first = shard * row_count
    near = (lax.dynamic_slice_in_dim(starts, first, row_count + filter_size, 0) - first)[None, :]
    masks_x, masks_dy, kinds = reset_masks(near, row_count, filter_size // TB)
    info = jnp.concatenate([kinds, tensor.astype(jnp.int32).reshape(1)])
    bias = jnp.tile(skip_bias.reshape(groups, chunk), (1, row_count // TB))
    big = (queries, cotangent, key_branch, value_branch)
    x, dy, turned, band_x, band_dy, bias_part = prepare(info, big, filters)

    right = []
    for part in range(PARTS):
        cut = lambda m: lax.slice(m, (0, part * width), (filter_size, (part + 1) * width))
        sent = product_bf16(cut(cotangent), cut(queries))
        if part:
            sent, right[-1] = lax.optimization_barrier((sent, right[-1]))
        else:
            sent, bias_part = lax.optimization_barrier((sent, bias_part))
        right.append(passed_along(sent, "ctx", -1))

    done, rim = None, left
    for part in range(PARTS):
        grouped = (x, turned, band_x, bias)
        done = run_part(
            conv_kernel, "conv", part, info, (queries, cotangent), grouped, rim, part, masks_x, filter_size, True, done
        )
    output, grad_query, filter_part = done
    done = None
    for part in range(PARTS):
        grouped = (dy, band_dy, bias)
        pair = (key_branch, value_branch)
        done = run_part(
            back_kernel, "back", part, info, pair, grouped, right[part], 0, masks_dy, filter_size, False, done
        )
    grad_key, grad_value = done

    terms = jnp.concatenate([filter_part, bias_part.reshape(channels // filter_size, filter_size)], axis=0)
    terms = sum_over(terms, "ctx")
    grad_filter = rows_of_all(terms[:groups], "tp") * (1.0 / math.sqrt(token_count * chunk))
    grad_bias = terms[groups:].reshape(channels) * (1.0 / math.sqrt(token_count))
    return (output, grad_query, grad_key, grad_value, grad_filter, grad_bias)


def solution(mesh):
    whole = P("ctx", "tp")
    return jax.shard_map(
        body,
        mesh=mesh,
        in_specs=(whole, whole, whole, whole, P(), P("tp"), P()),
        out_specs=(whole, whole, whole, whole, P(), P("tp")),
        check_vma=False,
    )
```

time: 149 us -> 136 us (0.913)
  the two profiles are of different devices: /device:TPU:0 before, /device:TPU:11 now
where the time goes in v4:
time: 136 us; the launch traced here: 135 us
  Pallas kernels  76.2 us (56%)
  waiting for transfers between devices  22.8 us (17%)
  local copies, waits for them, and re-layouts  14.8 us (11%)
  starting transfers between devices  13.9 us (10%)
  other arithmetic  6.64 us (5%)
    pallas_call x5, Pallas kernels, call(): pl.pallas_call(kernel, grid_spec=pltpu.PrefetchScalarGridSpec(num_scalar_...  75 us
    ppermute x4, waiting for transfers between devices, sum_over(): lax.ppermute(value, axis, [(i, i ^ step) for i in range(count)])  22.5 us
    unnamed x50, local copies, waits for them, and re-layouts  12.8 us
    ppermute x3, starting transfers between devices, passed_along(): lax.ppermute(value, axis, [(source, source + steps) for source in range(i...  7.37 us
    ppermute x4, starting transfers between devices, sum_over(): lax.ppermute(value, axis, [(i, i ^ step) for i in range(count)])  4.88 us
    convert_element_type x2, other arithmetic, product_bf16(): return (a.astype(F32) * b.astype(F32)).astype(BF16)  4.42 us
  transfers between devices with their start and end apart: 8, of which 4 were waited for; matrix products, arithmetic and copies ran while one was open for 4% of the time, Pallas kernels for 56%

profile of v4, /device:TPU:11, one launch (start us, length us, event | category | flops | bytes accessed | tf_op | source)
XLA Modules:
  0.0 135.2 jit_solution(15946971632221185222)
XLA Ops:
  0.7 2.8 %multiply_convert_fusion = bf16[128,4096]{1,0:T(8,128)(2,1)} fusion(bf16[256,4096]{1,0:T(8,128)(2,1)} %v_ref.5, bf16[256,4096]{1,0:T(8,128)(2,1)} %k_ref.5), kind=kLoop, calls=%fused_computation | loop fusion | flops 2097152 | bytes 3145728 | tf_op jit(solution)/shard_map/convert_element_type | solution.py:87
  3.5 3.1 %collective-permute-start = (bf16[128,4096]{1,0:T(8,128)(2,1)}, bf16[128,4096]{1,0:T(8,128)(2,1)S(1)}, u32[]{:S(2)}, u32[]{:S(2)}) collective-permute-start(bf16[128,4096]{1,0:T(8,128)(2,1)} %multiply_convert_fusion), channel_id=1, source_target_pairs={{0,2},{2,4},{4,6},{6,8},{8,10},{10,12},{12,14},{14,16},{16,18},{18... | collective-permute-start | bytes 3145736 | tf_op jit(solution)/shard_map/ppermute | solution.py:378
  6.7 1.1 resets.1
  12.2 18.8 %prepare.1 = (bf16[256,16,256]{2,1,0:T(8,128)(2,1)S(1)}, bf16[256,16,256]{2,1,0:T(8,128)(2,1)S(1)}, bf16[256,16,256]{2,1,0:T(8,128)(2,1)}, bf16[256,64,128]{2,1,...) custom-call(s32[2]{0:T(128)S(1)} %pad_add_fusion.info, bf16[256,4096]{1,0:T(8,128)(2,1)} %q_ref.5, ...), custom_call_target="tpu_custom_call" | custom-call | flops 16777216 | bytes 1048576 | tf_op jit(solution)/shard_map/prepare/pallas_call | solution.py:265
  31.0 1.3 copy-done.7
  32.4 1.6 %multiply_convert_fusion.1 = (bf16[128,2048]{1,0:T(8,128)(2,1)}, bf16[128,2048]{1,0:T(8,128)(2,1)}) fusion(bf16[256,4096]{1,0:T(8,128)(2,1)S(1)} %copy-done.2, bf16[256,4096]{1,0:T(8,128)(2,1)S(1)} %copy-done.4), kind=kLoop, calls=%fused_computation.1 | loop fusion | flops 2097152 | bytes 3145728 | tf_op jit(solution)/shard_map/convert_element_type | solution.py:87
  34.0 2.2 %collective-permute-start.1 = (bf16[128,2048]{1,0:T(8,128)(2,1)}, bf16[128,2048]{1,0:T(8,128)(2,1)}, u32[]{:S(2)}, u32[]{:S(2)}) collective-permute-start(bf16[128,2048]{1,0:T(8,128)(2,1)} %get-tuple-element.52), channel_id=1, source_target_pairs={{2,0},{4,2},{6,4},{8,6},{10,8},{12,10},{14,12},{16,14},{18,16},{20... | collective-permute-start | bytes 1572872 | tf_op jit(solution)/shard_map/ppermute | solution.py:378
  36.3 0.7 tile.11
  37.1 1.1 copy.20.bias_ref
  38.2 1.6 %copy-done.5 = bf16[256,4096]{1,0:T(8,128)(2,1)S(1)} copy-done((bf16[256,4096]{1,0:T(8,128)(2,1)S(1)}, bf16[256,4096]{1,0:T(8,128)(2,1)}, u32[]{:S(2)}) %copy-start.5) | copy-done | bytes 2097176
  39.8 0.9 copy-done.9
  40.7 0.8 copy-done.12
  43.6 18.2 %conv.2 = (bf16[256,4096]{1,0:T(8,128)(2,1)}, bf16[256,4096]{1,0:T(8,128)(2,1)}, f32[256,128]{1,0:T(8,128)S(1)}) custom-call(s32[2]{0:T(128)S(1)} %pad_add_fusion.info, bf16[256,4096]{1,0:T(8,128)(2,1)S(1)} %copy-done.2, bf16[256,4096]{1,0:T(8,128)(2,1)S(1)} %copy-done.5, bf16[256,16,256]{2,1,0:T(8,128)(2,1)} %copy-done.7, ...), custom_call_target="tpu_custom_call" | custom-call | flops 16777216 | bytes 1048576 | tf_op jit(solution)/shard_map/conv/pallas_call | solution.py:265
  61.9 18.3 %conv.3 = (bf16[256,4096]{1,0:T(8,128)(2,1)}, bf16[256,4096]{1,0:T(8,128)(2,1)}, f32[256,128]{1,0:T(8,128)S(1)}) custom-call(s32[2]{0:T(128)S(1)} %pad_add_fusion.info, bf16[256,4096]{1,0:T(8,128)(2,1)S(1)} %copy-done.3, bf16[256,4096]{1,0:T(8,128)(2,1)S(1)} %copy-done.5, ...), custom_call_target="tpu_custom_call", output_to_operand_aliasing={{0}: (13, {}), {1}: (14, {}), {2}: (15, {})} | custom-call | flops 16777216 | bytes 1048576 | tf_op jit(solution)/shard_map/conv/pallas_call | solution.py:265
  80.2 2.1 %collective-permute-start.3 = (f32[288,128]{1,0:T(8,128)S(1)}, f32[288,128]{1,0:T(8,128)S(1)}, u32[]{:S(2)}, u32[]{:S(2)}) collective-permute-start(f32[288,128]{1,0:T(8,128)S(1)} %pad_maximum_fusion), channel_id=1, source_target_pairs={{0,2},{2,0},{4,6},{6,4},{8,10},{10,8},{12,14},{14,12},{16,18},{18,... | collective-permute-start | bytes 442376 | tf_op jit(solution)/shard_map/ppermute | solution.py:387
  82.3 2.1 %collective-permute-start.2 = (bf16[128,2048]{1,0:T(8,128)(2,1)}, bf16[128,2048]{1,0:T(8,128)(2,1)S(1)}, u32[]{:S(2)}, u32[]{:S(2)}) collective-permute-start(bf16[128,2048]{1,0:T(8,128)(2,1)} %get-tuple-element.53), channel_id=1, source_target_pairs={{2,0},{4,2},{6,4},{8,6},{10,8},{12,10},{14,12},{16,14},{18,16},{20... | collective-permute-start | bytes 1572872 | tf_op jit(solution)/shard_map/ppermute | solution.py:378
  84.4 0.8 collective-permute-done.3
  85.6 16.7 %collective-permute-done.4 = f32[288,128]{1,0:T(8,128)S(1)} collective-permute-done((f32[288,128]{1,0:T(8,128)S(1)}, f32[288,128]{1,0:T(8,128)S(1)}, u32[]{:S(2)}, u32[]{:S(2)}) %collective-permute-start.4) | collective-permute-done | bytes 147488 | tf_op jit(solution)/shard_map/ppermute | solution.py:387
  102.4 4.9 %collective-permute-done.5 = f32[288,128]{1,0:T(8,128)S(1)} collective-permute-done((f32[288,128]{1,0:T(8,128)S(1)}, f32[288,128]{1,0:T(8,128)S(1)}, u32[]{:S(2)}, u32[]{:S(2)}) %collective-permute-start.5) | collective-permute-done | bytes 147488 | tf_op jit(solution)/shard_map/ppermute | solution.py:387
  107.3 2.4 %collective-permute-start.6 = (f32[288,128]{1,0:T(8,128)S(1)}, f32[288,128]{1,0:T(8,128)S(1)}, u32[]{:S(2)}, u32[]{:S(2)}) collective-permute-start(f32[288,128]{1,0:T(8,128)S(1)} %add.20), channel_id=1, source_target_pairs={{0,16},{2,18},{4,20},{6,22},{8,24},{10,26},{12,28},{14,30},{16,0},... | collective-permute-start | bytes 442376 | tf_op jit(solution)/shard_map/ppermute | solution.py:387
  109.7 1.6 %copy-done.1 = bf16[256,4096]{1,0:T(8,128)(2,1)S(1)} copy-done((bf16[256,4096]{1,0:T(8,128)(2,1)S(1)}, bf16[256,4096]{1,0:T(8,128)(2,1)}, u32[]{:S(2)}) %copy-start.1) | copy-done | bytes 2097176
  112.0 9.8 %back.2 = (bf16[256,4096]{1,0:T(8,128)(2,1)}, bf16[256,4096]{1,0:T(8,128)(2,1)}) custom-call(s32[2]{0:T(128)S(1)} %pad_add_fusion.info, bf16[256,4096]{1,0:T(8,128)(2,1)S(1)} %copy-done, bf16[256,4096]{1,0:T(8,128)(2,1)S(1)} %copy-done.1, bf16[256,16,256]{2,1,0:T(8,128)(2,1)} %copy-done.6, bf16[256,64,128]{2,1,0:T(8,128)(2,1)} %get-tuple-element.50.taps_ref, ...), custom_call_target="tpu_custom_call" | custom-call | flops 16777216 | bytes 1048576 | tf_op jit(solution)/shard_map/back/pallas_call | solution.py:265
  121.9 9.9 %back.3 = (bf16[256,4096]{1,0:T(8,128)(2,1)}, bf16[256,4096]{1,0:T(8,128)(2,1)}) custom-call(s32[2]{0:T(128)S(1)} %pad_add_fusion.info, bf16[256,4096]{1,0:T(8,128)(2,1)S(1)} %copy-done, bf16[256,4096]{1,0:T(8,128)(2,1)S(1)} %copy-done.1, bf16[256,16,256]{2,1,0:T(8,128)(2,1)} %copy-done.6, ...), custom_call_target="tpu_custom_call", output_to_operand_aliasing={{0}: (10, {}), {1}: (11, {})} | custom-call | flops 16777216 | bytes 1048576 | tf_op jit(solution)/shard_map/back/pallas_call | solution.py:265
  131.8 1.7 %collective-permute-start.7 = (f32[256,128]{1,0:T(8,128)S(1)}, f32[256,128]{1,0:T(8,128)S(1)}, u32[]{:S(2)}, u32[]{:S(2)}) collective-permute-start(f32[256,128]{1,0:T(8,128)S(1)} %slice.32), channel_id=1, source_target_pairs={{0,1},{1,0},{2,3},{3,2},{4,5},{5,4},{6,7},{7,6},{8,9},{9,8},{10,11... | collective-permute-start | bytes 393224 | tf_op jit(solution)/shard_map/ppermute | solution.py:396
  (66 shorter events, 9.8 us)
Async XLA Ops:
  0.6 6.0 %copy-start.24 = (s32[4096]{0:T(1024)S(1)}, s32[4096]{0:T(1024)}, u32[]{:S(2)}) copy-start(s32[4096]{0:T(1024)} %param.13) | copy-start | bytes 49156
  0.6 11.6 %copy-start.10 = (f32[512,128]{1,0:T(8,128)S(1)}, f32[512,128]{1,0:T(8,128)}, u32[]{:S(2)}) copy-start(f32[512,128]{1,0:T(8,128)} %taps_ref.1) | copy-start | bytes 786436
  3.5 34.7 %collective-permute-start = (bf16[128,4096]{1,0:T(8,128)(2,1)}, bf16[128,4096]{1,0:T(8,128)(2,1)S(1)}, u32[]{:S(2)}, u32[]{:S(2)}) collective-permute-start(bf16[128,4096]{1,0:T(8,128)(2,1)} %multiply_convert_fusion), channel_id=1, source_target_pairs={{0,2},{2,4},{4,6},{6,8},{8,10},{10,12},{12,14},{14,16},{16,18},{18... | collective-permute-start | bytes 3145736 | tf_op jit(solution)/shard_map/ppermute | solution.py:378
  12.2 20.1 %copy-start.2 = (bf16[256,4096]{1,0:T(8,128)(2,1)S(1)}, bf16[256,4096]{1,0:T(8,128)(2,1)}, u32[]{:S(2)}) copy-start(bf16[256,4096]{1,0:T(8,128)(2,1)} %q_ref.5) | copy-start | bytes 6291460
  12.2 20.1 %copy-start.4 = (bf16[256,4096]{1,0:T(8,128)(2,1)S(1)}, bf16[256,4096]{1,0:T(8,128)(2,1)}, u32[]{:S(2)}) copy-start(bf16[256,4096]{1,0:T(8,128)(2,1)} %ct_ref.5) | copy-start | bytes 6291460
  31.0 1.3 copy-start.7
  32.4 1.6 %copy-start.6 = (bf16[256,16,256]{2,1,0:T(8,128)(2,1)}, bf16[256,16,256]{2,1,0:T(8,128)(2,1)S(1)}, u32[]{:S(2)}) copy-start(bf16[256,16,256]{2,1,0:T(8,128)(2,1)S(1)} %get-tuple-element.49.dy_ref) | copy-start | bytes 6291460
  32.4 1.6 %copy-start.17 = (f32[1,4096]{1,0:T(1,128)}, f32[1,4096]{1,0:T(1,128)S(1)}, u32[]{:S(2)}) copy-start(f32[1,4096]{1,0:T(1,128)S(1)} %get-tuple-element.63) | copy-start | bytes 49156
  32.4 3.8 %copy-start.23 = (f32[4096]{0:T(1024)S(1)}, f32[4096]{0:T(1024)}, u32[]{:S(2)}) copy-start(f32[4096]{0:T(1024)} %param.12) | copy-start | bytes 49156
  34.0 48.3 %collective-permute-start.1 = (bf16[128,2048]{1,0:T(8,128)(2,1)}, bf16[128,2048]{1,0:T(8,128)(2,1)}, u32[]{:S(2)}, u32[]{:S(2)}) collective-permute-start(bf16[128,2048]{1,0:T(8,128)(2,1)} %get-tuple-element.52), channel_id=1, source_target_pairs={{2,0},{4,2},{6,4},{8,6},{10,8},{12,10},{14,12},{16,14},{18,16},{20... | collective-permute-start | bytes 1572872 | tf_op jit(solution)/shard_map/ppermute | solution.py:378
  38.2 1.6 %copy-start.5 = (bf16[256,4096]{1,0:T(8,128)(2,1)S(1)}, bf16[256,4096]{1,0:T(8,128)(2,1)}, u32[]{:S(2)}) copy-start(bf16[256,4096]{1,0:T(8,128)(2,1)} %ct_ref.5) | copy-start | bytes 6291460
  39.8 0.9 copy-start.9
  40.7 0.8 copy-start.12
  41.5 0.7 copy-start.14
  43.6 18.2 %copy-start.3 = (bf16[256,4096]{1,0:T(8,128)(2,1)S(1)}, bf16[256,4096]{1,0:T(8,128)(2,1)}, u32[]{:S(2)}) copy-start(bf16[256,4096]{1,0:T(8,128)(2,1)} %q_ref.5) | copy-start | bytes 6291460
  61.9 18.3 %copy-start.18 = (f32[1,4096]{1,0:T(1,128)S(1)}, f32[1,4096]{1,0:T(1,128)}, u32[]{:S(2)}) copy-start(f32[1,4096]{1,0:T(1,128)} %copy-done.17) | copy-start | bytes 49156
  61.9 47.8 %copy-start = (bf16[256,4096]{1,0:T(8,128)(2,1)S(1)}, bf16[256,4096]{1,0:T(8,128)(2,1)}, u32[]{:S(2)}) copy-start(bf16[256,4096]{1,0:T(8,128)(2,1)} %k_ref.5) | copy-start | bytes 6291460
  80.2 5.0 %collective-permute-start.3 = (f32[288,128]{1,0:T(8,128)S(1)}, f32[288,128]{1,0:T(8,128)S(1)}, u32[]{:S(2)}, u32[]{:S(2)}) collective-permute-start(f32[288,128]{1,0:T(8,128)S(1)} %pad_maximum_fusion), channel_id=1, source_target_pairs={{0,2},{2,0},{4,6},{6,4},{8,10},{10,8},{12,14},{14,12},{16,18},{18,... | collective-permute-start | bytes 442376 | tf_op jit(solution)/shard_map/ppermute | solution.py:387
  82.3 39.6 %collective-permute-start.2 = (bf16[128,2048]{1,0:T(8,128)(2,1)}, bf16[128,2048]{1,0:T(8,128)(2,1)S(1)}, u32[]{:S(2)}, u32[]{:S(2)}) collective-permute-start(bf16[128,2048]{1,0:T(8,128)(2,1)} %get-tuple-element.53), channel_id=1, source_target_pairs={{2,0},{4,2},{6,4},{8,6},{10,8},{12,10},{14,12},{16,14},{18,16},{20... | collective-permute-start | bytes 1572872 | tf_op jit(solution)/shard_map/ppermute | solution.py:378
  85.2 17.0 %collective-permute-start.4 = (f32[288,128]{1,0:T(8,128)S(1)}, f32[288,128]{1,0:T(8,128)S(1)}, u32[]{:S(2)}, u32[]{:S(2)}) collective-permute-start(f32[288,128]{1,0:T(8,128)S(1)} %fusion.2), channel_id=1, source_target_pairs={{0,4},{2,6},{4,0},{6,2},{8,12},{10,14},{12,8},{14,10},{16,20},{18,... | collective-permute-start | bytes 442376 | tf_op jit(solution)/shard_map/ppermute | solution.py:387
  102.3 5.0 %collective-permute-start.5 = (f32[288,128]{1,0:T(8,128)S(1)}, f32[288,128]{1,0:T(8,128)S(1)}, u32[]{:S(2)}, u32[]{:S(2)}) collective-permute-start(f32[288,128]{1,0:T(8,128)S(1)} %add.19), channel_id=1, source_target_pairs={{0,8},{2,10},{4,12},{6,14},{8,0},{10,2},{12,4},{14,6},{16,24},{18,... | collective-permute-start | bytes 442376 | tf_op jit(solution)/shard_map/ppermute | solution.py:387
  107.3 24.4 %collective-permute-start.6 = (f32[288,128]{1,0:T(8,128)S(1)}, f32[288,128]{1,0:T(8,128)S(1)}, u32[]{:S(2)}, u32[]{:S(2)}) collective-permute-start(f32[288,128]{1,0:T(8,128)S(1)} %add.20), channel_id=1, source_target_pairs={{0,16},{2,18},{4,20},{6,22},{8,24},{10,26},{12,28},{14,30},{16,0},... | collective-permute-start | bytes 442376 | tf_op jit(solution)/shard_map/ppermute | solution.py:387
  109.7 1.6 %copy-start.1 = (bf16[256,4096]{1,0:T(8,128)(2,1)S(1)}, bf16[256,4096]{1,0:T(8,128)(2,1)}, u32[]{:S(2)}) copy-start(bf16[256,4096]{1,0:T(8,128)(2,1)} %v_ref.5) | copy-start | bytes 6291460
  131.8 2.7 %collective-permute-start.7 = (f32[256,128]{1,0:T(8,128)S(1)}, f32[256,128]{1,0:T(8,128)S(1)}, u32[]{:S(2)}, u32[]{:S(2)}) collective-permute-start(f32[256,128]{1,0:T(8,128)S(1)} %slice.32), channel_id=1, source_target_pairs={{0,1},{1,0},{2,3},{3,2},{4,5},{5,4},{6,7},{7,6},{8,9},{9,8},{10,11... | collective-permute-start | bytes 393224 | tf_op jit(solution)/shard_map/ppermute | solution.py:396
  (9 other events, 5.8 us)

commit v5 on v4

--- a/solution.py
+++ b/solution.py
@@ -14,6 +14,7 @@
 WIDE = 256
 KINDS = 3
 PARTS = 2
+VMEM_BYTES = 60 * 1024 * 1024
 TOGETHER = 2
 
 
@@ -33,14 +34,13 @@
     return (iota(shape, 1) // chunk).astype(F32).astype(kind)
 
 
-def swap_chunks(arrays, bits, chunk):
+def swap_chunks(arrays, bits):
     count = len(arrays)
-    turned = [pltpu.roll(a, n * chunk, 1) if n else a for n, a in enumerate(arrays)]
-    rows = [turned[(-i) % count] for i in range(count)]
+    rows = [arrays[(-i) % count] for i in range(count)]
     for power, moved in enumerate(bits):
         bit = 1 << power
         rows = [jnp.where(moved, rows[(i - bit) % count], rows[i]) for i in range(count)]
-    return [pltpu.roll(a, LANES - n * chunk, 1) if n else a for n, a in enumerate(rows)]
+    return rows
 
 
 def chunk_bits(kind, chunk):
@@ -53,28 +53,53 @@
     sets = []
     for first in range(0, block.shape[0], TB * per):
         parts = [block[first + TB * n : first + TB * (n + 1)] for n in range(per)]
-        sets.append(swap_chunks(parts, bits, chunk))
+        sets.append(swap_chunks([pltpu.roll(a, n * chunk, 1) if n else a for n, a in enumerate(parts)], bits))
     return [[s[g] for s in sets] for g in range(per)]
 
 
 def from_groups(chunked, bits, chunk):
     rows = []
     for first in range(0, chunked[0].shape[1], LANES):
-        rows += swap_chunks([a[:, first : first + LANES] for a in chunked], bits, chunk)
+        parts = swap_chunks([a[:, first : first + LANES] for a in chunked], bits)
+        rows += [pltpu.roll(a, LANES - n * chunk, 1) if n else a for n, a in enumerate(parts)]
     return jnp.concatenate(rows, axis=0)
 
 
-def windows(ext, pos, chunk, count):
+def place_of(g, chunk):
+    per = LANES // chunk
+    return ((iota((TB, LANES), 1) // chunk + per - g) % per).astype(F32).astype(BF16)
+
+
+def past_windows(ext, place, chunk, count):
+    per = LANES // chunk
+    out = []
+    for back in range(count, -1, -1):
+        whole, part = divmod(back, per)
+        width = len(ext) - count // per
+        vregs = []
+        for v in range(width):
+            near = len(ext) - width + v - whole
+            if part:
+                vregs.append(pltpu.roll(jnp.where(place < per - part, ext[near], ext[near - 1]), part * chunk, 1))
+            else:
+                vregs.append(ext[near])
+        out.append(side_by_side(vregs))
+    return out
+
+
+def next_windows(ext, place, chunk, count):
     per = LANES // chunk
     width = len(ext) - count // per
     out = []
-    for i in range(count + 1):
-        whole, part = divmod(i, per)
-        if part == 0:
-            vregs = ext[whole : whole + width]
-        else:
-            turned = [pltpu.roll(a, LANES - chunk * part, 1) for a in ext[whole : whole + width + 1]]
-            vregs = [jnp.where(pos < per - part, turned[v], turned[v + 1]) for v in range(width)]
+    for ahead in range(count + 1):
+        whole, part = divmod(ahead, per)
+        vregs = []
+        for v in range(width):
+            near = v + whole
+            if part:
+                vregs.append(pltpu.roll(jnp.where(place >= part, ext[near], ext[near + 1]), LANES - part * chunk, 1))
+            else:
+                vregs.append(ext[near])
         out.append(side_by_side(vregs))
     return out
 
@@ -88,8 +113,16 @@
 
 
 def skew_left(products):
-    moved = pltpu.roll(products, WIDE - products.shape[0], 1, stride=1, stride_axis=0)
-    return jnp.sum(moved, axis=0, keepdims=True)
+    moved = pltpu.roll(products, LANES - TB, 1, stride=1, stride_axis=0)
+    return moved[: TB // 2] + moved[TB // 2 :]
+
+
+def exact_dot(a, b):
+    return jnp.dot(a, b, precision=lax.Precision.HIGHEST, preferred_element_type=F32)
+
+
+def group_rows(count, size):
+    return flag(iota((count, count * size), 1) // size == iota((count, count * size), 0), F32)
 
 
 def shifted_taps(row, first):
@@ -98,8 +131,10 @@
     return pltpu.roll(base, first, 1, stride=1, stride_axis=0).astype(BF16)
 
 
-def chosen(products, sel_ref):
-    return sum(products[kind * TB : (kind + 1) * TB] * sel_ref[kind * TB : (kind + 1) * TB, :] for kind in range(KINDS))
+def chosen(products, sel_ref, g):
+    return sum(
+        products[kind * TB : (kind + 1) * TB] * sel_ref[g, kind * TB : (kind + 1) * TB, :] for kind in range(KINDS)
+    )
 
 
 def with_kinds(taps, own, chunk):
@@ -114,7 +149,7 @@
     return jnp.concatenate([jnp.concatenate([stored[:TB], none], axis=0), stored[TB:]], axis=1)
 
 
-def prepare_kernel(chunk, info, q_ref, ct_ref, k_ref, v_ref, taps_ref, x_ref, dy_ref, turned_ref, bx_ref, bdy_ref, gb_ref):
+def prepare_kernel(chunk, info, q_ref, ct_ref, k_ref, v_ref, taps_ref, x_ref, dy_ref, turned_ref, bx_ref, bdy_ref, gb_ref, head_ref):
     width = q_ref.shape[1]
     filter_size = taps_ref.shape[1]
     per = LANES // chunk
@@ -124,6 +159,7 @@
         x = product_bf16(k_ref[:, lanes], v_ref[:, lanes])
         dy = product_bf16(ct_ref[:, lanes], q_ref[:, lanes])
         gb_ref[:, lanes] = jnp.sum(x.astype(F32) * dy.astype(F32), axis=0, keepdims=True)
+        head_ref[:, lanes] = dy[:filter_size]
         xs, dys = to_groups(x, bits, chunk), to_groups(dy, bits, chunk)
         taps = taps_ref[pl.ds(sub * per, per), :]
         back = jnp.dot(taps.astype(BF16), permutation(filter_size), preferred_element_type=F32)
@@ -150,48 +186,53 @@
     def one(sub, slot, further):
         lanes = pl.ds(pl.multiple_of(sub * LANES, LANES), LANES)
         bits, bits32 = chunk_bits(BF16, chunk), chunk_bits(F32, chunk)
-        pos = chunk_of((TB, LANES), BF16, chunk)
-        kind = KINDS - 1 - iota((KINDS * TB, WIDE), 0) // TB
-        col = iota((KINDS * TB, WIDE), 1) - (kind + 1) * TB
-        band = (col < filter_size) & ((kind == 0) | (col >= filter_size - TB))
+        late, lane = TB - 1 - iota((TB, LANES), 0), iota((TB, LANES), 1)
+        causal = lane % TB <= late
         rims = to_groups(rim_ref[:, lanes], bits, chunk)
         for g in range(per):
             at = sub * per + g
             xg = x_ref[at]
             ext = rims[g] + [xg[:, i : i + LANES] for i in range(0, xg.shape[1], LANES)]
-            window = windows(ext, pos, chunk, steps) + [xg] * (KINDS - 1)
-            window = jnp.concatenate(window, axis=0) * mask_ref[...]
+            window = past_windows(ext, place_of(g, chunk), chunk, steps) + [xg] * (KINDS - 1)
+            window = jnp.concatenate(window, axis=0) * mask_ref[g]
             y = jnp.dot(band_of(taps_ref[at])[:, :depth], window, preferred_element_type=F32)
-            conv_s[slot, g] = chosen(y, sel_ref) + bias_ref[pl.ds(at, 1), :] * xg.astype(F32)
-            turned = jnp.concatenate([turned_ref[at]] * KINDS, axis=0) * turned_mask_ref[...]
+            conv_s[slot, g] = chosen(y, sel_ref, g) + bias_ref[pl.ds(at, 1), :] * xg.astype(F32)
+            turned = jnp.concatenate([turned_ref[at]] * KINDS, axis=0) * turned_mask_ref[g]
             pairs = lax.dot_general(turned, window, (((1,), (1,)), ((), ())), preferred_element_type=F32)
             pairs = jnp.concatenate([pairs, jnp.zeros((KINDS * TB, WIDE - depth), F32)], axis=1)
-            grad_s[slot, g : g + 1, :] = skew_left(jnp.where(band, pairs, 0.0))
+            half = TB // 2
+            far = pairs[(KINDS - 1) * TB :, :LANES]
+            grad_s[slot, 0, g * half : (g + 1) * half, :] = skew_left(jnp.where(lane > late, far, 0.0))
+            own = jnp.zeros((TB, LANES), F32)
+            for kind in range(KINDS):
+                first = (KINDS - 1 - kind) * TB
+                own = jnp.where(causal & (lane // TB == kind), pairs[first : first + TB, LANES:], own)
+            grad_s[slot, 1, g * half : (g + 1) * half, :] = skew_left(own)
 
         def more(index, carry):
             level, g = index // per, index % per
             at = sub * per + g
-            here = order_ref[...] == level.astype(F32)
+            here = order_ref[g] == level.astype(F32)
             xq = jnp.where(here, x_ref[at].astype(F32), 0.0).astype(BF16)
-            turned = turned_order_ref[...] == level.astype(F32)
+            turned = turned_order_ref[g] == level.astype(F32)
             turned = jnp.where(turned, turned_ref[at].astype(F32), 0.0).astype(BF16)
             own = taps_ref[at][TB : 2 * TB, :TB]
             conv_s[slot, g] += jnp.where(here, jnp.dot(own, xq, preferred_element_type=F32), 0.0)
             pairs = lax.dot_general(turned, xq, (((1,), (1,)), ((), ())), preferred_element_type=F32)
-            pairs = jnp.concatenate(
-                [jnp.zeros((TB, filter_size), F32), pairs, jnp.zeros((TB, WIDE - filter_size - TB), F32)], axis=1
-            )
-            grad_s[slot, pl.ds(g, 1), :] += skew_left(pairs)
+            pairs = jnp.concatenate([pairs, jnp.zeros((TB, LANES - TB), F32)], axis=1)
+            rows = pl.ds(pl.multiple_of(g * (TB // 2), TB // 2), TB // 2)
+            grad_s[slot, 1, rows, :] += skew_left(jnp.where(causal & (lane < TB), pairs, 0.0))
             return carry
 
         if further:
             lax.fori_loop(KINDS * per, info[0] * per, more, 0)
-        gf_ref[pl.ds(pl.multiple_of(sub * per, per), per), :] = jnp.dot(
-            grad_s[slot, :, :filter_size],
-            permutation(filter_size).astype(F32),
-            precision=lax.Precision.HIGHEST,
-            preferred_element_type=F32,
-        )
+        own = exact_dot(group_rows(per, TB // 2), grad_s[slot, 1])
+        terms = exact_dot(group_rows(per, TB // 2), grad_s[slot, 0])
+        last = iota((per, LANES), 1) >= LANES - TB
+        for kind in range(KINDS):
+            shift = (LANES - kind * TB) % LANES
+            terms += jnp.where(last, pltpu.roll(own, shift, 1) if shift else own, 0.0)
+        gf_ref[pl.ds(pl.multiple_of(sub * per, per), per), :] = exact_dot(terms, permutation(LANES).astype(F32))
         filtered = from_groups([conv_s[slot, g] for g in range(per)], bits32, chunk)
         out_ref[:, lanes] = (q_ref[:, lanes].astype(F32) * filtered).astype(BF16)
         gq_ref[:, lanes] = (ct_ref[:, lanes].astype(F32) * filtered).astype(BF16)
@@ -201,7 +242,8 @@
 
 def back_kernel(chunk, filter_size, info, k_ref, v_ref, dy_ref, taps_ref, bias_ref, rim_ref, mask_ref, sel_ref,
                 order_ref, *rest):
-    gk_ref, gv_ref, back_s = rest[-3:]
+    gk_ref, gv_ref, token_ref, back_s = rest[-4:]
+    token_ref[...] = jnp.zeros_like(token_ref)
     width = k_ref.shape[1]
     per = LANES // chunk
     steps = filter_size // TB
@@ -210,21 +252,20 @@
     def one(sub, slot, further):
         lanes = pl.ds(pl.multiple_of(sub * LANES, LANES), LANES)
         bits, bits32 = chunk_bits(BF16, chunk), chunk_bits(F32, chunk)
-        pos = chunk_of((TB, LANES), BF16, chunk)
         rims = to_groups(rim_ref[:, lanes], bits, chunk)
         for g in range(per):
             at = sub * per + g
             dyg = dy_ref[at]
             ext = [dyg[:, i : i + LANES] for i in range(0, dyg.shape[1], LANES)] + rims[g]
-            window = windows(ext, pos, chunk, steps) + [dyg] * (KINDS - 1)
-            window = jnp.concatenate(window, axis=0) * mask_ref[...]
+            window = next_windows(ext, place_of(g, chunk), chunk, steps) + [dyg] * (KINDS - 1)
+            window = jnp.concatenate(window, axis=0) * mask_ref[g]
             y = jnp.dot(band_of(taps_ref[at])[:, :depth], window, preferred_element_type=F32)
-            back_s[slot, g] = chosen(y, sel_ref) + bias_ref[pl.ds(at, 1), :] * dyg.astype(F32)
+            back_s[slot, g] = chosen(y, sel_ref, g) + bias_ref[pl.ds(at, 1), :] * dyg.astype(F32)
 
         def more(index, carry):
             level, g = index // per, index % per
             at = sub * per + g
-            here = order_ref[...] == level.astype(F32)
+            here = order_ref[g] == level.astype(F32)
             dyq = jnp.where(here, dy_ref[at].astype(F32), 0.0).astype(BF16)
             own = taps_ref[at][:TB, :TB]
             back_s[slot, g] += jnp.where(here, jnp.dot(own, dyq, preferred_element_type=F32), 0.0)
@@ -273,7 +314,7 @@
         ),
         out_shape=[jax.ShapeDtypeStruct(shape, kind) for shape, kind, _, _ in outs],
         input_output_aliases=aliases,
-        compiler_params=pltpu.CompilerParams(vmem_limit_bytes=48 * 1024 * 1024),
+        compiler_params=pltpu.CompilerParams(vmem_limit_bytes=VMEM_BYTES),
         cost_estimate=pl.CostEstimate(flops=2**24, bytes_accessed=2**20, transcendentals=0),
         name=name,
     )(info, *operands)
@@ -289,7 +330,7 @@
 
 
 def fixed(array):
-    return (array, array.shape, lambda i, c: (0, 0))
+    return (array, array.shape, lambda i, c: (0, 0, 0))
 
 
 def prepare(info, big, filters):
@@ -301,6 +342,7 @@
     shapes = [(TB, row_count)] * 3 + [((1 + KINDS) * TB, LANES)] * 2
     outs = [((total, *s), BF16, (groups, *s), lambda i, c: (i, 0, 0)) for s in shapes]
     outs.append(((1, channels), F32, (1, block), lambda i, c: (0, i)))
+    outs.append(((filter_size, channels), BF16, (filter_size, block), lambda i, c: (0, i)))
     return call(functools.partial(prepare_kernel, chunk), "prepare", info, channels // block, ins, outs)
 
 
@@ -316,7 +358,9 @@
     scratch = [pltpu.VMEM((TOGETHER, per, TB, row_count), F32)]
     if small:
         outs += [((channels // chunk, filter_size), F32, (groups, filter_size), lambda i, c: (first + i, 0))]
-        scratch += [pltpu.VMEM((TOGETHER, per, WIDE), F32)]
+        scratch += [pltpu.VMEM((TOGETHER, 2, per * TB // 2, LANES), F32)]
+    else:
+        outs += [((8, LANES), F32, (8, LANES), lambda i, c: (0, 0))]
     kernel = functools.partial(kernel, chunk, filter_size)
     return call(kernel, name, info, width // block, ins, outs, scratch, previous)
 
@@ -328,8 +372,7 @@
     lane, row = iota((TB, total), 1), iota((TB, total), 0)
     spread = jnp.where(lane % TB == row, jnp.broadcast_to(near, (TB, total)), 0.0)
     same = flag(iota((total, total), 0) // TB == iota((total, total), 1) // TB, F32)
-    begin = jnp.dot(spread, same, precision=lax.Precision.HIGHEST, preferred_element_type=F32)
-    begin = jnp.floor(begin + 0.5)
+    begin = jnp.floor(exact_dot(spread, same) + 0.5)
     own = begin[:, :rows]
     block = iota((TB, rows), 1) // TB * TB
     pos = (block + iota((TB, rows), 0)).astype(F32)
@@ -338,35 +381,39 @@
     order = jnp.dot(before, marks, preferred_element_type=F32)
     behind = order[TB - 1 :] - order
     first = jnp.broadcast_to(own[:1], (TB, rows))
+    turn = permutation(TB)
+
+    def put(ref, at, value):
+        parts = [value[:, i : i + LANES] for i in range(0, rows, LANES)]
+        for g in range(ref.shape[0]):
+            turned = side_by_side([pltpu.roll(a, g * TB, 1) if g else a for a in parts])
+            ref[g, at * TB : (at + 1) * TB, :] = turned.astype(ref.dtype)
+
     for i in range(steps):
-        mask_x[i * TB : (i + 1) * TB, :] = flag(pos - TB * (steps - i) >= first)
+        put(mask_x, i, flag(pos - TB * (steps - i) >= first, F32))
         later = pltpu.roll(begin, total - (i + 1) * TB, 1)[:, :rows]
-        mask_dy[(i + 1) * TB : (i + 2) * TB, :] = flag(later <= (block + TB - 1).astype(F32))
-    turn = permutation(TB)
+        put(mask_dy, i + 1, flag(later <= (block + TB - 1).astype(F32), F32))
     for kind in range(KINDS):
-        at = steps + kind
-        mask_x[at * TB : (at + 1) * TB, :] = flag(order == kind)
-        sel_x[kind * TB : (kind + 1) * TB, :] = flag(order == kind, F32)
-        at = KINDS - 1 - kind
-        turned = jnp.dot(turn, flag(order == kind), preferred_element_type=F32)
-        turned_x[at * TB : (at + 1) * TB, :] = turned.astype(BF16)
-        at = steps + kind if kind else 0
-        mask_dy[at * TB : (at + 1) * TB, :] = flag(behind == kind)
-        sel_dy[kind * TB : (kind + 1) * TB, :] = flag(behind == kind, F32)
-    order_x[...], order_dy[...] = order, behind
-    turned_order_x[...] = jnp.dot(turn, order.astype(BF16), preferred_element_type=F32)
+        put(mask_x, steps + kind, flag(order == kind, F32))
+        put(sel_x, kind, flag(order == kind, F32))
+        put(turned_x, KINDS - 1 - kind, jnp.dot(turn, flag(order == kind), preferred_element_type=F32))
+        put(mask_dy, steps + kind if kind else 0, flag(behind == kind, F32))
+        put(sel_dy, kind, flag(behind == kind, F32))
+    put(order_x, 0, order)
+    put(order_dy, 0, behind)
+    put(turned_order_x, 0, jnp.dot(turn, order.astype(BF16), preferred_element_type=F32))
     kinds[0] = 1 + jnp.max(order).astype(jnp.int32)
 
 
 def reset_masks(near, row_count, steps):
-    depth, high = (steps + KINDS) * TB, KINDS * TB
+    depth, high, per = (steps + KINDS) * TB, KINDS * TB, LANES // TB
     shapes = [(depth, BF16), (high, BF16), (high, F32), (TB, F32), (TB, F32), (depth, BF16), (high, F32), (TB, F32)]
     out = pl.pallas_call(
         functools.partial(reset_kernel, steps),
-        out_shape=[jax.ShapeDtypeStruct((rows, row_count), kind) for rows, kind in shapes]
+        out_shape=[jax.ShapeDtypeStruct((per, rows, row_count), kind) for rows, kind in shapes]
         + [jax.ShapeDtypeStruct((1,), jnp.int32)],
         out_specs=[pl.BlockSpec(memory_space=pltpu.VMEM)] * len(shapes) + [pl.BlockSpec(memory_space=pltpu.SMEM)],
-        compiler_params=pltpu.CompilerParams(vmem_limit_bytes=32 * 1024 * 1024),
+        compiler_params=pltpu.CompilerParams(vmem_limit_bytes=VMEM_BYTES),
         name="resets",
     )(near)
     return out[:5], out[5:8], out[8]
@@ -378,14 +425,16 @@
     return lax.ppermute(value, axis, [(source, source + steps) for source in range(initial, last)])
 
 
-def sum_over(value, axis):
+def sum_over(value, axis, tokens):
     count = lax.axis_size(axis)
     if count & (count - 1):
         return lax.psum(value, axis)
-    step = 1
-    while step < count:
-        value = value + lax.ppermute(value, axis, [(i, i ^ step) for i in range(count)])
-        step *= 2
+    steps = count.bit_length() - 1
+    for index in range(steps):
+        other = lax.ppermute(value, axis, [(i, i ^ (1 << index)) for i in range(count)])
+        if index % 2 == 0 and index // 2 < len(tokens):
+            other = other + tokens[index // 2][0, 0]
+        value = value + other
     return value
 
 
@@ -418,36 +467,30 @@
     info = jnp.concatenate([kinds, tensor.astype(jnp.int32).reshape(1)])
     bias = jnp.tile(skip_bias.reshape(groups, chunk), (1, row_count // TB))
     big = (queries, cotangent, key_branch, value_branch)
-    x, dy, turned, band_x, band_dy, bias_part = prepare(info, big, filters)
-
-    right = []
-    for part in range(PARTS):
-        cut = lambda m: lax.slice(m, (0, part * width), (filter_size, (part + 1) * width))
-        sent = product_bf16(cut(cotangent), cut(queries))
-        if part:
-            sent, right[-1] = lax.optimization_barrier((sent, right[-1]))
-        else:
-            sent, bias_part = lax.optimization_barrier((sent, bias_part))
-        right.append(passed_along(sent, "ctx", -1))
-
-    done, rim = None, left
+    place = jnp.stack([tensor, tensor]).astype(jnp.int32)
+    x, dy, turned, band_x, band_dy, bias_part, head = prepare(place, big, filters)
+
+    right = passed_along(head, "ctx", -1)
+
+    done = None
     for part in range(PARTS):
         grouped = (x, turned, band_x, bias)
-        done = run_part(
-            conv_kernel, "conv", part, info, (queries, cotangent), grouped, rim, part, masks_x, filter_size, True, done
-        )
+        pair = (queries, cotangent)
+        done = run_part(conv_kernel, "conv", part, info, pair, grouped, left, part, masks_x, filter_size, True, done)
     output, grad_query, filter_part = done
-    done = None
+    terms = jnp.concatenate([filter_part, bias_part.reshape(channels // filter_size, filter_size)], axis=0)
+
+    done, tokens = None, []
     for part in range(PARTS):
         grouped = (dy, band_dy, bias)
         pair = (key_branch, value_branch)
-        done = run_part(
-            back_kernel, "back", part, info, pair, grouped, right[part], 0, masks_dy, filter_size, False, done
+        *done, token = run_part(
+            back_kernel, "back", part, info, pair, grouped, right, part, masks_dy, filter_size, False, done
         )
+        tokens.append(token)
     grad_key, grad_value = done
 
-    terms = jnp.concatenate([filter_part, bias_part.reshape(channels // filter_size, filter_size)], axis=0)
-    terms = sum_over(terms, "ctx")
+    terms = sum_over(terms, "ctx", tokens)
     grad_filter = rows_of_all(terms[:groups], "tp") * (1.0 / math.sqrt(token_count * chunk))
     grad_bias = terms[groups:].reshape(channels) * (1.0 / math.sqrt(token_count))
     return (output, grad_query, grad_key, grad_value, grad_filter, grad_bias)

time: 136 us -> 136 us (level)
  the two profiles are of different devices: /device:TPU:11 before, /device:TPU:0 now
where the time goes in v5:
time: 136 us; the launch traced here: 135 us
  Pallas kernels  74 us (54%)
  waiting for transfers between devices  34.9 us (26%)
  starting transfers between devices  11.6 us (9%)
  other arithmetic  7.27 us (5%)
  local copies, waits for them, and re-layouts  5.99 us (4%)
    pallas_call x5, Pallas kernels, call(): pl.pallas_call(kernel, grid_spec=pltpu.PrefetchScalarGridSpec(num_scalar_...  70.9 us
    ppermute x2, waiting for transfers between devices, passed_along(): lax.ppermute(value, axis, [(source, source + steps) for source in range(i...  22.6 us
    ppermute x4, waiting for transfers between devices, sum_over(): lax.ppermute(value, axis, [(i, i ^ 1 << index) for i in range(count)])  11.6 us
    ppermute x2, starting transfers between devices, passed_along(): lax.ppermute(value, axis, [(source, source + steps) for source in range(i...  6.2 us
    ppermute x4, starting transfers between devices, sum_over(): lax.ppermute(value, axis, [(i, i ^ 1 << index) for i in range(count)])  5.37 us
    pallas_call x1, Pallas kernels, reset_masks(): pl.pallas_call(functools.partial(reset_kernel, steps), out_shape=[jax.Sha...  3.1 us
  transfers between devices with their start and end apart: 7, of which 4 were waited for; matrix products, arithmetic and copies ran while one was open for 6% of the time, Pallas kernels for 55%

profile of v5, /device:TPU:0, one launch (start us, length us, event | category | flops | bytes accessed | tf_op | source)
XLA Modules:
  0.0 134.7 jit_solution(850285053827491117)
XLA Ops:
  0.6 1.8 %multiply_convert_fusion = bf16[128,4096]{1,0:T(8,128)(2,1)S(1)} fusion(bf16[256,4096]{1,0:T(8,128)(2,1)} %v_ref.5, bf16[256,4096]{1,0:T(8,128)(2,1)} %k_ref.5), kind=kLoop, calls=%fused_computation | loop fusion | flops 2097152 | bytes 3145728 | tf_op jit(solution)/shard_map/convert_element_type | solution.py:112
  2.4 4.9 %collective-permute-start = (bf16[128,4096]{1,0:T(8,128)(2,1)S(1)}, bf16[128,4096]{1,0:T(8,128)(2,1)S(1)}, u32[]{:S(2)}, u32[]{:S(2)}) collective-permute-start(bf16[128,4096]{1,0:T(8,128)(2,1)S(1)} %multiply_convert_fusion), channel_id=1, source_target_pairs={{0,2},{2,4},{4,6},{6,8},{8,10},{10,12},{12,14},{14,16},{16,18},{18... | collective-permute-start | bytes 3145736 | tf_op jit(solution)/shard_map/ppermute | solution.py:425
  7.9 14.2 %prepare.1 = (bf16[256,16,256]{2,1,0:T(8,128)(2,1)}, bf16[256,16,256]{2,1,0:T(8,128)(2,1)}, bf16[256,16,256]{2,1,0:T(8,128)(2,1)}, bf16[256,64,128]{2,1,0:T(8,12...) custom-call(s32[2]{0:T(128)} %pad_add_fusion.1.info, ...), custom_call_target="tpu_custom_call" | custom-call | flops 16777216 | bytes 1048576 | tf_op jit(solution)/shard_map/prepare/pallas_call | solution.py:306
  22.2 1.3 collective-permute-start.1
  24.3 0.8 copy.20.bias_ref
  25.2 3.1 %resets.1 = (bf16[8,176,256]{2,1,0:T(8,128)(2,1)}, bf16[8,48,256]{2,1,0:T(8,128)(2,1)}, f32[8,48,256]{2,1,0:T(8,128)}, f32[8,16,256]{2,1,0:T(8,128)}, f32[8,16,2...) custom-call(s32[1,384]{1,0:T(1,128)} %broadcast_in_dim.4.near_ref), custom_call_target="tpu_custom_call" | custom-call | tf_op jit(solution)/shard_map/resets/pallas_call | solution.py:411
  28.3 1.3 pad_add_fusion.info
  29.5 22.6 %collective-permute-done.rim_ref = bf16[128,4096]{1,0:T(8,128)(2,1)S(1)} collective-permute-done((bf16[128,4096]{1,0:T(8,128)(2,1)S(1)}, bf16[128,4096]{1,0:T(8,128)(2,1)S(1)}, u32[]{:S(2)}, u32[]{:S(2)}) %collective-permute-start) | collective-permute-done | bytes 1048608 | tf_op jit(solution)/shard_map/ppermute | solution.py:425
  52.2 1.0 copy-done.1
  53.2 19.0 %conv.2 = (bf16[256,4096]{1,0:T(8,128)(2,1)}, bf16[256,4096]{1,0:T(8,128)(2,1)}, f32[256,128]{1,0:T(8,128)}) custom-call(s32[2]{0:T(128)} %pad_add_fusion.info, bf16[256,4096]{1,0:T(8,128)(2,1)} %q_ref.5, bf16[256,4096]{1,0:T(8,128)(2,1)} %ct_ref.5, bf16[256,16,256]{2,1,0:T(8,128)(2,1)} %get-tuple-element.35.x_ref, ...), custom_call_target="tpu_custom_call" | custom-call | flops 16777216 | bytes 1048576 | tf_op jit(solution)/shard_map/conv/pallas_call | solution.py:306
  72.2 19.0 %conv.3 = (bf16[256,4096]{1,0:T(8,128)(2,1)}, bf16[256,4096]{1,0:T(8,128)(2,1)}, f32[256,128]{1,0:T(8,128)}) custom-call(s32[2]{0:T(128)} %pad_add_fusion.info, bf16[256,4096]{1,0:T(8,128)(2,1)} %q_ref.5, bf16[256,4096]{1,0:T(8,128)(2,1)} %ct_ref.5, ...), custom_call_target="tpu_custom_call", output_to_operand_aliasing={{0}: (13, {}), {1}: (14, {}), {2}: (15, {})} | custom-call | flops 16777216 | bytes 1048576 | tf_op jit(solution)/shard_map/conv/pallas_call | solution.py:306
  91.3 0.9 pad_maximum_fusion
  92.2 2.5 %collective-permute-start.2 = (f32[288,128]{1,0:T(8,128)S(1)}, f32[288,128]{1,0:T(8,128)S(1)}, u32[]{:S(2)}, u32[]{:S(2)}) collective-permute-start(f32[288,128]{1,0:T(8,128)S(1)} %pad_maximum_fusion), channel_id=1, source_target_pairs={{0,2},{2,0},{4,6},{6,4},{8,10},{10,8},{12,14},{14,12},{16,18},{18,... | collective-permute-start | bytes 442376 | tf_op jit(solution)/shard_map/ppermute | solution.py:434
  94.7 1.0 copy-done
  95.7 9.4 %back.2 = (bf16[256,4096]{1,0:T(8,128)(2,1)}, bf16[256,4096]{1,0:T(8,128)(2,1)}, f32[8,128]{1,0:T(8,128)}) custom-call(s32[2]{0:T(128)} %pad_add_fusion.info, bf16[256,4096]{1,0:T(8,128)(2,1)} %k_ref.5, bf16[256,4096]{1,0:T(8,128)(2,1)} %v_ref.5, bf16[256,16,256]{2,1,0:T(8,128)(2,1)} %get-tuple-element.48.dy_ref, ...), custom_call_target="tpu_custom_call" | custom-call | flops 16777216 | bytes 1048576 | tf_op jit(solution)/shard_map/back/pallas_call | solution.py:306
  105.1 1.2 slice.20
  107.0 5.1 %collective-permute-done.3 = f32[288,128]{1,0:T(8,128)S(1)} collective-permute-done((f32[288,128]{1,0:T(8,128)S(1)}, f32[288,128]{1,0:T(8,128)S(1)}, u32[]{:S(2)}, u32[]{:S(2)}) %collective-permute-start.3) | collective-permute-done | bytes 147488 | tf_op jit(solution)/shard_map/ppermute | solution.py:434
  112.1 1.6 %collective-permute-start.4 = (f32[288,128]{1,0:T(8,128)S(1)}, f32[288,128]{1,0:T(8,128)S(1)}, u32[]{:S(2)}, u32[]{:S(2)}) collective-permute-start(f32[288,128]{1,0:T(8,128)S(1)} %add.33), channel_id=1, source_target_pairs={{0,8},{2,10},{4,12},{6,14},{8,0},{10,2},{12,4},{14,6},{16,24},{18,... | collective-permute-start | bytes 442376 | tf_op jit(solution)/shard_map/ppermute | solution.py:434
  113.8 9.2 %back.3 = (bf16[256,4096]{1,0:T(8,128)(2,1)}, bf16[256,4096]{1,0:T(8,128)(2,1)}, f32[8,128]{1,0:T(8,128)}) custom-call(s32[2]{0:T(128)} %pad_add_fusion.info, bf16[256,4096]{1,0:T(8,128)(2,1)} %k_ref.5, bf16[256,4096]{1,0:T(8,128)(2,1)} %v_ref.5, bf16[256,16,256]{2,1,0:T(8,128)(2,1)} %get-tuple-element.48.dy_ref, ...), custom_call_target="tpu_custom_call", output_to_operand_aliasing={{0}: (10, {}), {1}: (11, {})} | custom-call | flops 16777216 | bytes 1048576 | tf_op jit(solution)/shard_map/back/pallas_call | solution.py:306
  123.0 1.2 slice.21
  124.9 1.1 collective-permute-start.5
  126.0 6.5 %collective-permute-done.5 = f32[288,128]{1,0:T(8,128)S(1)} collective-permute-done((f32[288,128]{1,0:T(8,128)S(1)}, f32[288,128]{1,0:T(8,128)S(1)}, u32[]{:S(2)}, u32[]{:S(2)}) %collective-permute-start.5) | collective-permute-done | bytes 147488 | tf_op jit(solution)/shard_map/ppermute | solution.py:434
  133.2 0.7 collective-permute-done.6
  133.9 0.7 maximum_multiply_fusion
  (28 shorter events, 3.5 us)
Async XLA Ops:
  2.4 49.7 %collective-permute-start = (bf16[128,4096]{1,0:T(8,128)(2,1)S(1)}, bf16[128,4096]{1,0:T(8,128)(2,1)S(1)}, u32[]{:S(2)}, u32[]{:S(2)}) collective-permute-start(bf16[128,4096]{1,0:T(8,128)(2,1)S(1)} %multiply_convert_fusion), channel_id=1, source_target_pairs={{0,2},{2,4},{4,6},{6,8},{8,10},{10,12},{12,14},{14,16},{16,18},{18... | collective-permute-start | bytes 3145736 | tf_op jit(solution)/shard_map/ppermute | solution.py:425
  7.9 15.5 %copy-start.5 = (s32[4096]{0:T(1024)S(1)}, s32[4096]{0:T(1024)}, u32[]{:S(2)}) copy-start(s32[4096]{0:T(1024)} %param.13) | copy-start | bytes 49156
  7.9 16.2 %copy-start.4 = (f32[4096]{0:T(1024)S(1)}, f32[4096]{0:T(1024)}, u32[]{:S(2)}) copy-start(f32[4096]{0:T(1024)} %param.12) | copy-start | bytes 49156
  22.2 72.6 %collective-permute-start.1 = (bf16[128,4096]{1,0:T(8,128)(2,1)}, bf16[128,4096]{1,0:T(8,128)(2,1)S(1)}, u32[]{:S(2)}, u32[]{:S(2)}) collective-permute-start(bf16[128,4096]{1,0:T(8,128)(2,1)} %get-tuple-element.50), channel_id=1, source_target_pairs={{2,0},{4,2},{6,4},{8,6},{10,8},{12,10},{14,12},{16,14},{18,16},{20... | collective-permute-start | bytes 3145736 | tf_op jit(solution)/shard_map/ppermute | solution.py:425
  52.1 1.0 copy-start.1
  72.2 19.1 %copy-start.3 = (f32[1,4096]{1,0:T(1,128)S(1)}, f32[1,4096]{1,0:T(1,128)}, u32[]{:S(2)}) copy-start(f32[1,4096]{1,0:T(1,128)} %get-tuple-element.59) | copy-start | bytes 49156
  92.2 14.1 %collective-permute-start.2 = (f32[288,128]{1,0:T(8,128)S(1)}, f32[288,128]{1,0:T(8,128)S(1)}, u32[]{:S(2)}, u32[]{:S(2)}) collective-permute-start(f32[288,128]{1,0:T(8,128)S(1)} %pad_maximum_fusion), channel_id=1, source_target_pairs={{0,2},{2,0},{4,6},{6,4},{8,10},{10,8},{12,14},{14,12},{16,18},{18,... | collective-permute-start | bytes 442376 | tf_op jit(solution)/shard_map/ppermute | solution.py:434
  94.7 1.0 copy-start
  95.7 10.6 %copy-start.2 = (f32[256,128]{1,0:T(8,128)S(1)}, f32[256,128]{1,0:T(8,128)}, u32[]{:S(2)}) copy-start(f32[256,128]{1,0:T(8,128)} %get-tuple-element.58) | copy-start | bytes 393220
  106.9 5.2 %collective-permute-start.3 = (f32[288,128]{1,0:T(8,128)S(1)}, f32[288,128]{1,0:T(8,128)S(1)}, u32[]{:S(2)}, u32[]{:S(2)}) collective-permute-start(f32[288,128]{1,0:T(8,128)S(1)} %add_add_fusion.1), channel_id=1, source_target_pairs={{0,4},{2,6},{4,0},{6,2},{8,12},{10,14},{12,8},{14,10},{16,20},{18,... | collective-permute-start | bytes 442376 | tf_op jit(solution)/shard_map/ppermute | solution.py:434
  112.1 12.1 %collective-permute-start.4 = (f32[288,128]{1,0:T(8,128)S(1)}, f32[288,128]{1,0:T(8,128)S(1)}, u32[]{:S(2)}, u32[]{:S(2)}) collective-permute-start(f32[288,128]{1,0:T(8,128)S(1)} %add.33), channel_id=1, source_target_pairs={{0,8},{2,10},{4,12},{6,14},{8,0},{10,2},{12,4},{14,6},{16,24},{18,... | collective-permute-start | bytes 442376 | tf_op jit(solution)/shard_map/ppermute | solution.py:434
  124.9 7.6 %collective-permute-start.5 = (f32[288,128]{1,0:T(8,128)S(1)}, f32[288,128]{1,0:T(8,128)S(1)}, u32[]{:S(2)}, u32[]{:S(2)}) collective-permute-start(f32[288,128]{1,0:T(8,128)S(1)} %add_add_fusion), channel_id=1, source_target_pairs={{0,16},{2,18},{4,20},{6,22},{8,24},{10,26},{12,28},{14,30},{16,0},... | collective-permute-start | bytes 442376 | tf_op jit(solution)/shard_map/ppermute | solution.py:434
  132.5 1.4 %collective-permute-start.6 = (f32[256,128]{1,0:T(8,128)S(1)}, f32[256,128]{1,0:T(8,128)S(1)}, u32[]{:S(2)}, u32[]{:S(2)}) collective-permute-start(f32[256,128]{1,0:T(8,128)S(1)} %slice.24), channel_id=1, source_target_pairs={{0,1},{1,0},{2,3},{3,2},{4,5},{5,4},{6,7},{7,6},{8,9},{9,8},{10,11... | collective-permute-start | bytes 393224 | tf_op jit(solution)/shard_map/ppermute | solution.py:445

commit v6 on v5

--- a/solution.py
+++ b/solution.py
@@ -13,7 +13,7 @@
 TB = 16
 WIDE = 256
 KINDS = 3
-PARTS = 2
+BACK_PARTS = 4
 VMEM_BYTES = 60 * 1024 * 1024
 TOGETHER = 2
 
@@ -114,15 +114,11 @@
 
 def skew_left(products):
     moved = pltpu.roll(products, LANES - TB, 1, stride=1, stride_axis=0)
-    return moved[: TB // 2] + moved[TB // 2 :]
+    return jnp.sum(moved, axis=0, keepdims=True)
 
 
 def exact_dot(a, b):
     return jnp.dot(a, b, precision=lax.Precision.HIGHEST, preferred_element_type=F32)
-
-
-def group_rows(count, size):
-    return flag(iota((count, count * size), 1) // size == iota((count, count * size), 0), F32)
 
 
 def shifted_taps(row, first):
@@ -200,14 +196,13 @@
             turned = jnp.concatenate([turned_ref[at]] * KINDS, axis=0) * turned_mask_ref[g]
             pairs = lax.dot_general(turned, window, (((1,), (1,)), ((), ())), preferred_element_type=F32)
             pairs = jnp.concatenate([pairs, jnp.zeros((KINDS * TB, WIDE - depth), F32)], axis=1)
-            half = TB // 2
             far = pairs[(KINDS - 1) * TB :, :LANES]
-            grad_s[slot, 0, g * half : (g + 1) * half, :] = skew_left(jnp.where(lane > late, far, 0.0))
+            grad_s[slot, 0, g : g + 1, :] = skew_left(jnp.where(lane > late, far, 0.0))
             own = jnp.zeros((TB, LANES), F32)
             for kind in range(KINDS):
                 first = (KINDS - 1 - kind) * TB
                 own = jnp.where(causal & (lane // TB == kind), pairs[first : first + TB, LANES:], own)
-            grad_s[slot, 1, g * half : (g + 1) * half, :] = skew_left(own)
+            grad_s[slot, 1, g : g + 1, :] = skew_left(own)
 
         def more(index, carry):
             level, g = index // per, index % per
@@ -220,19 +215,17 @@
             conv_s[slot, g] += jnp.where(here, jnp.dot(own, xq, preferred_element_type=F32), 0.0)
             pairs = lax.dot_general(turned, xq, (((1,), (1,)), ((), ())), preferred_element_type=F32)
             pairs = jnp.concatenate([pairs, jnp.zeros((TB, LANES - TB), F32)], axis=1)
-            rows = pl.ds(pl.multiple_of(g * (TB // 2), TB // 2), TB // 2)
-            grad_s[slot, 1, rows, :] += skew_left(jnp.where(causal & (lane < TB), pairs, 0.0))
+            grad_s[slot, 1, pl.ds(g, 1), :] += skew_left(jnp.where(causal & (lane < TB), pairs, 0.0))
             return carry
 
         if further:
             lax.fori_loop(KINDS * per, info[0] * per, more, 0)
-        own = exact_dot(group_rows(per, TB // 2), grad_s[slot, 1])
-        terms = exact_dot(group_rows(per, TB // 2), grad_s[slot, 0])
+        terms, own = grad_s[slot, 0], grad_s[slot, 1]
         last = iota((per, LANES), 1) >= LANES - TB
         for kind in range(KINDS):
             shift = (LANES - kind * TB) % LANES
             terms += jnp.where(last, pltpu.roll(own, shift, 1) if shift else own, 0.0)
-        gf_ref[pl.ds(pl.multiple_of(sub * per, per), per), :] = exact_dot(terms, permutation(LANES).astype(F32))
+        gf_ref[pl.ds(pl.multiple_of(sub * per, per), per), :] = terms
         filtered = from_groups([conv_s[slot, g] for g in range(per)], bits32, chunk)
         out_ref[:, lanes] = (q_ref[:, lanes].astype(F32) * filtered).astype(BF16)
         gq_ref[:, lanes] = (ct_ref[:, lanes].astype(F32) * filtered).astype(BF16)
@@ -295,7 +288,7 @@
     pl.when(info[0] > KINDS)(lambda: run(True))
 
 
-def call(kernel, name, info, count, ins, outs, scratch=(), previous=None):
+def call(kernel, name, info, count, ins, outs, scratch=(), previous=None, after=()):
     operands = [a for a, _, _ in ins]
     in_specs = [pl.BlockSpec(block, at) for _, block, at in ins]
     aliases = {}
@@ -303,6 +296,8 @@
         aliases = {1 + len(operands) + i: i for i in range(len(previous))}
         in_specs += [pl.BlockSpec(memory_space=pl.ANY)] * len(previous)
         operands += list(previous)
+    in_specs += [pl.BlockSpec(memory_space=pl.ANY)] * len(after)
+    operands += list(after)
     return pl.pallas_call(
         kernel,
         grid_spec=pltpu.PrefetchScalarGridSpec(
@@ -337,7 +332,7 @@
     row_count, channels = big[0].shape
     chunk, block = TB, math.gcd(channels, 512)
     groups, total, filter_size = block // chunk, channels // chunk, filters.shape[1]
-    taps = (filters, (groups, filter_size), lambda i, c: (c[1] * (channels // block) + i, 0))
+    taps = (filters, (groups, filter_size), lambda i, c: (c[0] * (channels // block) + i, 0))
     ins = [wide(a, block, 0) for a in big] + [taps]
     shapes = [(TB, row_count)] * 3 + [((1 + KINDS) * TB, LANES)] * 2
     outs = [((total, *s), BF16, (groups, *s), lambda i, c: (i, 0, 0)) for s in shapes]
@@ -346,9 +341,9 @@
     return call(functools.partial(prepare_kernel, chunk), "prepare", info, channels // block, ins, outs)
 
 
-def run_part(kernel, name, part, info, pair, grouped, rim, rim_first, masks, filter_size, small, previous):
+def run_part(kernel, name, part, parts, info, pair, grouped, rim, rim_first, masks, filter_size, small, previous=None, after=()):
     row_count, channels = pair[0].shape
-    chunk, width = TB, channels // PARTS
+    chunk, width = TB, channels // parts
     block = math.gcd(width, 512)
     groups, first = block // chunk, part * (width // block)
     per = LANES // chunk
@@ -358,11 +353,11 @@
     scratch = [pltpu.VMEM((TOGETHER, per, TB, row_count), F32)]
     if small:
         outs += [((channels // chunk, filter_size), F32, (groups, filter_size), lambda i, c: (first + i, 0))]
-        scratch += [pltpu.VMEM((TOGETHER, 2, per * TB // 2, LANES), F32)]
+        scratch += [pltpu.VMEM((TOGETHER, 2, per, LANES), F32)]
     else:
         outs += [((8, LANES), F32, (8, LANES), lambda i, c: (0, 0))]
     kernel = functools.partial(kernel, chunk, filter_size)
-    return call(kernel, name, info, width // block, ins, outs, scratch, previous)
+    return call(kernel, name, info, width // block, ins, outs, scratch, previous, after)
 
 
 def reset_kernel(steps, near_ref, mask_x, turned_x, sel_x, order_x, turned_order_x, mask_dy, sel_dy, order_dy, kinds):
@@ -425,17 +420,18 @@
     return lax.ppermute(value, axis, [(source, source + steps) for source in range(initial, last)])
 
 
-def sum_over(value, axis, tokens):
+def doubling(value, axis):
     count = lax.axis_size(axis)
     if count & (count - 1):
-        return lax.psum(value, axis)
-    steps = count.bit_length() - 1
-    for index in range(steps):
-        other = lax.ppermute(value, axis, [(i, i ^ (1 << index)) for i in range(count)])
-        if index % 2 == 0 and index // 2 < len(tokens):
-            other = other + tokens[index // 2][0, 0]
-        value = value + other
-    return value
+        yield [value, lax.psum(value, axis)]
+        return
+    step = 1
+    while step < count:
+        state = [lax.ppermute(value, axis, [(i, i ^ step) for i in range(count)]), value]
+        yield state
+        value = state[1] = state[0] + value
+        step *= 2
+    yield [value, value]
 
 
 def rows_of_all(value, axis):
@@ -455,7 +451,6 @@
     token_count = row_count * ctx_count
     chunk = channels * tp_count // group_total
     groups = channels // chunk
-    width = channels // PARTS
 
     tail = lambda m: m[row_count - filter_size :]
     left = passed_along(product_bf16(tail(key_branch), tail(value_branch)), "ctx", 1)
@@ -464,34 +459,38 @@
     first = shard * row_count
     near = (lax.dynamic_slice_in_dim(starts, first, row_count + filter_size, 0) - first)[None, :]
     masks_x, masks_dy, kinds = reset_masks(near, row_count, filter_size // TB)
-    info = jnp.concatenate([kinds, tensor.astype(jnp.int32).reshape(1)])
     bias = jnp.tile(skip_bias.reshape(groups, chunk), (1, row_count // TB))
     big = (queries, cotangent, key_branch, value_branch)
-    place = jnp.stack([tensor, tensor]).astype(jnp.int32)
+    place = tensor.astype(jnp.int32).reshape(1)
+    place, kinds, bias = lax.optimization_barrier((place, kinds, bias))
     x, dy, turned, band_x, band_dy, bias_part, head = prepare(place, big, filters)
 
+    left, head = lax.optimization_barrier((left, head))
     right = passed_along(head, "ctx", -1)
 
-    done = None
-    for part in range(PARTS):
-        grouped = (x, turned, band_x, bias)
-        pair = (queries, cotangent)
-        done = run_part(conv_kernel, "conv", part, info, pair, grouped, left, part, masks_x, filter_size, True, done)
-    output, grad_query, filter_part = done
+    pair, grouped = (queries, cotangent), (x, turned, band_x, bias)
+    output, grad_query, filter_part = run_part(
+        conv_kernel, "conv", 0, 1, kinds, pair, grouped, left, 0, masks_x, filter_size, True
+    )
     terms = jnp.concatenate([filter_part, bias_part.reshape(channels // filter_size, filter_size)], axis=0)
 
-    done, tokens = None, []
-    for part in range(PARTS):
-        grouped = (dy, band_dy, bias)
-        pair = (key_branch, value_branch)
+    pair, grouped = (key_branch, value_branch), (dy, band_dy, bias)
+    sums = doubling(terms, "ctx")
+    done, after, state = None, (), None
+    for part in range(BACK_PARTS):
+        arriving = next(sums, None)
+        state = arriving or state
         *done, token = run_part(
-            back_kernel, "back", part, info, pair, grouped, right, part, masks_dy, filter_size, False, done
+            back_kernel, "back", part, BACK_PARTS, kinds, pair, grouped, right, part, masks_dy, filter_size, False, done, after
         )
-        tokens.append(token)
+        if arriving is not None:
+            arriving[0], token = lax.optimization_barrier((arriving[0], token))
+        after = (token,)
     grad_key, grad_value = done
-
-    terms = sum_over(terms, "ctx", tokens)
-    grad_filter = rows_of_all(terms[:groups], "tp") * (1.0 / math.sqrt(token_count * chunk))
+    for state in sums:
+        pass
+    terms = state[1]
+    grad_filter = rows_of_all(terms[:groups], "tp")[:, ::-1] * (1.0 / math.sqrt(token_count * chunk))
     grad_bias = terms[groups:].reshape(channels) * (1.0 / math.sqrt(token_count))
     return (output, grad_query, grad_key, grad_value, grad_filter, grad_bias)
 

time: 136 us -> 95.5 us (0.70)
  waiting for transfers between devices: 34.9 us -> 5.66 us
  Pallas kernels: 74 us -> 64.4 us
  starting transfers between devices: 11.6 us -> 16.8 us
  local copies, waits for them, and re-layouts: 5.99 us -> 2.95 us
  other arithmetic: 7.27 us -> 4.25 us
    ppermute x2, waiting for transfers between devices: 22.6 us -> 4.93 us  [passed_along(): lax.ppermute(value, axis, [(source, source + steps) for source in range(i...]
    ppermute x4, waiting for transfers between devices: 11.6 us -> 0.01 us  [doubling(): lax.ppermute(value, axis, [(i, i ^ step) for i in range(count)])]
    pallas_call x5 -> x6, Pallas kernels: 70.9 us -> 61.3 us  [call(): pl.pallas_call(kernel, grid_spec=pltpu.PrefetchScalarGridSpec(num_scalar_...]
    ppermute x4, starting transfers between devices: 5.37 us -> 10.5 us  [doubling(): lax.ppermute(value, axis, [(i, i ^ step) for i in range(count)])]
    slice x2 -> x0, local copies, waits for them, and re-layouts: 2.4 us -> none  [sum_over(): other = other + tokens[index // 2][0, 0]]
  transfers between devices with their start and end apart: 7 -> 7, of which waited for: 4 -> 2; matrix products, arithmetic and copies ran while one was open for 6% -> 3% of each run, Pallas kernels for 55% -> 68%
where the time goes in v6:
time: 95.5 us; the launch traced here: 94.9 us
  Pallas kernels  64.4 us (67%)
  starting transfers between devices  16.8 us (18%)
  waiting for transfers between devices  5.66 us (6%)
  other arithmetic  4.25 us (4%)
  local copies, waits for them, and re-layouts  2.95 us (3%)
    pallas_call x6, Pallas kernels, call(): pl.pallas_call(kernel, grid_spec=pltpu.PrefetchScalarGridSpec(num_scalar_...  61.3 us
    ppermute x4, starting transfers between devices, doubling(): lax.ppermute(value, axis, [(i, i ^ step) for i in range(count)])  10.5 us
    ppermute x2, starting transfers between devices, passed_along(): lax.ppermute(value, axis, [(source, source + steps) for source in range(i...  6.19 us
    ppermute x2, waiting for transfers between devices, passed_along(): lax.ppermute(value, axis, [(source, source + steps) for source in range(i...  4.93 us
    pallas_call x1, Pallas kernels, reset_masks(): pl.pallas_call(functools.partial(reset_kernel, steps), out_shape=[jax.Sha...  3.11 us
  transfers between devices with their start and end apart: 7, of which 2 were waited for; matrix products, arithmetic and copies ran while one was open for 3% of the time, Pallas kernels for 68%

profile of v6, /device:TPU:0, one launch (start us, length us, event | category | flops | bytes accessed | tf_op | source)
XLA Modules:
  0.0 94.9 jit_solution(3226354401922431224)
XLA Ops:
  0.7 1.8 %multiply_convert_fusion = bf16[128,4096]{1,0:T(8,128)(2,1)S(1)} fusion(bf16[256,4096]{1,0:T(8,128)(2,1)} %v_ref.9, bf16[256,4096]{1,0:T(8,128)(2,1)} %k_ref.9), kind=kLoop, calls=%fused_computation | loop fusion | flops 2097152 | bytes 3145728 | tf_op jit(solution)/shard_map/convert_element_type | solution.py:112
  2.5 4.9 %collective-permute-start = (bf16[128,4096]{1,0:T(8,128)(2,1)S(1)}, bf16[128,4096]{1,0:T(8,128)(2,1)S(1)}, u32[]{:S(2)}, u32[]{:S(2)}) collective-permute-start(bf16[128,4096]{1,0:T(8,128)(2,1)S(1)} %multiply_convert_fusion), channel_id=1, source_target_pairs={{0,2},{2,4},{4,6},{6,8},{8,10},{10,12},{12,14},{14,16},{16,18},{18... | collective-permute-start | bytes 3145736 | tf_op jit(solution)/shard_map/ppermute | solution.py:420
  7.5 0.6 broadcast_in_dim.4.near_ref
  8.0 0.1 tile.10
  8.2 3.1 %resets.1 = (bf16[8,176,256]{2,1,0:T(8,128)(2,1)}, bf16[8,48,256]{2,1,0:T(8,128)(2,1)}, f32[8,48,256]{2,1,0:T(8,128)}, f32[8,16,256]{2,1,0:T(8,128)}, f32[8,16,2...) custom-call(s32[1,384]{1,0:T(1,128)} %broadcast_in_dim.4.near_ref), custom_call_target="tpu_custom_call" | custom-call | tf_op jit(solution)/shard_map/resets/pallas_call | solution.py:406
  11.3 13.4 %prepare.1 = (bf16[256,16,256]{2,1,0:T(8,128)(2,1)}, bf16[256,16,256]{2,1,0:T(8,128)(2,1)}, bf16[256,16,256]{2,1,0:T(8,128)(2,1)}, bf16[256,64,128]{2,1,0:T(8,12...) custom-call(s32[1]{0:T(128)} %bitcast.info, bf16[256,4096]{1,0:T(8,128)(2,1)} %q_ref.3, ...), custom_call_target="tpu_custom_call" | custom-call | flops 16777216 | bytes 1048576 | tf_op jit(solution)/shard_map/prepare/pallas_call | solution.py:301
  24.8 4.9 %collective-permute-done.rim_ref = bf16[128,4096]{1,0:T(8,128)(2,1)S(1)} collective-permute-done((bf16[128,4096]{1,0:T(8,128)(2,1)S(1)}, bf16[128,4096]{1,0:T(8,128)(2,1)S(1)}, u32[]{:S(2)}, u32[]{:S(2)}) %collective-permute-start) | collective-permute-done | bytes 1048608 | tf_op jit(solution)/shard_map/ppermute | solution.py:420
  29.7 1.3 %collective-permute-start.1 = (bf16[128,4096]{1,0:T(8,128)(2,1)}, bf16[128,4096]{1,0:T(8,128)(2,1)S(1)}, u32[]{:S(2)}, u32[]{:S(2)}) collective-permute-start(bf16[128,4096]{1,0:T(8,128)(2,1)} %get-tuple-element.65), channel_id=1, source_target_pairs={{2,0},{4,2},{6,4},{8,6},{10,8},{12,10},{14,12},{16,14},{18,16},{20... | collective-permute-start | bytes 3145736 | tf_op jit(solution)/shard_map/ppermute | solution.py:420
  31.0 0.8 copy.20.bias_ref
  31.8 22.7 %conv.1 = (bf16[256,4096]{1,0:T(8,128)(2,1)}, bf16[256,4096]{1,0:T(8,128)(2,1)}, f32[256,128]{1,0:T(8,128)}) custom-call(s32[1]{0:T(128)} %get-tuple-element.48.info, bf16[256,4096]{1,0:T(8,128)(2,1)} %q_ref.3, bf16[256,4096]{1,0:T(8,128)(2,1)} %ct_ref.3, bf16[256,16,256]{2,1,0:T(8,128)(2,1)} %get-tuple-element.50.x_ref, ...), custom_call_target="tpu_custom_call" | custom-call | flops 16777216 | bytes 1048576 | tf_op jit(solution)/shard_map/conv/pallas_call | solution.py:301
  54.6 0.9 pad_maximum_fusion.1
  55.5 3.2 %collective-permute-start.2 = (f32[288,128]{1,0:T(8,128)S(1)}, f32[288,128]{1,0:T(8,128)S(1)}, u32[]{:S(2)}, u32[]{:S(2)}) collective-permute-start(f32[288,128]{1,0:T(8,128)S(1)} %pad_maximum_fusion.1), channel_id=1, source_target_pairs={{0,2},{2,0},{4,6},{6,4},{8,10},{10,8},{12,14},{14,12},{16,18},{18,... | collective-permute-start | bytes 442376 | tf_op jit(solution)/shard_map/ppermute | solution.py:430
  58.7 1.0 %copy-done = bf16[128,4096]{1,0:T(8,128)(2,1)} copy-done((bf16[128,4096]{1,0:T(8,128)(2,1)}, bf16[128,4096]{1,0:T(8,128)(2,1)S(1)}, u32[]{:S(2)}) %copy-start) | copy-done | bytes 1048600
  59.7 6.3 %back.4 = (bf16[256,4096]{1,0:T(8,128)(2,1)}, bf16[256,4096]{1,0:T(8,128)(2,1)}, f32[8,128]{1,0:T(8,128)}) custom-call(s32[1]{0:T(128)} %get-tuple-element.48.info, bf16[256,4096]{1,0:T(8,128)(2,1)} %k_ref.9, bf16[256,4096]{1,0:T(8,128)(2,1)} %v_ref.9, bf16[256,16,256]{2,1,0:T(8,128)(2,1)} %get-tuple-element.63.dy_ref, ...), custom_call_target="tpu_custom_call" | custom-call | flops 16777216 | bytes 1048576 | tf_op jit(solution)/shard_map/back/pallas_call | solution.py:301
  66.0 3.0 %collective-permute-start.3 = (f32[288,128]{1,0:T(8,128)S(1)}, f32[288,128]{1,0:T(8,128)S(1)}, u32[]{:S(2)}, u32[]{:S(2)}) collective-permute-start(f32[288,128]{1,0:T(8,128)S(1)} %fusion.2), channel_id=1, source_target_pairs={{0,4},{2,6},{4,0},{6,2},{8,12},{10,14},{12,8},{14,10},{16,20},{18,... | collective-permute-start | bytes 442376 | tf_op jit(solution)/shard_map/ppermute | solution.py:430
  69.0 6.3 %back.5 = (bf16[256,4096]{1,0:T(8,128)(2,1)}, bf16[256,4096]{1,0:T(8,128)(2,1)}, f32[8,128]{1,0:T(8,128)}) custom-call(s32[1]{0:T(128)} %get-tuple-element.48.info, bf16[256,4096]{1,0:T(8,128)(2,1)} %k_ref.9, bf16[256,4096]{1,0:T(8,128)(2,1)} %v_ref.9, ...), custom_call_target="tpu_custom_call", output_to_operand_aliasing={{0}: (10, {}), {1}: (11, {})} | custom-call | flops 16777216 | bytes 1048576 | tf_op jit(solution)/shard_map/back/pallas_call | solution.py:301
  75.3 1.6 %collective-permute-start.4 = (f32[288,128]{1,0:T(8,128)S(1)}, f32[288,128]{1,0:T(8,128)S(1)}, u32[]{:S(2)}, u32[]{:S(2)}) collective-permute-start(f32[288,128]{1,0:T(8,128)S(1)} %add.19), channel_id=1, source_target_pairs={{0,8},{2,10},{4,12},{6,14},{8,0},{10,2},{12,4},{14,6},{16,24},{18,... | collective-permute-start | bytes 442376 | tf_op jit(solution)/shard_map/ppermute | solution.py:430
  77.0 6.3 %back.6 = (bf16[256,4096]{1,0:T(8,128)(2,1)}, bf16[256,4096]{1,0:T(8,128)(2,1)}, f32[8,128]{1,0:T(8,128)}) custom-call(s32[1]{0:T(128)} %get-tuple-element.48.info, bf16[256,4096]{1,0:T(8,128)(2,1)} %k_ref.9, bf16[256,4096]{1,0:T(8,128)(2,1)} %v_ref.9, ...), custom_call_target="tpu_custom_call", output_to_operand_aliasing={{0}: (10, {}), {1}: (11, {})} | custom-call | flops 16777216 | bytes 1048576 | tf_op jit(solution)/shard_map/back/pallas_call | solution.py:301
  83.3 2.7 %collective-permute-start.5 = (f32[288,128]{1,0:T(8,128)S(1)}, f32[288,128]{1,0:T(8,128)S(1)}, u32[]{:S(2)}, u32[]{:S(2)}) collective-permute-start(f32[288,128]{1,0:T(8,128)S(1)} %add.20), channel_id=1, source_target_pairs={{0,16},{2,18},{4,20},{6,22},{8,24},{10,26},{12,28},{14,30},{16,0},... | collective-permute-start | bytes 442376 | tf_op jit(solution)/shard_map/ppermute | solution.py:430
  86.0 6.3 %back.7 = (bf16[256,4096]{1,0:T(8,128)(2,1)}, bf16[256,4096]{1,0:T(8,128)(2,1)}, f32[8,128]{1,0:T(8,128)}) custom-call(s32[1]{0:T(128)} %get-tuple-element.48.info, bf16[256,4096]{1,0:T(8,128)(2,1)} %k_ref.9, bf16[256,4096]{1,0:T(8,128)(2,1)} %v_ref.9, ...), custom_call_target="tpu_custom_call", output_to_operand_aliasing={{0}: (10, {}), {1}: (11, {})} | custom-call | flops 16777216 | bytes 1048576 | tf_op jit(solution)/shard_map/back/pallas_call | solution.py:301
  92.4 0.6 fusion
  93.0 0.7 collective-permute-done.6
  93.8 0.4 rev.3
  94.1 0.7 broadcast_multiply_fusion
  (27 shorter events, 0.4 us)
Async XLA Ops:
  0.6 6.8 %copy-start.5 = (s32[4096]{0:T(1024)S(1)}, s32[4096]{0:T(1024)}, u32[]{:S(2)}) copy-start(s32[4096]{0:T(1024)} %param.13) | copy-start | bytes 49156
  0.6 7.4 %copy-start.4 = (f32[4096]{0:T(1024)S(1)}, f32[4096]{0:T(1024)}, u32[]{:S(2)}) copy-start(f32[4096]{0:T(1024)} %param.12) | copy-start | bytes 49156
  2.5 27.2 %collective-permute-start = (bf16[128,4096]{1,0:T(8,128)(2,1)S(1)}, bf16[128,4096]{1,0:T(8,128)(2,1)S(1)}, u32[]{:S(2)}, u32[]{:S(2)}) collective-permute-start(bf16[128,4096]{1,0:T(8,128)(2,1)S(1)} %multiply_convert_fusion), channel_id=1, source_target_pairs={{0,2},{2,4},{4,6},{6,8},{8,10},{10,12},{12,14},{14,16},{16,18},{18... | collective-permute-start | bytes 3145736 | tf_op jit(solution)/shard_map/ppermute | solution.py:420
  29.7 2.1 %copy-start.1 = (bf16[128,4096]{1,0:T(8,128)(2,1)}, bf16[128,4096]{1,0:T(8,128)(2,1)S(1)}, u32[]{:S(2)}) copy-start(bf16[128,4096]{1,0:T(8,128)(2,1)S(1)} %collective-permute-done.rim_ref) | copy-start | bytes 3145732
  29.7 29.0 %collective-permute-start.1 = (bf16[128,4096]{1,0:T(8,128)(2,1)}, bf16[128,4096]{1,0:T(8,128)(2,1)S(1)}, u32[]{:S(2)}, u32[]{:S(2)}) collective-permute-start(bf16[128,4096]{1,0:T(8,128)(2,1)} %get-tuple-element.65), channel_id=1, source_target_pairs={{2,0},{4,2},{6,4},{8,6},{10,8},{12,10},{14,12},{16,14},{18,16},{20... | collective-permute-start | bytes 3145736 | tf_op jit(solution)/shard_map/ppermute | solution.py:420
  31.8 22.7 %copy-start.3 = (f32[1,4096]{1,0:T(1,128)S(1)}, f32[1,4096]{1,0:T(1,128)}, u32[]{:S(2)}) copy-start(f32[1,4096]{1,0:T(1,128)} %get-tuple-element.72) | copy-start | bytes 49156
  55.5 10.5 %collective-permute-start.2 = (f32[288,128]{1,0:T(8,128)S(1)}, f32[288,128]{1,0:T(8,128)S(1)}, u32[]{:S(2)}, u32[]{:S(2)}) collective-permute-start(f32[288,128]{1,0:T(8,128)S(1)} %pad_maximum_fusion.1), channel_id=1, source_target_pairs={{0,2},{2,0},{4,6},{6,4},{8,10},{10,8},{12,14},{14,12},{16,18},{18,... | collective-permute-start | bytes 442376 | tf_op jit(solution)/shard_map/ppermute | solution.py:430
  58.7 1.0 %copy-start = (bf16[128,4096]{1,0:T(8,128)(2,1)}, bf16[128,4096]{1,0:T(8,128)(2,1)S(1)}, u32[]{:S(2)}) copy-start(bf16[128,4096]{1,0:T(8,128)(2,1)S(1)} %collective-permute-done.1.rim_ref) | copy-start | bytes 3145732
  59.7 6.3 %copy-start.2 = (f32[256,128]{1,0:T(8,128)S(1)}, f32[256,128]{1,0:T(8,128)}, u32[]{:S(2)}) copy-start(f32[256,128]{1,0:T(8,128)} %get-tuple-element.71) | copy-start | bytes 393220
  66.0 9.3 %collective-permute-start.3 = (f32[288,128]{1,0:T(8,128)S(1)}, f32[288,128]{1,0:T(8,128)S(1)}, u32[]{:S(2)}, u32[]{:S(2)}) collective-permute-start(f32[288,128]{1,0:T(8,128)S(1)} %fusion.2), channel_id=1, source_target_pairs={{0,4},{2,6},{4,0},{6,2},{8,12},{10,14},{12,8},{14,10},{16,20},{18,... | collective-permute-start | bytes 442376 | tf_op jit(solution)/shard_map/ppermute | solution.py:430
  75.3 7.9 %collective-permute-start.4 = (f32[288,128]{1,0:T(8,128)S(1)}, f32[288,128]{1,0:T(8,128)S(1)}, u32[]{:S(2)}, u32[]{:S(2)}) collective-permute-start(f32[288,128]{1,0:T(8,128)S(1)} %add.19), channel_id=1, source_target_pairs={{0,8},{2,10},{4,12},{6,14},{8,0},{10,2},{12,4},{14,6},{16,24},{18,... | collective-permute-start | bytes 442376 | tf_op jit(solution)/shard_map/ppermute | solution.py:430
  83.3 9.0 %collective-permute-start.5 = (f32[288,128]{1,0:T(8,128)S(1)}, f32[288,128]{1,0:T(8,128)S(1)}, u32[]{:S(2)}, u32[]{:S(2)}) collective-permute-start(f32[288,128]{1,0:T(8,128)S(1)} %add.20), channel_id=1, source_target_pairs={{0,16},{2,18},{4,20},{6,22},{8,24},{10,26},{12,28},{14,30},{16,0},... | collective-permute-start | bytes 442376 | tf_op jit(solution)/shard_map/ppermute | solution.py:430
  92.3 1.4 %collective-permute-start.6 = (f32[256,128]{1,0:T(8,128)S(1)}, f32[256,128]{1,0:T(8,128)S(1)}, u32[]{:S(2)}, u32[]{:S(2)}) collective-permute-start(f32[256,128]{1,0:T(8,128)S(1)} %slice.16), channel_id=1, source_target_pairs={{0,1},{1,0},{2,3},{3,2},{4,5},{5,4},{6,7},{7,6},{8,9},{9,8},{10,11... | collective-permute-start | bytes 393224 | tf_op jit(solution)/shard_map/ppermute | solution.py:441

commit v7 on v6

--- a/solution.py
+++ b/solution.py
@@ -13,7 +13,7 @@
 TB = 16
 WIDE = 256
 KINDS = 3
-BACK_PARTS = 4
+BACK_PARTS = 2
 VMEM_BYTES = 60 * 1024 * 1024
 TOGETHER = 2
 
@@ -127,9 +127,9 @@
     return pltpu.roll(base, first, 1, stride=1, stride_axis=0).astype(BF16)
 
 
-def chosen(products, sel_ref, g):
+def chosen(products, sel_ref, g, kinds):
     return sum(
-        products[kind * TB : (kind + 1) * TB] * sel_ref[g, kind * TB : (kind + 1) * TB, :] for kind in range(KINDS)
+        products[kind * TB : (kind + 1) * TB] * sel_ref[g, kind * TB : (kind + 1) * TB, :] for kind in range(kinds)
     )
 
 
@@ -140,9 +140,9 @@
     return jnp.concatenate([taps[:, :LANES], taps[:, LANES:]] + further, axis=0)
 
 
-def band_of(stored):
-    none = jnp.zeros(((KINDS - 1) * TB, LANES), BF16)
-    return jnp.concatenate([jnp.concatenate([stored[:TB], none], axis=0), stored[TB:]], axis=1)
+def band_of(stored, kinds):
+    none = jnp.zeros(((kinds - 1) * TB, LANES), BF16)
+    return jnp.concatenate([jnp.concatenate([stored[:TB], none], axis=0), stored[TB : (1 + kinds) * TB]], axis=1)
 
 
 def prepare_kernel(chunk, info, q_ref, ct_ref, k_ref, v_ref, taps_ref, x_ref, dy_ref, turned_ref, bx_ref, bdy_ref, gb_ref, head_ref):
@@ -177,9 +177,9 @@
     width = q_ref.shape[1]
     per = LANES // chunk
     steps = filter_size // TB
-    depth = (steps + KINDS) * TB
-
-    def one(sub, slot, further):
+
+    def one(sub, slot, kinds, further):
+        depth = (steps + kinds) * TB
         lanes = pl.ds(pl.multiple_of(sub * LANES, LANES), LANES)
         bits, bits32 = chunk_bits(BF16, chunk), chunk_bits(F32, chunk)
         late, lane = TB - 1 - iota((TB, LANES), 0), iota((TB, LANES), 1)
@@ -189,18 +189,18 @@
             at = sub * per + g
             xg = x_ref[at]
             ext = rims[g] + [xg[:, i : i + LANES] for i in range(0, xg.shape[1], LANES)]
-            window = past_windows(ext, place_of(g, chunk), chunk, steps) + [xg] * (KINDS - 1)
-            window = jnp.concatenate(window, axis=0) * mask_ref[g]
-            y = jnp.dot(band_of(taps_ref[at])[:, :depth], window, preferred_element_type=F32)
-            conv_s[slot, g] = chosen(y, sel_ref, g) + bias_ref[pl.ds(at, 1), :] * xg.astype(F32)
-            turned = jnp.concatenate([turned_ref[at]] * KINDS, axis=0) * turned_mask_ref[g]
+            window = past_windows(ext, place_of(g, chunk), chunk, steps) + [xg] * (kinds - 1)
+            window = jnp.concatenate(window, axis=0) * mask_ref[g, :depth, :]
+            y = jnp.dot(band_of(taps_ref[at], kinds)[:, :depth], window, preferred_element_type=F32)
+            conv_s[slot, g] = chosen(y, sel_ref, g, kinds) + bias_ref[pl.ds(at, 1), :] * xg.astype(F32)
+            turned = jnp.concatenate([turned_ref[at]] * kinds, axis=0) * turned_mask_ref[g, (KINDS - kinds) * TB :, :]
             pairs = lax.dot_general(turned, window, (((1,), (1,)), ((), ())), preferred_element_type=F32)
-            pairs = jnp.concatenate([pairs, jnp.zeros((KINDS * TB, WIDE - depth), F32)], axis=1)
-            far = pairs[(KINDS - 1) * TB :, :LANES]
+            pairs = jnp.concatenate([pairs, jnp.zeros((kinds * TB, WIDE - depth), F32)], axis=1)
+            far = pairs[(kinds - 1) * TB :, :LANES]
             grad_s[slot, 0, g : g + 1, :] = skew_left(jnp.where(lane > late, far, 0.0))
             own = jnp.zeros((TB, LANES), F32)
-            for kind in range(KINDS):
-                first = (KINDS - 1 - kind) * TB
+            for kind in range(kinds):
+                first = (kinds - 1 - kind) * TB
                 own = jnp.where(causal & (lane // TB == kind), pairs[first : first + TB, LANES:], own)
             grad_s[slot, 1, g : g + 1, :] = skew_left(own)
 
@@ -222,7 +222,7 @@
             lax.fori_loop(KINDS * per, info[0] * per, more, 0)
         terms, own = grad_s[slot, 0], grad_s[slot, 1]
         last = iota((per, LANES), 1) >= LANES - TB
-        for kind in range(KINDS):
+        for kind in range(kinds):
             shift = (LANES - kind * TB) % LANES
             terms += jnp.where(last, pltpu.roll(own, shift, 1) if shift else own, 0.0)
         gf_ref[pl.ds(pl.multiple_of(sub * per, per), per), :] = terms
@@ -240,9 +240,9 @@
     width = k_ref.shape[1]
     per = LANES // chunk
     steps = filter_size // TB
-    depth = (steps + KINDS) * TB
-
-    def one(sub, slot, further):
+
+    def one(sub, slot, kinds, further):
+        depth = (steps + kinds) * TB
         lanes = pl.ds(pl.multiple_of(sub * LANES, LANES), LANES)
         bits, bits32 = chunk_bits(BF16, chunk), chunk_bits(F32, chunk)
         rims = to_groups(rim_ref[:, lanes], bits, chunk)
@@ -250,10 +250,10 @@
             at = sub * per + g
             dyg = dy_ref[at]
             ext = [dyg[:, i : i + LANES] for i in range(0, dyg.shape[1], LANES)] + rims[g]
-            window = next_windows(ext, place_of(g, chunk), chunk, steps) + [dyg] * (KINDS - 1)
-            window = jnp.concatenate(window, axis=0) * mask_ref[g]
-            y = jnp.dot(band_of(taps_ref[at])[:, :depth], window, preferred_element_type=F32)
-            back_s[slot, g] = chosen(y, sel_ref, g) + bias_ref[pl.ds(at, 1), :] * dyg.astype(F32)
+            window = next_windows(ext, place_of(g, chunk), chunk, steps) + [dyg] * (kinds - 1)
+            window = jnp.concatenate(window, axis=0) * mask_ref[g, :depth, :]
+            y = jnp.dot(band_of(taps_ref[at], kinds)[:, :depth], window, preferred_element_type=F32)
+            back_s[slot, g] = chosen(y, sel_ref, g, kinds) + bias_ref[pl.ds(at, 1), :] * dyg.astype(F32)
 
         def more(index, carry):
             level, g = index // per, index % per
@@ -276,16 +276,17 @@
 def for_all_lanes(one, count, info):
     together = math.gcd(count, TOGETHER)
 
-    def run(further):
+    def run(kinds, further):
         def step(index, carry):
             for slot in range(together):
-                one(index * together + slot, slot, further)
+                one(index * together + slot, slot, kinds, further)
             return carry
 
         lax.fori_loop(0, count // together, step, 0)
 
-    pl.when(info[0] <= KINDS)(lambda: run(False))
-    pl.when(info[0] > KINDS)(lambda: run(True))
+    pl.when(info[0] < KINDS)(lambda: run(KINDS - 1, False))
+    pl.when(info[0] == KINDS)(lambda: run(KINDS, False))
+    pl.when(info[0] > KINDS)(lambda: run(KINDS, True))
 
 
 def call(kernel, name, info, count, ins, outs, scratch=(), previous=None, after=()):
@@ -420,18 +421,23 @@
     return lax.ppermute(value, axis, [(source, source + steps) for source in range(initial, last)])
 
 
-def doubling(value, axis):
+def rounds_of_sum(value, axis):
     count = lax.axis_size(axis)
     if count & (count - 1):
-        yield [value, lax.psum(value, axis)]
+        yield [[value], lax.psum(value, axis)]
         return
     step = 1
     while step < count:
-        state = [lax.ppermute(value, axis, [(i, i ^ step) for i in range(count)]), value]
+        flips = [step] if 2 * step == count else [step, 2 * step, 3 * step]
+        state = [[lax.ppermute(value, axis, [(i, i ^ flip) for i in range(count)]) for flip in flips], value]
         yield state
-        value = state[1] = state[0] + value
-        step *= 2
-    yield [value, value]
+        near, *far = state[0]
+        value = value + near
+        if far:
+            value = value + (far[0] + far[1])
+        state[1] = value
+        step <<= len(flips).bit_length()
+    yield [[value], value]
 
 
 def rows_of_all(value, axis):
@@ -475,7 +481,7 @@
     terms = jnp.concatenate([filter_part, bias_part.reshape(channels // filter_size, filter_size)], axis=0)
 
     pair, grouped = (key_branch, value_branch), (dy, band_dy, bias)
-    sums = doubling(terms, "ctx")
+    sums = rounds_of_sum(terms, "ctx")
     done, after, state = None, (), None
     for part in range(BACK_PARTS):
         arriving = next(sums, None)
@@ -484,7 +490,7 @@
             back_kernel, "back", part, BACK_PARTS, kinds, pair, grouped, right, part, masks_dy, filter_size, False, done, after
         )
         if arriving is not None:
-            arriving[0], token = lax.optimization_barrier((arriving[0], token))
+            *arriving[0], token = lax.optimization_barrier((*arriving[0], token))
         after = (token,)
     grad_key, grad_value = done
     for state in sums:

time: 95.5 us -> 89.9 us (0.941)
  Pallas kernels: 64.4 us -> 56.7 us
  starting transfers between devices: 16.8 us -> 18.1 us
    pallas_call x6 -> x4, Pallas kernels: 61.3 us -> 53.6 us  [call(): pl.pallas_call(kernel, grid_spec=pltpu.PrefetchScalarGridSpec(num_scalar_...]
    ppermute x4 -> x6, starting transfers between devices: 10.5 us -> 11.8 us  [rounds_of_sum(): lax.ppermute(value, axis, [(i, i ^ flip) for i in range(count)])]
  transfers between devices with their start and end apart: 7 -> 9, of which waited for: 2 -> 3; matrix products, arithmetic and copies ran while one was open for 3% -> 4% of each run, Pallas kernels for 68% -> 64%
where the time goes in v7:
time: 89.9 us; the launch traced here: 89.1 us
  Pallas kernels  56.7 us (63%)
  starting transfers between devices  18.1 us (20%)
  waiting for transfers between devices  6.35 us (7%)
  other arithmetic  4.24 us (5%)
  local copies, waits for them, and re-layouts  2.95 us (3%)
    pallas_call x4, Pallas kernels, call(): pl.pallas_call(kernel, grid_spec=pltpu.PrefetchScalarGridSpec(num_scalar_...  53.6 us
    ppermute x6, starting transfers between devices, rounds_of_sum(): lax.ppermute(value, axis, [(i, i ^ flip) for i in range(count)])  11.8 us
    ppermute x2, starting transfers between devices, passed_along(): lax.ppermute(value, axis, [(source, source + steps) for source in range(i...  6.19 us
    ppermute x2, waiting for transfers between devices, passed_along(): lax.ppermute(value, axis, [(source, source + steps) for source in range(i...  4.93 us
    pallas_call x1, Pallas kernels, reset_masks(): pl.pallas_call(functools.partial(reset_kernel, steps), out_shape=[jax.Sha...  3.11 us
  transfers between devices with their start and end apart: 9, of which 3 were waited for; matrix products, arithmetic and copies ran while one was open for 4% of the time, Pallas kernels for 64%

profile of v7, /device:TPU:0, one launch (start us, length us, event | category | flops | bytes accessed | tf_op | source)
XLA Modules:
  0.0 89.1 jit_solution(8629795948926275741)
XLA Ops:
  0.7 1.8 %multiply_convert_fusion = bf16[128,4096]{1,0:T(8,128)(2,1)S(1)} fusion(bf16[256,4096]{1,0:T(8,128)(2,1)} %v_ref.5, bf16[256,4096]{1,0:T(8,128)(2,1)} %k_ref.5), kind=kLoop, calls=%fused_computation | loop fusion | flops 2097152 | bytes 3145728 | tf_op jit(solution)/shard_map/convert_element_type | solution.py:112
  2.5 4.9 %collective-permute-start = (bf16[128,4096]{1,0:T(8,128)(2,1)S(1)}, bf16[128,4096]{1,0:T(8,128)(2,1)S(1)}, u32[]{:S(2)}, u32[]{:S(2)}) collective-permute-start(bf16[128,4096]{1,0:T(8,128)(2,1)S(1)} %multiply_convert_fusion), channel_id=1, source_target_pairs={{0,2},{2,4},{4,6},{6,8},{8,10},{10,12},{12,14},{14,16},{16,18},{18... | collective-permute-start | bytes 3145736 | tf_op jit(solution)/shard_map/ppermute | solution.py:421
  7.4 0.1 fusion.1
  7.5 0.6 broadcast_in_dim.4.near_ref
  8.0 0.1 tile.10
  8.2 3.1 %resets.1 = (bf16[8,176,256]{2,1,0:T(8,128)(2,1)}, bf16[8,48,256]{2,1,0:T(8,128)(2,1)}, f32[8,48,256]{2,1,0:T(8,128)}, f32[8,16,256]{2,1,0:T(8,128)}, f32[8,16,2...) custom-call(s32[1,384]{1,0:T(1,128)} %broadcast_in_dim.4.near_ref), custom_call_target="tpu_custom_call" | custom-call | tf_op jit(solution)/shard_map/resets/pallas_call | solution.py:407
  11.3 13.4 %prepare.1 = (bf16[256,16,256]{2,1,0:T(8,128)(2,1)}, bf16[256,16,256]{2,1,0:T(8,128)(2,1)}, bf16[256,16,256]{2,1,0:T(8,128)(2,1)}, bf16[256,64,128]{2,1,0:T(8,12...) custom-call(s32[1]{0:T(128)} %bitcast.info, bf16[256,4096]{1,0:T(8,128)(2,1)} %q_ref.3, ...), custom_call_target="tpu_custom_call" | custom-call | flops 16777216 | bytes 1048576 | tf_op jit(solution)/shard_map/prepare/pallas_call | solution.py:302
  24.8 4.9 %collective-permute-done.rim_ref = bf16[128,4096]{1,0:T(8,128)(2,1)S(1)} collective-permute-done((bf16[128,4096]{1,0:T(8,128)(2,1)S(1)}, bf16[128,4096]{1,0:T(8,128)(2,1)S(1)}, u32[]{:S(2)}, u32[]{:S(2)}) %collective-permute-start) | collective-permute-done | bytes 1048608 | tf_op jit(solution)/shard_map/ppermute | solution.py:421
  29.7 1.3 %collective-permute-start.1 = (bf16[128,4096]{1,0:T(8,128)(2,1)}, bf16[128,4096]{1,0:T(8,128)(2,1)S(1)}, u32[]{:S(2)}, u32[]{:S(2)}) collective-permute-start(bf16[128,4096]{1,0:T(8,128)(2,1)} %get-tuple-element.60), channel_id=1, source_target_pairs={{2,0},{4,2},{6,4},{8,6},{10,8},{12,10},{14,12},{16,14},{18,16},{20... | collective-permute-start | bytes 3145736 | tf_op jit(solution)/shard_map/ppermute | solution.py:421
  31.0 0.8 copy.16.bias_ref
  31.8 21.8 %conv.1 = (bf16[256,4096]{1,0:T(8,128)(2,1)}, bf16[256,4096]{1,0:T(8,128)(2,1)}, f32[256,128]{1,0:T(8,128)}) custom-call(s32[1]{0:T(128)} %get-tuple-element.43.info, bf16[256,4096]{1,0:T(8,128)(2,1)} %q_ref.3, bf16[256,4096]{1,0:T(8,128)(2,1)} %ct_ref.3, bf16[256,16,256]{2,1,0:T(8,128)(2,1)} %get-tuple-element.45.x_ref, ...), custom_call_target="tpu_custom_call" | custom-call | flops 16777216 | bytes 1048576 | tf_op jit(solution)/shard_map/conv/pallas_call | solution.py:302
  53.7 0.9 %pad_maximum_fusion.1 = f32[288,128]{1,0:T(8,128)S(1)} fusion(f32[32,128]{1,0:T(8,128)S(1)} %bitcast.6, f32[256,128]{1,0:T(8,128)} %get-tuple-element.66), kind=kLoop, calls=%fused_computation.2 | loop fusion | flops 36864 | bytes 294912 | tf_op jit(solution)/shard_map/concatenate | solution.py:481
  54.6 5.6 %collective-permute-start.4 = (f32[288,128]{1,0:T(8,128)S(1)}, f32[288,128]{1,0:T(8,128)S(1)}, u32[]{:S(2)}, u32[]{:S(2)}) collective-permute-start(f32[288,128]{1,0:T(8,128)S(1)} %pad_maximum_fusion.1), channel_id=1, source_target_pairs={{0,6},{2,4},{4,2},{6,0},{8,14},{10,12},{12,10},{14,8},{16,22},{18,... | collective-permute-start | bytes 442376 | tf_op jit(solution)/shard_map/ppermute | solution.py:432
  60.2 0.6 collective-permute-start.2
  60.8 1.0 %copy-done = bf16[128,4096]{1,0:T(8,128)(2,1)} copy-done((bf16[128,4096]{1,0:T(8,128)(2,1)}, bf16[128,4096]{1,0:T(8,128)(2,1)S(1)}, u32[]{:S(2)}) %copy-start) | copy-done | bytes 1048600
  61.8 9.2 %back.2 = (bf16[256,4096]{1,0:T(8,128)(2,1)}, bf16[256,4096]{1,0:T(8,128)(2,1)}, f32[8,128]{1,0:T(8,128)}) custom-call(s32[1]{0:T(128)} %get-tuple-element.43.info, bf16[256,4096]{1,0:T(8,128)(2,1)} %k_ref.5, bf16[256,4096]{1,0:T(8,128)(2,1)} %v_ref.5, bf16[256,16,256]{2,1,0:T(8,128)(2,1)} %get-tuple-element.58.dy_ref, ...), custom_call_target="tpu_custom_call" | custom-call | flops 16777216 | bytes 1048576 | tf_op jit(solution)/shard_map/back/pallas_call | solution.py:302
  71.1 5.0 %collective-permute-start.7 = (f32[288,128]{1,0:T(8,128)S(1)}, f32[288,128]{1,0:T(8,128)S(1)}, u32[]{:S(2)}, u32[]{:S(2)}) collective-permute-start(f32[288,128]{1,0:T(8,128)S(1)} %add_add_fusion.1), channel_id=1, source_target_pairs={{0,24},{2,26},{4,28},{6,30},{8,16},{10,18},{12,20},{14,22},{16,8},... | collective-permute-start | bytes 442376 | tf_op jit(solution)/shard_map/ppermute | solution.py:432
  76.0 0.6 collective-permute-start.5
  76.7 9.1 %back.3 = (bf16[256,4096]{1,0:T(8,128)(2,1)}, bf16[256,4096]{1,0:T(8,128)(2,1)}, f32[8,128]{1,0:T(8,128)}) custom-call(s32[1]{0:T(128)} %get-tuple-element.43.info, bf16[256,4096]{1,0:T(8,128)(2,1)} %k_ref.5, bf16[256,4096]{1,0:T(8,128)(2,1)} %v_ref.5, ...), custom_call_target="tpu_custom_call", output_to_operand_aliasing={{0}: (10, {}), {1}: (11, {})} | custom-call | flops 16777216 | bytes 1048576 | tf_op jit(solution)/shard_map/back/pallas_call | solution.py:302
  85.8 0.7 collective-permute-done.6
  86.7 0.6 fusion
  87.3 0.7 collective-permute-done.8
  88.0 0.4 rev.3
  88.4 0.7 broadcast_multiply_fusion
  (27 shorter events, 0.3 us)
Async XLA Ops:
  0.6 6.8 %copy-start.5 = (s32[4096]{0:T(1024)S(1)}, s32[4096]{0:T(1024)}, u32[]{:S(2)}) copy-start(s32[4096]{0:T(1024)} %param.13) | copy-start | bytes 49156
  0.6 7.4 %copy-start.4 = (f32[4096]{0:T(1024)S(1)}, f32[4096]{0:T(1024)}, u32[]{:S(2)}) copy-start(f32[4096]{0:T(1024)} %param.12) | copy-start | bytes 49156
  2.5 27.2 %collective-permute-start = (bf16[128,4096]{1,0:T(8,128)(2,1)S(1)}, bf16[128,4096]{1,0:T(8,128)(2,1)S(1)}, u32[]{:S(2)}, u32[]{:S(2)}) collective-permute-start(bf16[128,4096]{1,0:T(8,128)(2,1)S(1)} %multiply_convert_fusion), channel_id=1, source_target_pairs={{0,2},{2,4},{4,6},{6,8},{8,10},{10,12},{12,14},{14,16},{16,18},{18... | collective-permute-start | bytes 3145736 | tf_op jit(solution)/shard_map/ppermute | solution.py:421
  29.7 2.1 %copy-start.1 = (bf16[128,4096]{1,0:T(8,128)(2,1)}, bf16[128,4096]{1,0:T(8,128)(2,1)S(1)}, u32[]{:S(2)}) copy-start(bf16[128,4096]{1,0:T(8,128)(2,1)S(1)} %collective-permute-done.rim_ref) | copy-start | bytes 3145732
  29.7 31.1 %collective-permute-start.1 = (bf16[128,4096]{1,0:T(8,128)(2,1)}, bf16[128,4096]{1,0:T(8,128)(2,1)S(1)}, u32[]{:S(2)}, u32[]{:S(2)}) collective-permute-start(bf16[128,4096]{1,0:T(8,128)(2,1)} %get-tuple-element.60), channel_id=1, source_target_pairs={{2,0},{4,2},{6,4},{8,6},{10,8},{12,10},{14,12},{16,14},{18,16},{20... | collective-permute-start | bytes 3145736 | tf_op jit(solution)/shard_map/ppermute | solution.py:421
  31.8 21.9 %copy-start.3 = (f32[1,4096]{1,0:T(1,128)S(1)}, f32[1,4096]{1,0:T(1,128)}, u32[]{:S(2)}) copy-start(f32[1,4096]{1,0:T(1,128)} %get-tuple-element.67) | copy-start | bytes 49156
  54.6 16.4 %collective-permute-start.4 = (f32[288,128]{1,0:T(8,128)S(1)}, f32[288,128]{1,0:T(8,128)S(1)}, u32[]{:S(2)}, u32[]{:S(2)}) collective-permute-start(f32[288,128]{1,0:T(8,128)S(1)} %pad_maximum_fusion.1), channel_id=1, source_target_pairs={{0,6},{2,4},{4,2},{6,0},{8,14},{10,12},{12,10},{14,8},{16,22},{18,... | collective-permute-start | bytes 442376 | tf_op jit(solution)/shard_map/ppermute | solution.py:432
  60.2 10.8 %collective-permute-start.3 = (f32[288,128]{1,0:T(8,128)S(1)}, f32[288,128]{1,0:T(8,128)S(1)}, u32[]{:S(2)}, u32[]{:S(2)}) collective-permute-start(f32[288,128]{1,0:T(8,128)S(1)} %pad_maximum_fusion.1), channel_id=1, source_target_pairs={{0,4},{2,6},{4,0},{6,2},{8,12},{10,14},{12,8},{14,10},{16,20},{18,... | collective-permute-start | bytes 442376 | tf_op jit(solution)/shard_map/ppermute | solution.py:432
  60.2 10.8 %collective-permute-start.2 = (f32[288,128]{1,0:T(8,128)S(1)}, f32[288,128]{1,0:T(8,128)S(1)}, u32[]{:S(2)}, u32[]{:S(2)}) collective-permute-start(f32[288,128]{1,0:T(8,128)S(1)} %pad_maximum_fusion.1), channel_id=1, source_target_pairs={{0,2},{2,0},{4,6},{6,4},{8,10},{10,8},{12,14},{14,12},{16,18},{18,... | collective-permute-start | bytes 442376 | tf_op jit(solution)/shard_map/ppermute | solution.py:432
  60.8 1.0 %copy-start = (bf16[128,4096]{1,0:T(8,128)(2,1)}, bf16[128,4096]{1,0:T(8,128)(2,1)S(1)}, u32[]{:S(2)}) copy-start(bf16[128,4096]{1,0:T(8,128)(2,1)S(1)} %collective-permute-done.1.rim_ref) | copy-start | bytes 3145732
  61.8 9.2 %copy-start.2 = (f32[256,128]{1,0:T(8,128)S(1)}, f32[256,128]{1,0:T(8,128)}, u32[]{:S(2)}) copy-start(f32[256,128]{1,0:T(8,128)} %get-tuple-element.66) | copy-start | bytes 393220
  71.1 14.8 %collective-permute-start.7 = (f32[288,128]{1,0:T(8,128)S(1)}, f32[288,128]{1,0:T(8,128)S(1)}, u32[]{:S(2)}, u32[]{:S(2)}) collective-permute-start(f32[288,128]{1,0:T(8,128)S(1)} %add_add_fusion.1), channel_id=1, source_target_pairs={{0,24},{2,26},{4,28},{6,30},{8,16},{10,18},{12,20},{14,22},{16,8},... | collective-permute-start | bytes 442376 | tf_op jit(solution)/shard_map/ppermute | solution.py:432
  76.0 10.5 %collective-permute-start.6 = (f32[288,128]{1,0:T(8,128)S(1)}, f32[288,128]{1,0:T(8,128)S(1)}, u32[]{:S(2)}, u32[]{:S(2)}) collective-permute-start(f32[288,128]{1,0:T(8,128)S(1)} %add_add_fusion.1), channel_id=1, source_target_pairs={{0,16},{2,18},{4,20},{6,22},{8,24},{10,26},{12,28},{14,30},{16,0},... | collective-permute-start | bytes 442376 | tf_op jit(solution)/shard_map/ppermute | solution.py:432
  76.0 10.5 %collective-permute-start.5 = (f32[288,128]{1,0:T(8,128)S(1)}, f32[288,128]{1,0:T(8,128)S(1)}, u32[]{:S(2)}, u32[]{:S(2)}) collective-permute-start(f32[288,128]{1,0:T(8,128)S(1)} %add_add_fusion.1), channel_id=1, source_target_pairs={{0,8},{2,10},{4,12},{6,14},{8,0},{10,2},{12,4},{14,6},{16,24},{18,... | collective-permute-start | bytes 442376 | tf_op jit(solution)/shard_map/ppermute | solution.py:432
  86.6 1.4 %collective-permute-start.8 = (f32[256,128]{1,0:T(8,128)S(1)}, f32[256,128]{1,0:T(8,128)S(1)}, u32[]{:S(2)}, u32[]{:S(2)}) collective-permute-start(f32[256,128]{1,0:T(8,128)S(1)} %slice.16), channel_id=1, source_target_pairs={{0,1},{1,0},{2,3},{3,2},{4,5},{5,4},{6,7},{7,6},{8,9},{9,8},{10,11... | collective-permute-start | bytes 393224 | tf_op jit(solution)/shard_map/ppermute | solution.py:447

commit v8 on v7

--- a/solution.py
+++ b/solution.py
@@ -15,7 +15,7 @@
 KINDS = 3
 BACK_PARTS = 2
 VMEM_BYTES = 60 * 1024 * 1024
-TOGETHER = 2
+TOGETHER = 4
 
 
 def iota(shape, axis):

time: 89.9 us -> 86 us (0.957)
  Pallas kernels: 56.7 us -> 52 us
  starting transfers between devices: 18.1 us -> 19.7 us
    pallas_call x4, Pallas kernels: 53.6 us -> 48.8 us  [call(): pl.pallas_call(kernel, grid_spec=pltpu.PrefetchScalarGridSpec(num_scalar_...]
    ppermute x6, starting transfers between devices: 11.8 us -> 13.2 us  [rounds_of_sum(): lax.ppermute(value, axis, [(i, i ^ flip) for i in range(count)])]
  transfers between devices with their start and end apart: 9 -> 9, of which waited for: 3 -> 2; matrix products, arithmetic and copies ran while one was open for 4% -> 4% of each run, Pallas kernels for 64% -> 61%
where the time goes in v8:
time: 86 us; the launch traced here: 85.3 us
  Pallas kernels  52 us (60%)
  starting transfers between devices  19.7 us (23%)
  waiting for transfers between devices  5.67 us (7%)
  other arithmetic  4.25 us (5%)
  local copies, waits for them, and re-layouts  2.95 us (3%)
    pallas_call x4, Pallas kernels, call(): pl.pallas_call(kernel, grid_spec=pltpu.PrefetchScalarGridSpec(num_scalar_...  48.8 us
    ppermute x6, starting transfers between devices, rounds_of_sum(): lax.ppermute(value, axis, [(i, i ^ flip) for i in range(count)])  13.2 us
    ppermute x2, starting transfers between devices, passed_along(): lax.ppermute(value, axis, [(source, source + steps) for source in range(i...  6.37 us
    ppermute x2, waiting for transfers between devices, passed_along(): lax.ppermute(value, axis, [(source, source + steps) for source in range(i...  4.93 us
    pallas_call x1, Pallas kernels, reset_masks(): pl.pallas_call(functools.partial(reset_kernel, steps), out_shape=[jax.Sha...  3.11 us
    convert_element_type x1, other arithmetic, product_bf16(): return (a.astype(F32) * b.astype(F32)).astype(BF16)  1.8 us
  transfers between devices with their start and end apart: 9, of which 2 were waited for; matrix products, arithmetic and copies ran while one was open for 4% of the time, Pallas kernels for 61%

profile of v8, /device:TPU:0, one launch (start us, length us, event | category | flops | bytes accessed | tf_op | source)
XLA Modules:
  0.0 85.3 jit_solution(5548559125004569766)
XLA Ops:
  0.7 1.8 %multiply_convert_fusion = bf16[128,4096]{1,0:T(8,128)(2,1)S(1)} fusion(bf16[256,4096]{1,0:T(8,128)(2,1)} %v_ref.5, bf16[256,4096]{1,0:T(8,128)(2,1)} %k_ref.5), kind=kLoop, calls=%fused_computation | loop fusion | flops 2097152 | bytes 3145728 | tf_op jit(solution)/shard_map/convert_element_type | solution.py:112
  2.5 4.9 %collective-permute-start = (bf16[128,4096]{1,0:T(8,128)(2,1)S(1)}, bf16[128,4096]{1,0:T(8,128)(2,1)S(1)}, u32[]{:S(2)}, u32[]{:S(2)}) collective-permute-start(bf16[128,4096]{1,0:T(8,128)(2,1)S(1)} %multiply_convert_fusion), channel_id=1, source_target_pairs={{0,2},{2,4},{4,6},{6,8},{8,10},{10,12},{12,14},{14,16},{16,18},{18... | collective-permute-start | bytes 3145736 | tf_op jit(solution)/shard_map/ppermute | solution.py:421
  7.4 0.1 fusion.1
  7.5 0.6 broadcast_in_dim.4.near_ref
  8.0 0.1 tile.10
  8.2 3.1 %resets.1 = (bf16[8,176,256]{2,1,0:T(8,128)(2,1)}, bf16[8,48,256]{2,1,0:T(8,128)(2,1)}, f32[8,48,256]{2,1,0:T(8,128)}, f32[8,16,256]{2,1,0:T(8,128)}, f32[8,16,2...) custom-call(s32[1,384]{1,0:T(1,128)} %broadcast_in_dim.4.near_ref), custom_call_target="tpu_custom_call" | custom-call | tf_op jit(solution)/shard_map/resets/pallas_call | solution.py:407
  11.3 13.4 %prepare.1 = (bf16[256,16,256]{2,1,0:T(8,128)(2,1)}, bf16[256,16,256]{2,1,0:T(8,128)(2,1)}, bf16[256,16,256]{2,1,0:T(8,128)(2,1)}, bf16[256,64,128]{2,1,0:T(8,12...) custom-call(s32[1]{0:T(128)} %bitcast.info, bf16[256,4096]{1,0:T(8,128)(2,1)} %q_ref.3, ...), custom_call_target="tpu_custom_call" | custom-call | flops 16777216 | bytes 1048576 | tf_op jit(solution)/shard_map/prepare/pallas_call | solution.py:302
  24.8 4.9 %collective-permute-done.rim_ref = bf16[128,4096]{1,0:T(8,128)(2,1)S(1)} collective-permute-done((bf16[128,4096]{1,0:T(8,128)(2,1)S(1)}, bf16[128,4096]{1,0:T(8,128)(2,1)S(1)}, u32[]{:S(2)}, u32[]{:S(2)}) %collective-permute-start) | collective-permute-done | bytes 1048608 | tf_op jit(solution)/shard_map/ppermute | solution.py:421
  29.7 1.5 %collective-permute-start.1 = (bf16[128,4096]{1,0:T(8,128)(2,1)}, bf16[128,4096]{1,0:T(8,128)(2,1)S(1)}, u32[]{:S(2)}, u32[]{:S(2)}) collective-permute-start(bf16[128,4096]{1,0:T(8,128)(2,1)} %get-tuple-element.60), channel_id=1, source_target_pairs={{2,0},{4,2},{6,4},{8,6},{10,8},{12,10},{14,12},{16,14},{18,16},{20... | collective-permute-start | bytes 3145736 | tf_op jit(solution)/shard_map/ppermute | solution.py:421
  31.2 0.8 copy.16.bias_ref
  32.0 18.5 %conv.1 = (bf16[256,4096]{1,0:T(8,128)(2,1)}, bf16[256,4096]{1,0:T(8,128)(2,1)}, f32[256,128]{1,0:T(8,128)}) custom-call(s32[1]{0:T(128)} %get-tuple-element.43.info, bf16[256,4096]{1,0:T(8,128)(2,1)} %q_ref.3, bf16[256,4096]{1,0:T(8,128)(2,1)} %ct_ref.3, bf16[256,16,256]{2,1,0:T(8,128)(2,1)} %get-tuple-element.45.x_ref, ...), custom_call_target="tpu_custom_call" | custom-call | flops 16777216 | bytes 1048576 | tf_op jit(solution)/shard_map/conv/pallas_call | solution.py:302
  50.5 0.9 %pad_maximum_fusion.1 = f32[288,128]{1,0:T(8,128)S(1)} fusion(f32[32,128]{1,0:T(8,128)S(1)} %bitcast.6, f32[256,128]{1,0:T(8,128)} %get-tuple-element.66), kind=kLoop, calls=%fused_computation.2 | loop fusion | flops 36864 | bytes 294912 | tf_op jit(solution)/shard_map/concatenate | solution.py:481
  51.5 5.6 %collective-permute-start.4 = (f32[288,128]{1,0:T(8,128)S(1)}, f32[288,128]{1,0:T(8,128)S(1)}, u32[]{:S(2)}, u32[]{:S(2)}) collective-permute-start(f32[288,128]{1,0:T(8,128)S(1)} %pad_maximum_fusion.1), channel_id=1, source_target_pairs={{0,6},{2,4},{4,2},{6,0},{8,14},{10,12},{12,10},{14,8},{16,22},{18,... | collective-permute-start | bytes 442376 | tf_op jit(solution)/shard_map/ppermute | solution.py:432
  57.0 0.2 collective-permute-start.3
  57.2 1.4 %collective-permute-start.2 = (f32[288,128]{1,0:T(8,128)S(1)}, f32[288,128]{1,0:T(8,128)S(1)}, u32[]{:S(2)}, u32[]{:S(2)}) collective-permute-start(f32[288,128]{1,0:T(8,128)S(1)} %pad_maximum_fusion.1), channel_id=1, source_target_pairs={{0,2},{2,0},{4,6},{6,4},{8,10},{10,8},{12,14},{14,12},{16,18},{18,... | collective-permute-start | bytes 442376 | tf_op jit(solution)/shard_map/ppermute | solution.py:432
  58.6 1.0 %copy-done = bf16[128,4096]{1,0:T(8,128)(2,1)} copy-done((bf16[128,4096]{1,0:T(8,128)(2,1)}, bf16[128,4096]{1,0:T(8,128)(2,1)S(1)}, u32[]{:S(2)}) %copy-start) | copy-done | bytes 1048600
  59.6 8.5 %back.2 = (bf16[256,4096]{1,0:T(8,128)(2,1)}, bf16[256,4096]{1,0:T(8,128)(2,1)}, f32[8,128]{1,0:T(8,128)}) custom-call(s32[1]{0:T(128)} %get-tuple-element.43.info, bf16[256,4096]{1,0:T(8,128)(2,1)} %k_ref.5, bf16[256,4096]{1,0:T(8,128)(2,1)} %v_ref.5, bf16[256,16,256]{2,1,0:T(8,128)(2,1)} %get-tuple-element.58.dy_ref, ...), custom_call_target="tpu_custom_call" | custom-call | flops 16777216 | bytes 1048576 | tf_op jit(solution)/shard_map/back/pallas_call | solution.py:302
  68.1 5.5 %collective-permute-start.7 = (f32[288,128]{1,0:T(8,128)S(1)}, f32[288,128]{1,0:T(8,128)S(1)}, u32[]{:S(2)}, u32[]{:S(2)}) collective-permute-start(f32[288,128]{1,0:T(8,128)S(1)} %add_add_fusion.1), channel_id=1, source_target_pairs={{0,24},{2,26},{4,28},{6,30},{8,16},{10,18},{12,20},{14,22},{16,8},... | collective-permute-start | bytes 442376 | tf_op jit(solution)/shard_map/ppermute | solution.py:432
  73.6 0.6 collective-permute-start.5
  74.2 8.4 %back.3 = (bf16[256,4096]{1,0:T(8,128)(2,1)}, bf16[256,4096]{1,0:T(8,128)(2,1)}, f32[8,128]{1,0:T(8,128)}) custom-call(s32[1]{0:T(128)} %get-tuple-element.43.info, bf16[256,4096]{1,0:T(8,128)(2,1)} %k_ref.5, bf16[256,4096]{1,0:T(8,128)(2,1)} %v_ref.5, ...), custom_call_target="tpu_custom_call", output_to_operand_aliasing={{0}: (10, {}), {1}: (11, {})} | custom-call | flops 16777216 | bytes 1048576 | tf_op jit(solution)/shard_map/back/pallas_call | solution.py:302
  82.8 0.6 fusion
  83.4 0.7 collective-permute-done.8
  84.2 0.4 rev.3
  84.6 0.7 broadcast_multiply_fusion
  (27 shorter events, 0.3 us)
Async XLA Ops:
  0.6 6.8 %copy-start.5 = (s32[4096]{0:T(1024)S(1)}, s32[4096]{0:T(1024)}, u32[]{:S(2)}) copy-start(s32[4096]{0:T(1024)} %param.13) | copy-start | bytes 49156
  0.6 7.4 %copy-start.4 = (f32[4096]{0:T(1024)S(1)}, f32[4096]{0:T(1024)}, u32[]{:S(2)}) copy-start(f32[4096]{0:T(1024)} %param.12) | copy-start | bytes 49156
  2.5 27.2 %collective-permute-start = (bf16[128,4096]{1,0:T(8,128)(2,1)S(1)}, bf16[128,4096]{1,0:T(8,128)(2,1)S(1)}, u32[]{:S(2)}, u32[]{:S(2)}) collective-permute-start(bf16[128,4096]{1,0:T(8,128)(2,1)S(1)} %multiply_convert_fusion), channel_id=1, source_target_pairs={{0,2},{2,4},{4,6},{6,8},{8,10},{10,12},{12,14},{14,16},{16,18},{18... | collective-permute-start | bytes 3145736 | tf_op jit(solution)/shard_map/ppermute | solution.py:421
  29.7 2.3 %copy-start.1 = (bf16[128,4096]{1,0:T(8,128)(2,1)}, bf16[128,4096]{1,0:T(8,128)(2,1)S(1)}, u32[]{:S(2)}) copy-start(bf16[128,4096]{1,0:T(8,128)(2,1)S(1)} %collective-permute-done.rim_ref) | copy-start | bytes 3145732
  29.7 28.9 %collective-permute-start.1 = (bf16[128,4096]{1,0:T(8,128)(2,1)}, bf16[128,4096]{1,0:T(8,128)(2,1)S(1)}, u32[]{:S(2)}, u32[]{:S(2)}) collective-permute-start(bf16[128,4096]{1,0:T(8,128)(2,1)} %get-tuple-element.60), channel_id=1, source_target_pairs={{2,0},{4,2},{6,4},{8,6},{10,8},{12,10},{14,12},{16,14},{18,16},{20... | collective-permute-start | bytes 3145736 | tf_op jit(solution)/shard_map/ppermute | solution.py:421
  32.0 18.5 %copy-start.3 = (f32[1,4096]{1,0:T(1,128)S(1)}, f32[1,4096]{1,0:T(1,128)}, u32[]{:S(2)}) copy-start(f32[1,4096]{1,0:T(1,128)} %get-tuple-element.67) | copy-start | bytes 49156
  51.5 16.6 %collective-permute-start.4 = (f32[288,128]{1,0:T(8,128)S(1)}, f32[288,128]{1,0:T(8,128)S(1)}, u32[]{:S(2)}, u32[]{:S(2)}) collective-permute-start(f32[288,128]{1,0:T(8,128)S(1)} %pad_maximum_fusion.1), channel_id=1, source_target_pairs={{0,6},{2,4},{4,2},{6,0},{8,14},{10,12},{12,10},{14,8},{16,22},{18,... | collective-permute-start | bytes 442376 | tf_op jit(solution)/shard_map/ppermute | solution.py:432
  57.0 11.0 %collective-permute-start.3 = (f32[288,128]{1,0:T(8,128)S(1)}, f32[288,128]{1,0:T(8,128)S(1)}, u32[]{:S(2)}, u32[]{:S(2)}) collective-permute-start(f32[288,128]{1,0:T(8,128)S(1)} %pad_maximum_fusion.1), channel_id=1, source_target_pairs={{0,4},{2,6},{4,0},{6,2},{8,12},{10,14},{12,8},{14,10},{16,20},{18,... | collective-permute-start | bytes 442376 | tf_op jit(solution)/shard_map/ppermute | solution.py:432
  57.2 10.9 %collective-permute-start.2 = (f32[288,128]{1,0:T(8,128)S(1)}, f32[288,128]{1,0:T(8,128)S(1)}, u32[]{:S(2)}, u32[]{:S(2)}) collective-permute-start(f32[288,128]{1,0:T(8,128)S(1)} %pad_maximum_fusion.1), channel_id=1, source_target_pairs={{0,2},{2,0},{4,6},{6,4},{8,10},{10,8},{12,14},{14,12},{16,18},{18,... | collective-permute-start | bytes 442376 | tf_op jit(solution)/shard_map/ppermute | solution.py:432
  58.6 1.0 %copy-start = (bf16[128,4096]{1,0:T(8,128)(2,1)}, bf16[128,4096]{1,0:T(8,128)(2,1)S(1)}, u32[]{:S(2)}) copy-start(bf16[128,4096]{1,0:T(8,128)(2,1)S(1)} %collective-permute-done.1.rim_ref) | copy-start | bytes 3145732
  59.6 8.5 %copy-start.2 = (f32[256,128]{1,0:T(8,128)S(1)}, f32[256,128]{1,0:T(8,128)}, u32[]{:S(2)}) copy-start(f32[256,128]{1,0:T(8,128)} %get-tuple-element.66) | copy-start | bytes 393220
  68.1 14.5 %collective-permute-start.7 = (f32[288,128]{1,0:T(8,128)S(1)}, f32[288,128]{1,0:T(8,128)S(1)}, u32[]{:S(2)}, u32[]{:S(2)}) collective-permute-start(f32[288,128]{1,0:T(8,128)S(1)} %add_add_fusion.1), channel_id=1, source_target_pairs={{0,24},{2,26},{4,28},{6,30},{8,16},{10,18},{12,20},{14,22},{16,8},... | collective-permute-start | bytes 442376 | tf_op jit(solution)/shard_map/ppermute | solution.py:432
  73.6 9.1 %collective-permute-start.6 = (f32[288,128]{1,0:T(8,128)S(1)}, f32[288,128]{1,0:T(8,128)S(1)}, u32[]{:S(2)}, u32[]{:S(2)}) collective-permute-start(f32[288,128]{1,0:T(8,128)S(1)} %add_add_fusion.1), channel_id=1, source_target_pairs={{0,16},{2,18},{4,20},{6,22},{8,24},{10,26},{12,28},{14,30},{16,0},... | collective-permute-start | bytes 442376 | tf_op jit(solution)/shard_map/ppermute | solution.py:432
  73.6 9.1 %collective-permute-start.5 = (f32[288,128]{1,0:T(8,128)S(1)}, f32[288,128]{1,0:T(8,128)S(1)}, u32[]{:S(2)}, u32[]{:S(2)}) collective-permute-start(f32[288,128]{1,0:T(8,128)S(1)} %add_add_fusion.1), channel_id=1, source_target_pairs={{0,8},{2,10},{4,12},{6,14},{8,0},{10,2},{12,4},{14,6},{16,24},{18,... | collective-permute-start | bytes 442376 | tf_op jit(solution)/shard_map/ppermute | solution.py:432
  82.7 1.4 %collective-permute-start.8 = (f32[256,128]{1,0:T(8,128)S(1)}, f32[256,128]{1,0:T(8,128)S(1)}, u32[]{:S(2)}, u32[]{:S(2)}) collective-permute-start(f32[256,128]{1,0:T(8,128)S(1)} %slice.16), channel_id=1, source_target_pairs={{0,1},{1,0},{2,3},{3,2},{4,5},{5,4},{6,7},{7,6},{8,9},{9,8},{10,11... | collective-permute-start | bytes 393224 | tf_op jit(solution)/shard_map/ppermute | solution.py:447
